TPU v7x, 32 devices: a whole 2x2x4 slice. The times are simulated.
32 devices in a mesh: rows: 8 (over z, y), heads: 4 (over x, core).
Axes of the slice: x: 2, y: 2, z: 4, core: 2. Of those that a mesh axis runs over, the one named last changes fastest.
Arguments:
- queries: bfloat16 [4096, 512], P('rows', 'heads'), may hold values from -6 to 6
- key_vectors: bfloat16 [4096, 512], P('rows', 'heads'), may hold values from -6 to 6
- value_vectors: bfloat16 [4096, 512], P('rows', 'heads'), may hold values from -120 to 120
- gating: bfloat16 [4096, 512], P('rows', 'heads'), may hold values from -6 to 6
- bounds: int32 [2, 4096], P(None, 'rows'), may hold values from 0 to 4095, as said below
- cotangent: bfloat16 [4096, 512], P('rows', 'heads'), may hold values from -6 to 6
Outputs:
- layer_out: bfloat16 [4096, 512], P('rows', 'heads')
- grad_queries: bfloat16 [4096, 512], P('rows', 'heads')
- grad_keys: bfloat16 [4096, 512], P('rows', 'heads')
- grad_values: bfloat16 [4096, 512], P('rows', 'heads')
- grad_gating: bfloat16 [4096, 512], P('rows', 'heads')
Inputs may be any that keep to these rules, and one draw needn't show every extreme that they name: bounds[0, r] and bounds[1, r] are the first and the last row of the history that holds row r; histories are runs of consecutive rows that cover all 4096 rows, each at most 1024 rows long, and one of them exactly that long.
All inputs are finite; a program needn't handle non-finite values.
Results may differ from a plain program's by a relative error of at most 0.006.
Values may be sent and summed in bfloat16 or wider, within the bound.
No kernel may reach another device: no remote copies, remote signals or barrier semaphores. Data moves between devices by JAX's collectives and lax.ppermute only.
A program may use at most 64 MiB of HBM per device.

v0:
```python
import jax
import jax.numpy as jnp
from jax import lax
from jax.sharding import PartitionSpec as P

DH = 128
REACH = 2


EPSILON = 1e-05


def from_behind(value, axis, steps):
    count = lax.axis_size(axis)
    initial, last = (max(0, -steps), min(count, count - steps))
    return lax.ppermute(value, axis, [(source, source + steps) for source in range(initial, last)])


def silu_parts(query_tile, key_tile, allowed, factor):
    scores = (
        jnp.einsum("qhd,khd->hqk", query_tile, key_tile, preferred_element_type=jnp.float32)
        * factor
    )
    sigmoid = jax.nn.sigmoid(scores)
    weights = jnp.where(allowed[None], scores * sigmoid, 0.0).astype(jnp.bfloat16)
    return (scores, sigmoid, weights)


def tile_backward(query_part, key_part, value_part, delta_part, allowed, factor):
    scores, sigmoid, weights = silu_parts(query_part, key_part, allowed, factor)
    pulled = jnp.einsum("qhd,khd->hqk", delta_part, value_part, preferred_element_type=jnp.float32)
    score_grad = jnp.where(
        allowed[None], pulled * sigmoid * (1.0 + scores * (1.0 - sigmoid)), 0.0
    ).astype(jnp.bfloat16)
    query_add = jnp.einsum("hqk,khd->qhd", score_grad, key_part, preferred_element_type=jnp.float32)
    key_add = (
        jnp.einsum("hqk,qhd->khd", score_grad, query_part, preferred_element_type=jnp.float32)
        * factor
    )
    value_add = jnp.einsum("hqk,qhd->khd", weights, delta_part, preferred_element_type=jnp.float32)
    return (query_add, key_add, value_add)


def local(queries, key_vectors, value_vectors, gating, bounds, cotangent):
    rows_dev, feature_width = queries.shape
    heads_dev = feature_width // DH
    factor = DH ** (-0.5)
    features = feature_width * lax.axis_size("heads")
    position = lax.axis_index("rows")
    first_row = position * rows_dev
    local_rows = jnp.arange(rows_dev, dtype=jnp.int32)
    row_ids = first_row + local_rows
    starts = bounds[0]
    query_tile = queries.reshape(rows_dev, heads_dev, DH)
    key_tile = key_vectors.reshape(rows_dev, heads_dev, DH)
    value_tile = value_vectors.reshape(rows_dev, heads_dev, DH)
    empty_tile = jnp.zeros((rows_dev, heads_dev, DH), jnp.float32)
    neighbours = [(key_tile, value_tile)]
    carried = (key_tile, value_tile)
    for offset in range(1, REACH + 1):
        carried = from_behind((carried[0], carried[1]), "rows", 1)
        neighbours.append(carried)

    def owner_mask(offset):
        key_ids = first_row - offset * rows_dev + local_rows
        return (key_ids[None, :] >= starts[:, None]) & (key_ids[None, :] <= row_ids[:, None])

    attended = empty_tile
    for offset in range(REACH + 1):
        key_part, value_part = neighbours[offset]
        allowed = owner_mask(offset)
        weights = silu_parts(query_tile, key_part, allowed, factor)[2]
        attended = attended + jnp.einsum(
            "hqk,khd->qhd", weights, value_part, preferred_element_type=jnp.float32
        )
    attended = attended.reshape(rows_dev, feature_width)
    total_sum, square_sum = lax.psum(
        (jnp.sum(attended, axis=1), jnp.sum(attended * attended, axis=1)), "heads"
    )
    average = total_sum[:, None] / features
    variance = square_sum[:, None] / features - average * average
    inverse = lax.rsqrt(variance + EPSILON)
    normed = (attended - average) * inverse
    gate_float = gating.astype(jnp.float32)
    layer_out = (normed * gate_float).astype(jnp.bfloat16)
    upstream = cotangent.astype(jnp.float32)
    grad_gating = (upstream * normed).astype(jnp.bfloat16)
    scaled = upstream * gate_float
    grad_sum, cross_sum = lax.psum(
        (jnp.sum(scaled, axis=1), jnp.sum(scaled * normed, axis=1)), "heads"
    )
    delta_rows = (
        inverse * (scaled - grad_sum[:, None] / features - normed * (cross_sum[:, None] / features))
    ).astype(jnp.bfloat16)
    delta_tile = delta_rows.reshape(rows_dev, heads_dev, DH)
    grad_query = empty_tile
    grad_key = empty_tile
    grad_value = empty_tile
    for offset in range(REACH + 1):
        key_part, value_part = neighbours[offset]
        allowed = owner_mask(offset)
        query_add, key_add, value_add = tile_backward(
            query_tile, key_part, value_part, delta_tile, allowed, factor
        )
        grad_query = grad_query + query_add
        if offset == 0:
            grad_key = key_add
            grad_value = value_add
        else:
            key_back, value_back = from_behind((key_add, value_add), "rows", -offset)
            grad_key = grad_key + key_back
            grad_value = grad_value + value_back
    grad_queries = (grad_query * factor).reshape(rows_dev, feature_width).astype(jnp.bfloat16)
    grad_keys = grad_key.reshape(rows_dev, feature_width).astype(jnp.bfloat16)
    grad_values = grad_value.reshape(rows_dev, feature_width).astype(jnp.bfloat16)
    return (layer_out, grad_queries, grad_keys, grad_values, grad_gating)


def solution(mesh):
    return jax.shard_map(
        local,
        mesh=mesh,
        in_specs=(
            P("rows", "heads"),
            P("rows", "heads"),
            P("rows", "heads"),
            P("rows", "heads"),
            P(None, "rows"),
            P("rows", "heads"),
        ),
        out_specs=(
            P("rows", "heads"),
            P("rows", "heads"),
            P("rows", "heads"),
            P("rows", "heads"),
            P("rows", "heads"),
        ),
        check_vma=False,
    )
```

profile of v0, /device:TPU:22, one launch (start us, length us, event | category | flops | bytes accessed | tf_op | source)
XLA Modules:
  0.0 66.9 jit_solution(488827510066615355)
XLA Ops:
  0.6 0.0 copy-start
  0.6 3.6 %collective-permute-start = (bf16[512,1,128]{2,0,1:T(8,128)(2,1)}, bf16[512,1,128]{2,0,1:T(8,128)(2,1)S(1)}, u32[]{:S(2)}, u32[]{:S(2)}) collective-permute-start(bf16[512,1,128]{2,0,1:T(8,128)(2,1)} %bitcast.105), channel_id=1, source_target_pairs={{0,4},{4,8},{8,12},{12,16},{16,20},{20,24},{24,28},{1,5},{5,9},{9,... | collective-permute-start | bytes 393224 | tf_op jit(solution)/shard_map/ppermute | solution.py:16
  4.2 3.4 %collective-permute-start.1 = (bf16[512,1,128]{2,0,1:T(8,128)(2,1)}, bf16[512,1,128]{2,0,1:T(8,128)(2,1)}, u32[]{:S(2)}, u32[]{:S(2)}) collective-permute-start(bf16[512,1,128]{2,0,1:T(8,128)(2,1)} %bitcast.106), channel_id=1, source_target_pairs={{0,4},{4,8},{8,12},{12,16},{16,20},{20,24},{24,28},{1,5},{5,9},{9,... | collective-permute-start | bytes 393224 | tf_op jit(solution)/shard_map/ppermute | solution.py:16
  7.7 1.2 %convolution_multiply_fusion.5 = f32[512,512]{1,0:T(8,128)S(1)} fusion(bf16[512,128]{1,0:T(8,128)(2,1)S(1)} %copy-done, bf16[512,128]{1,0:T(8,128)(2,1)} %param.7), kind=kOutput, calls=%fused_computation.5 | convolution fusion | flops 67371008 | bytes 1310720 | tf_op jit(solution)/shard_map/qhd,khd->hqk/dot_general | solution.py:21
  8.9 0.0 copy-start.18
  8.9 0.7 copy-done.18
  9.6 0.1 copy.11
  9.7 0.8 %copy-done.11 = bf16[512,128]{1,0:T(8,128)(2,1)S(1)} copy-done((bf16[512,128]{1,0:T(8,128)(2,1)S(1)}, bf16[512,128]{1,0:T(8,128)(2,1)}, u32[]{:S(2)}) %copy-start.11) | copy-done | bytes 131096
  10.5 0.1 copy.12
  10.7 1.9 %collective-permute-start.2 = (bf16[512,1,128]{2,0,1:T(8,128)(2,1)S(1)}, bf16[512,1,128]{2,0,1:T(8,128)(2,1)S(1)}, u32[]{:S(2)}, u32[]{:S(2)}) collective-permute-start(bf16[512,1,128]{2,0,1:T(8,128)(2,1)S(1)} %collective-permute-done), channel_id=1, source_target_pairs={{0,4},{4,8},{8,12},{12,16},{16,20},{20,24},{24,28},{1,5},{5,9},{9,... | collective-permute-start | bytes 393224 | tf_op jit(solution)/shard_map/ppermute | solution.py:16
  12.6 3.3 %collective-permute-start.3 = (bf16[512,1,128]{2,0,1:T(8,128)(2,1)}, bf16[512,1,128]{2,0,1:T(8,128)(2,1)S(1)}, u32[]{:S(2)}, u32[]{:S(2)}) collective-permute-start(bf16[512,1,128]{2,0,1:T(8,128)(2,1)} %collective-permute-done.1), channel_id=1, source_target_pairs={{0,4},{4,8},{8,12},{12,16},{16,20},{20,24},{24,28},{1,5},{5,9},{9,... | collective-permute-start | bytes 393224 | tf_op jit(solution)/shard_map/ppermute | solution.py:16
  15.9 0.3 convolution_multiply_fusion.4
  16.2 2.4 %collective-permute-done.2 = bf16[512,1,128]{2,0,1:T(8,128)(2,1)S(1)} collective-permute-done((bf16[512,1,128]{2,0,1:T(8,128)(2,1)S(1)}, bf16[512,1,128]{2,0,1:T(8,128)(2,1)S(1)}, u32[]{:S(2)}, u32[]{:S(2)}) %collective-permute-start.2) | collective-permute-done | bytes 131104 | tf_op jit(solution)/shard_map/ppermute | solution.py:16
  18.6 2.2 %select_convert_fusion = (bf16[512,512]{1,0:T(8,128)(2,1)S(1)}, bf16[512,512]{1,0:T(8,128)(2,1)S(1)}, bf16[512,512]{1,0:T(8,128)(2,1)S(1)}, f32[512,512]{1,0:T(8,128)}) fusion(s32[512]{0:T(512)S(1)} %get-tuple-element.28, s32[512]{0:T(512)S(1)} %get-tuple-element.29, s32[512]{0:T(512)S(1)} %bitcast.107, f32[512,512]{1,0:T(8,128)S(1)} %convolution_multiply_fusion.4, ...), kind=kOutput, calls=%fused_computation.38 | convolution fusion | flops 74448896 | bytes 4988928 | tf_op jit(solution)/shard_map/qhd,khd->hqk/dot_general | solution.py:21
  20.8 0.3 fusion.34
  21.1 1.2 %convolution_add_fusion.3 = f32[512,128]{0,1:T(8,128)S(1)} fusion(f32[512,128]{0,1:T(8,128)S(1)} %fusion.34, bf16[512,512]{1,0:T(8,128)(2,1)S(1)} %get-tuple-element.22, bf16[512,1,128]{2,0,1:T(8,128)(2,1)} %collective-permute-done.1), kind=kOutput, calls=%fused_computation.27 | convolution fusion | flops 67174400 | bytes 1179648 | tf_op jit(solution)/shard_map/hqk,khd->qhd/dot_general | solution.py:73
  22.4 0.3 fusion.33
  22.7 0.3 copy-done.8
  23.0 5.9 %all-reduce.1 = (f32[512]{0:T(512)S(1)}, f32[512]{0:T(512)S(1)}) all-reduce(f32[512]{0:T(512)S(1)} %get-tuple-element.13, f32[512]{0:T(512)S(1)} %get-tuple-element.12), channel_id=1, replica_groups=mesh['rows'=8,'heads'=4] {'heads'}, use_global_device_ids=true, to_apply=%region_3.4 | all-reduce | flops 1024 | bytes 8192 | tf_op jit(solution)/shard_map/psum | solution.py:77
  28.9 0.1 fusion.24
  29.0 5.8 %all-reduce = (f32[512]{0:T(512)S(1)}, f32[512]{0:T(512)S(1)}) all-reduce(f32[512]{0:T(512)S(1)} %get-tuple-element.11, f32[512]{0:T(512)S(1)} %get-tuple-element.10), channel_id=1, replica_groups=mesh['rows'=8,'heads'=4] {'heads'}, use_global_device_ids=true, to_apply=%region_7.8 | all-reduce | flops 1024 | bytes 8192 | tf_op jit(solution)/shard_map/psum | solution.py:89
  34.8 0.8 %fusion.23 = (bf16[512,128]{0,1:T(8,128)(2,1)}, bf16[512,128]{0,1:T(8,128)(2,1)S(1)}, bf16[512,128]{0,1:T(8,128)(2,1)}) fusion(bf16[512,128]{0,1:T(8,128)(2,1)S(1)} %copy.12, f32[512,128]{0,1:T(8,128)S(1)} %get-tuple-element.27, f32[512]{0:T(512)S(1)} %get-tuple-element.25, f32[512]{0:T(512)S(1)} %get-tuple-element.24, f32[512]{0:T(512)S(1)} %broadcast_multiply_fusion, ...), kind=kLoop, calls=%fused_computation.51 | loop fusion | flops 917504 | bytes 925696 | tf_op jit(solution)/shard_map/convert_element_type | solution.py:87
  35.6 0.9 %convolution_bitcast_fusion.1 = f32[512,1,128]{0,2,1:T(8,128)} fusion(bf16[512,128]{0,1:T(8,128)(2,1)S(1)} %get-tuple-element.19, bf16[512,512]{1,0:T(8,128)(2,1)S(1)} %get-tuple-element.22), kind=kOutput, calls=%fused_computation.16 | convolution fusion | flops 67108864 | bytes 917504 | tf_op jit(solution)/shard_map/hqk,qhd->khd/dot_general | solution.py:40
  36.5 0.2 convolution_bitcast_fusion
  36.8 0.7 %copy-done.7 = bf16[512,128]{1,0:T(8,128)(2,1)S(1)} copy-done((bf16[512,128]{1,0:T(8,128)(2,1)S(1)}, bf16[512,128]{1,0:T(8,128)(2,1)}, u32[]{:S(2)}) %copy-start.7) | copy-done | bytes 131096
  37.5 0.6 fusion.8
  38.1 2.3 %collective-permute-start.6 = (f32[512,1,128]{0,2,1:T(8,128)}, f32[512,1,128]{0,2,1:T(8,128)S(1)}, u32[]{:S(2)}, u32[]{:S(2)}) collective-permute-start(f32[512,1,128]{0,2,1:T(8,128)} %convolution_bitcast_fusion.1), channel_id=1, source_target_pairs={{4,0},{8,4},{12,8},{16,12},{20,16},{24,20},{28,24},{5,1},{9,5},{13... | collective-permute-start | bytes 786440 | tf_op jit(solution)/shard_map/ppermute | solution.py:16
  40.4 2.4 %collective-permute-start.7 = (f32[512,1,128]{0,2,1:T(8,128)S(1)}, f32[512,1,128]{0,2,1:T(8,128)S(1)}, u32[]{:S(2)}, u32[]{:S(2)}) collective-permute-start(f32[512,1,128]{0,2,1:T(8,128)S(1)} %convolution_bitcast_fusion), channel_id=1, source_target_pairs={{8,0},{12,4},{16,8},{20,12},{24,16},{28,20},{9,1},{13,5},{17,9},{2... | collective-permute-start | bytes 786440 | tf_op jit(solution)/shard_map/ppermute | solution.py:16
  42.8 0.6 fusion.6
  43.4 0.3 fusion.9
  43.8 1.9 %collective-permute-start.5 = (f32[512,1,128]{2,0,1:T(8,128)S(1)}, f32[512,1,128]{2,0,1:T(8,128)S(1)}, u32[]{:S(2)}, u32[]{:S(2)}) collective-permute-start(f32[512,1,128]{2,0,1:T(8,128)S(1)} %fusion.9), channel_id=1, source_target_pairs={{8,0},{12,4},{16,8},{20,12},{24,16},{28,20},{9,1},{13,5},{17,9},{2... | collective-permute-start | bytes 786440 | tf_op jit(solution)/shard_map/ppermute | solution.py:16
  45.7 1.5 %fusion.7 = bf16[512,512]{1,0:T(8,128)(2,1)S(1)} fusion(bf16[512,128]{0,1:T(8,128)(2,1)S(1)} %get-tuple-element.19, f32[512,512]{1,0:T(8,128)S(1)} %copy-done.2, s32[512]{0:T(512)S(1)} %iota_add_fusion.1, s32[512]{0:T(512)S(1)} %copy-done.15, s32[512]{0:T(512)S(1)} %bitcast.110, bf16[512,1,128]{2,0,1:T(8,128)(2,1)} %collective-permute-done.1), kind=kOutput, calls=%fused_computation.13 | convolution fusion | flops 70516736 | bytes 1841152 | tf_op jit(solution)/shard_map/qhd,khd->hqk/dot_general | solution.py:31
  47.2 0.0 copy-start.3
  47.3 0.3 fusion.10
  47.6 2.8 %collective-permute-start.4 = (f32[512,1,128]{2,0,1:T(8,128)S(1)}, f32[512,1,128]{2,0,1:T(8,128)S(1)}, u32[]{:S(2)}, u32[]{:S(2)}) collective-permute-start(f32[512,1,128]{2,0,1:T(8,128)S(1)} %fusion.10), channel_id=1, source_target_pairs={{4,0},{8,4},{12,8},{16,12},{20,16},{24,20},{28,24},{5,1},{9,5},{13... | collective-permute-start | bytes 786440 | tf_op jit(solution)/shard_map/ppermute | solution.py:16
  50.4 0.3 fusion.35
  50.7 0.0 copy-start.13
  50.7 0.3 convolution_add_fusion.1
  51.0 0.6 copy-done.13
  51.6 1.0 %fusion.18 = bf16[512,128]{1,0:T(8,128)(2,1)} fusion(f32[512,128]{1,0:T(8,128)S(1)} %convolution_add_fusion.1, bf16[512,512]{1,0:T(8,128)(2,1)S(1)} %fusion.6, bf16[512,1,128]{2,0,1:T(8,128)(2,1)S(1)} %copy-done.13), kind=kOutput, calls=%fused_computation.34 | convolution fusion | flops 67305472 | bytes 1048576 | tf_op jit(solution)/shard_map/hqk,khd->qhd/dot_general | solution.py:35
  52.6 0.8 %copy.13 = bf16[512,128]{1,0:T(8,128)(2,1)} copy(bf16[512,128]{0,1:T(8,128)(2,1)S(1)} %copy-done.5) | data formatting | bytes 262144
  53.3 0.1 copy-done.4
  53.5 0.8 %copy.15 = bf16[512,128]{1,0:T(8,128)(2,1)} copy(bf16[512,128]{0,1:T(8,128)(2,1)S(1)} %copy-done.4) | data formatting | bytes 262144
  54.2 0.2 fusion.20
  54.5 0.8 %copy.14 = bf16[512,128]{1,0:T(8,128)(2,1)} copy(bf16[512,128]{0,1:T(8,128)(2,1)S(1)} %fusion.20) | data formatting | bytes 262144
  55.2 0.3 collective-permute-done.5
  55.6 10.3 %collective-permute-done.4 = f32[512,1,128]{2,0,1:T(8,128)S(1)} collective-permute-done((f32[512,1,128]{2,0,1:T(8,128)S(1)}, f32[512,1,128]{2,0,1:T(8,128)S(1)}, u32[]{:S(2)}, u32[]{:S(2)}) %collective-permute-start.4) | collective-permute-done | bytes 262176 | tf_op jit(solution)/shard_map/ppermute | solution.py:16
  65.9 1.0 %fusion.21 = bf16[512,128]{1,0:T(8,128)(2,1)} fusion(f32[512,1,128]{2,0,1:T(8,128)S(1)} %collective-permute-done.5, f32[512,1,128]{2,0,1:T(8,128)S(1)} %collective-permute-done.4, bf16[512,512]{1,0:T(8,128)(2,1)S(1)} %fusion.8, bf16[512,128]{1,0:T(8,128)(2,1)S(1)} %copy-done), kind=kOutput, calls=%fused_computation.37 | convolution fusion | flops 67371008 | bytes 1310720 | tf_op jit(solution)/shard_map/hqk,qhd->khd/dot_general | solution.py:37
  (41 shorter events, 0.1 us)
Async XLA Ops:
  0.6 7.0 %copy-start = (bf16[512,128]{1,0:T(8,128)(2,1)S(1)}, bf16[512,128]{1,0:T(8,128)(2,1)}, u32[]{:S(2)}) copy-start(bf16[512,128]{1,0:T(8,128)(2,1)} %param.6) | copy-start | bytes 393220
  0.6 10.0 %collective-permute-start = (bf16[512,1,128]{2,0,1:T(8,128)(2,1)}, bf16[512,1,128]{2,0,1:T(8,128)(2,1)S(1)}, u32[]{:S(2)}, u32[]{:S(2)}) collective-permute-start(bf16[512,1,128]{2,0,1:T(8,128)(2,1)} %bitcast.105), channel_id=1, source_target_pairs={{0,4},{4,8},{8,12},{12,16},{16,20},{20,24},{24,28},{1,5},{5,9},{9,... | collective-permute-start | bytes 393224 | tf_op jit(solution)/shard_map/ppermute | solution.py:16
  4.2 8.4 %collective-permute-start.1 = (bf16[512,1,128]{2,0,1:T(8,128)(2,1)}, bf16[512,1,128]{2,0,1:T(8,128)(2,1)}, u32[]{:S(2)}, u32[]{:S(2)}) collective-permute-start(bf16[512,1,128]{2,0,1:T(8,128)(2,1)} %bitcast.106), channel_id=1, source_target_pairs={{0,4},{4,8},{8,12},{12,16},{16,20},{20,24},{24,28},{1,5},{5,9},{9,... | collective-permute-start | bytes 393224 | tf_op jit(solution)/shard_map/ppermute | solution.py:16
  7.7 1.9 %copy-start.10 = (bf16[512,128]{1,0:T(8,128)(2,1)S(1)}, bf16[512,128]{1,0:T(8,128)(2,1)}, u32[]{:S(2)}) copy-start(bf16[512,128]{1,0:T(8,128)(2,1)} %param.9) | copy-start | bytes 393220
  8.9 0.7 %copy-start.18 = (s32[2,512]{1,0:T(2,128)S(1)}, s32[2,512]{1,0:T(2,128)}, u32[]{:S(2)}) copy-start(s32[2,512]{1,0:T(2,128)} %param.10) | copy-start | bytes 12292
  9.6 0.9 %copy-start.11 = (bf16[512,128]{1,0:T(8,128)(2,1)S(1)}, bf16[512,128]{1,0:T(8,128)(2,1)}, u32[]{:S(2)}) copy-start(bf16[512,128]{1,0:T(8,128)(2,1)} %param.11) | copy-start | bytes 393220
  10.7 7.9 %copy-start.14 = (s32[512]{0:T(512)}, s32[512]{0:T(512)S(1)}, u32[]{:S(2)}) copy-start(s32[512]{0:T(512)S(1)} %get-tuple-element.29) | copy-start | bytes 6148
  10.7 7.9 %copy-start.16 = (s32[512]{0:T(512)}, s32[512]{0:T(512)S(1)}, u32[]{:S(2)}) copy-start(s32[512]{0:T(512)S(1)} %get-tuple-element.28) | copy-start | bytes 6148
  10.7 7.9 %collective-permute-start.2 = (bf16[512,1,128]{2,0,1:T(8,128)(2,1)S(1)}, bf16[512,1,128]{2,0,1:T(8,128)(2,1)S(1)}, u32[]{:S(2)}, u32[]{:S(2)}) collective-permute-start(bf16[512,1,128]{2,0,1:T(8,128)(2,1)S(1)} %collective-permute-done), channel_id=1, source_target_pairs={{0,4},{4,8},{8,12},{12,16},{16,20},{20,24},{24,28},{1,5},{5,9},{9,... | collective-permute-start | bytes 393224 | tf_op jit(solution)/shard_map/ppermute | solution.py:16
  12.6 9.7 %collective-permute-start.3 = (bf16[512,1,128]{2,0,1:T(8,128)(2,1)}, bf16[512,1,128]{2,0,1:T(8,128)(2,1)S(1)}, u32[]{:S(2)}, u32[]{:S(2)}) collective-permute-start(bf16[512,1,128]{2,0,1:T(8,128)(2,1)} %collective-permute-done.1), channel_id=1, source_target_pairs={{0,4},{4,8},{8,12},{12,16},{16,20},{20,24},{24,28},{1,5},{5,9},{9,... | collective-permute-start | bytes 393224 | tf_op jit(solution)/shard_map/ppermute | solution.py:16
  16.2 4.6 %copy-start.1 = (f32[512,512]{1,0:T(8,128)}, f32[512,512]{1,0:T(8,128)S(1)}, u32[]{:S(2)}) copy-start(f32[512,512]{1,0:T(8,128)S(1)} %convolution_multiply_fusion.4) | copy-start | bytes 3145732
  18.6 2.2 %copy-start.12 = (bf16[512,1,128]{2,0,1:T(8,128)(2,1)}, bf16[512,1,128]{2,0,1:T(8,128)(2,1)S(1)}, u32[]{:S(2)}) copy-start(bf16[512,1,128]{2,0,1:T(8,128)(2,1)S(1)} %collective-permute-done.2) | copy-start | bytes 393220
  18.6 2.2 %copy-start.6 = (bf16[512,128]{1,0:T(8,128)(2,1)S(1)}, bf16[512,128]{1,0:T(8,128)(2,1)}, u32[]{:S(2)}) copy-start(bf16[512,128]{1,0:T(8,128)(2,1)} %param.8) | copy-start | bytes 393220
  22.4 0.7 copy-start.8
  36.5 0.9 %copy-start.7 = (bf16[512,128]{1,0:T(8,128)(2,1)S(1)}, bf16[512,128]{1,0:T(8,128)(2,1)}, u32[]{:S(2)}) copy-start(bf16[512,128]{1,0:T(8,128)(2,1)} %param.8) | copy-start | bytes 393220
  36.5 0.9 %copy-start.15 = (s32[512]{0:T(512)S(1)}, s32[512]{0:T(512)}, u32[]{:S(2)}) copy-start(s32[512]{0:T(512)} %copy-done.14) | copy-start | bytes 6148
  37.4 5.3 %copy-start.9 = (bf16[512,1,128]{2,0,1:T(8,128)(2,1)S(1)}, bf16[512,1,128]{2,0,1:T(8,128)(2,1)}, u32[]{:S(2)}) copy-start(bf16[512,1,128]{2,0,1:T(8,128)(2,1)} %copy-done.8) | copy-start | bytes 393220
  37.4 5.3 %copy-start.17 = (s32[512]{0:T(512)S(1)}, s32[512]{0:T(512)}, u32[]{:S(2)}) copy-start(s32[512]{0:T(512)} %copy-done.16) | copy-start | bytes 6148
  37.4 5.3 %copy-start.19 = (f32[512,512]{1,0:T(8,128)S(1)}, f32[512,512]{1,0:T(8,128)}, u32[]{:S(2)}) copy-start(f32[512,512]{1,0:T(8,128)} %get-tuple-element.26) | copy-start | bytes 3145732
  38.1 16.1 %collective-permute-start.6 = (f32[512,1,128]{0,2,1:T(8,128)}, f32[512,1,128]{0,2,1:T(8,128)S(1)}, u32[]{:S(2)}, u32[]{:S(2)}) collective-permute-start(f32[512,1,128]{0,2,1:T(8,128)} %convolution_bitcast_fusion.1), channel_id=1, source_target_pairs={{4,0},{8,4},{12,8},{16,12},{20,16},{24,20},{28,24},{5,1},{9,5},{13... | collective-permute-start | bytes 786440 | tf_op jit(solution)/shard_map/ppermute | solution.py:16
  40.4 13.9 %collective-permute-start.7 = (f32[512,1,128]{0,2,1:T(8,128)S(1)}, f32[512,1,128]{0,2,1:T(8,128)S(1)}, u32[]{:S(2)}, u32[]{:S(2)}) collective-permute-start(f32[512,1,128]{0,2,1:T(8,128)S(1)} %convolution_bitcast_fusion), channel_id=1, source_target_pairs={{8,0},{12,4},{16,8},{20,12},{24,16},{28,20},{9,1},{13,5},{17,9},{2... | collective-permute-start | bytes 786440 | tf_op jit(solution)/shard_map/ppermute | solution.py:16
  42.8 2.9 %copy-start.2 = (f32[512,512]{1,0:T(8,128)S(1)}, f32[512,512]{1,0:T(8,128)}, u32[]{:S(2)}) copy-start(f32[512,512]{1,0:T(8,128)} %copy-done.1) | copy-start | bytes 3145732
  43.8 11.8 %collective-permute-start.5 = (f32[512,1,128]{2,0,1:T(8,128)S(1)}, f32[512,1,128]{2,0,1:T(8,128)S(1)}, u32[]{:S(2)}, u32[]{:S(2)}) collective-permute-start(f32[512,1,128]{2,0,1:T(8,128)S(1)} %fusion.9), channel_id=1, source_target_pairs={{8,0},{12,4},{16,8},{20,12},{24,16},{28,20},{9,1},{13,5},{17,9},{2... | collective-permute-start | bytes 786440 | tf_op jit(solution)/shard_map/ppermute | solution.py:16
  47.2 3.1 %copy-start.3 = (bf16[512,128]{1,0:T(8,128)(2,1)S(1)}, bf16[512,128]{1,0:T(8,128)(2,1)}, u32[]{:S(2)}) copy-start(bf16[512,128]{1,0:T(8,128)(2,1)} %param.7) | copy-start | bytes 393220
  47.6 18.3 %collective-permute-start.4 = (f32[512,1,128]{2,0,1:T(8,128)S(1)}, f32[512,1,128]{2,0,1:T(8,128)S(1)}, u32[]{:S(2)}, u32[]{:S(2)}) collective-permute-start(f32[512,1,128]{2,0,1:T(8,128)S(1)} %fusion.10), channel_id=1, source_target_pairs={{4,0},{8,4},{12,8},{16,12},{20,16},{24,20},{28,24},{5,1},{9,5},{13... | collective-permute-start | bytes 786440 | tf_op jit(solution)/shard_map/ppermute | solution.py:16
  50.7 0.9 %copy-start.13 = (bf16[512,1,128]{2,0,1:T(8,128)(2,1)S(1)}, bf16[512,1,128]{2,0,1:T(8,128)(2,1)}, u32[]{:S(2)}) copy-start(bf16[512,1,128]{2,0,1:T(8,128)(2,1)} %copy-done.12) | copy-start | bytes 393220
  51.6 1.0 %copy-start.5 = (bf16[512,128]{0,1:T(8,128)(2,1)S(1)}, bf16[512,128]{0,1:T(8,128)(2,1)}, u32[]{:S(2)}) copy-start(bf16[512,128]{0,1:T(8,128)(2,1)} %get-tuple-element.20) | copy-start | bytes 393220
  52.6 0.9 %copy-start.4 = (bf16[512,128]{0,1:T(8,128)(2,1)S(1)}, bf16[512,128]{0,1:T(8,128)(2,1)}, u32[]{:S(2)}) copy-start(bf16[512,128]{0,1:T(8,128)(2,1)} %get-tuple-element.18) | copy-start | bytes 393220
where the time goes:
time: 67.4 us; the launch traced here: 66.9 us
  starting transfers between devices  21.5 us (32%)
  matrix products  13 us (19%)
  waiting for transfers between devices  13 us (19%)
  blocking collectives  11.6 us (17%)
  local copies, waits for them, and re-layouts  5.75 us (9%)
  between operations  1.01 us (1%)
  other arithmetic  0.93 us (1%)
    ppermute x8, starting transfers between devices, from_behind(): lax.ppermute(value, axis, [(source, source + steps) for source in range(i...  21.5 us
    ppermute x8, waiting for transfers between devices, from_behind(): lax.ppermute(value, axis, [(source, source + steps) for source in range(i...  13 us
    psum x1, blocking collectives, local(): lax.psum((jnp.sum(attended, axis=1), jnp.sum(attended * attended, axis=1)...  5.88 us
    psum x1, blocking collectives, local(): lax.psum((jnp.sum(scaled, axis=1), jnp.sum(scaled * normed, axis=1)), 'he...  5.77 us
    unnamed x45, local copies, waits for them, and re-layouts  5.75 us
    dot_general x3, matrix products, silu_parts(): jnp.einsum('qhd,khd->hqk', query_tile, key_tile, preferred_element_type=j...  3.75 us
    dot_general x3, matrix products, tile_backward(): jnp.einsum('qhd,khd->hqk', delta_part, value_part, preferred_element_type...  2.79 us
    dot_general x3, matrix products, local(): jnp.einsum('hqk,khd->qhd', weights, value_part, preferred_element_type=jn...  1.86 us
  transfers between devices with their start and end apart: 8, of which 3 were waited for; matrix products, arithmetic and copies ran while one was open for 19% of the time, Pallas kernels for 0%

commit v1 on v0

v1 whole, which is shorter than its diff:
```python
import functools

import jax
import jax.numpy as jnp
from jax import lax
from jax.experimental import pallas as pl
from jax.experimental.pallas import tpu as pltpu
from jax.sharding import PartitionSpec as P

DH = 128
REACH = 2
EPSILON = 1e-05
VMEM_LIMIT = 48 * 1024 * 1024

NT = (((1,), (1,)), ((), ()))
NN = (((1,), (0,)), ((), ()))


def dot(left, right, dims):
    return lax.dot_general(left, right, dims, preferred_element_type=jnp.float32)


def column(row, width):
    return jnp.transpose(jnp.broadcast_to(row, (width, row.shape[1])))


def lane_sums(values):
    ones = jnp.ones((8, values.shape[1]), jnp.float32)
    return lax.dot_general(
        ones, values, NT, precision=lax.Precision.HIGHEST, preferred_element_type=jnp.float32
    )[:1]


def chunk_of(rows):
    return 256 if rows % 256 == 0 else rows


def key_chunks(offset, chunk, chunks):
    if offset == 0:
        return range(chunk + 1)
    if offset == REACH:
        return range(chunk, chunks)
    return range(chunks)


def query_mask(start, rows, size, offset, chunk, other):
    keys = lax.broadcasted_iota(jnp.int32, (size, size), 1) + (other * size - offset * rows)
    mask = keys.astype(jnp.float32) >= start
    if offset == 0 and other == chunk:
        queries = lax.broadcasted_iota(jnp.int32, (size, size), 0) + chunk * size
        mask = mask & (keys <= queries)
    return mask


def key_mask(last, rows, size, offset, chunk, other):
    queries = lax.broadcasted_iota(jnp.int32, (size, size), 1) + (chunk * size + offset * rows)
    mask = queries.astype(jnp.float32) <= last
    if offset == 0 and other == chunk:
        keys = lax.broadcasted_iota(jnp.int32, (size, size), 0) + other * size
        mask = mask & (keys <= queries)
    return mask


def forward_kernel(factor, start_ref, gate_ref, up_ref, q_ref, *refs):
    kv = refs[: 2 * (REACH + 1)]
    att_ref, stats_ref = refs[2 * (REACH + 1) :]
    rows, features = q_ref.shape
    size = chunk_of(rows)
    chunks = rows // size
    starts = column(start_ref[...], size)
    for head in range(features // DH):
        lanes = slice(head * DH, head * DH + DH)
        for chunk in range(chunks):
            here = slice(chunk * size, chunk * size + size)
            query = q_ref[here, lanes]
            total = jnp.zeros((size, DH), jnp.float32)
            for offset in range(REACH + 1):
                for other in key_chunks(offset, chunk, chunks):
                    there = slice(other * size, other * size + size)
                    scores = dot(query, kv[2 * offset][there, lanes], NT) * factor
                    mask = query_mask(starts[here], rows, size, offset, chunk, other)
                    weights = jnp.where(mask, scores * jax.nn.sigmoid(scores), 0.0)
                    total += dot(weights.astype(jnp.bfloat16), kv[2 * offset + 1][there, lanes], NN)
            att_ref[here, lanes] = total
    att = att_ref[...]
    scaled = up_ref[...].astype(jnp.float32) * gate_ref[...].astype(jnp.float32)
    stats_ref[0:1, :] = lane_sums(att)
    stats_ref[1:2, :] = lane_sums(att * att)
    stats_ref[2:3, :] = lane_sums(scaled)
    stats_ref[3:4, :] = lane_sums(scaled * att)


def delta_kernel(total_features, att_ref, gate_ref, up_ref, stats_ref, out_ref, grad_gate_ref, delta_ref):
    stats = jnp.sum(stats_ref[...], axis=0)
    width = att_ref.shape[1]
    average = stats[0:1] / total_features
    inverse = lax.rsqrt(stats[1:2] / total_features - average * average + EPSILON)
    first = stats[2:3] / total_features
    second = inverse * (stats[3:4] - average * stats[2:3]) / total_features
    average, inverse, first, second = [column(row, width) for row in (average, inverse, first, second)]
    normed = (att_ref[...] - average) * inverse
    gate = gate_ref[...].astype(jnp.float32)
    up = up_ref[...].astype(jnp.float32)
    out_ref[...] = (normed * gate).astype(jnp.bfloat16)
    grad_gate_ref[...] = (up * normed).astype(jnp.bfloat16)
    delta_ref[...] = (inverse * (up * gate - first - normed * second)).astype(jnp.bfloat16)


def near_kernel(factor, start_ref, last_ref, q_ref, d_ref, *refs):
    kv = refs[: 2 * (REACH + 1)]
    gq_ref, gk_ref, gv_ref = refs[2 * (REACH + 1) :]
    rows, features = q_ref.shape
    size = chunk_of(rows)
    chunks = rows // size
    starts = column(start_ref[...], size)
    for head in range(features // DH):
        lanes = slice(head * DH, head * DH + DH)
        for chunk in range(chunks):
            here = slice(chunk * size, chunk * size + size)
            query = q_ref[here, lanes]
            delta = d_ref[here, lanes]
            total = jnp.zeros((size, DH), jnp.float32)
            for offset in range(REACH + 1):
                for other in key_chunks(offset, chunk, chunks):
                    there = slice(other * size, other * size + size)
                    key = kv[2 * offset][there, lanes]
                    scores = dot(query, key, NT) * factor
                    sigmoid = jax.nn.sigmoid(scores)
                    pulled = dot(delta, kv[2 * offset + 1][there, lanes], NT)
                    mask = query_mask(starts[here], rows, size, offset, chunk, other)
                    grad = jnp.where(mask, pulled * sigmoid * (1.0 + scores * (1.0 - sigmoid)), 0.0)
                    total += dot(grad.astype(jnp.bfloat16), key, NN)
            gq_ref[here, lanes] = (total * factor).astype(jnp.bfloat16)
    add_key_side(factor, 0, last_ref, kv[0], kv[1], q_ref, d_ref, None, None, gk_ref, gv_ref)


def add_key_side(factor, offset, last_ref, k_ref, v_ref, q_ref, d_ref, bk_ref, bv_ref, gk_ref, gv_ref):
    rows, features = q_ref.shape
    size = chunk_of(rows)
    chunks = rows // size
    lasts = column(last_ref[...], size)
    for head in range(features // DH):
        lanes = slice(head * DH, head * DH + DH)
        for other in range(chunks):
            there = slice(other * size, other * size + size)
            key = k_ref[there, lanes]
            value = v_ref[there, lanes]
            key_total = jnp.zeros((size, DH), jnp.float32)
            value_total = jnp.zeros((size, DH), jnp.float32)
            for chunk in range(chunks):
                if other not in key_chunks(offset, chunk, chunks):
                    continue
                here = slice(chunk * size, chunk * size + size)
                query = q_ref[here, lanes]
                delta = d_ref[here, lanes]
                scores = dot(key, query, NT) * factor
                sigmoid = jax.nn.sigmoid(scores)
                pulled = dot(value, delta, NT)
                mask = key_mask(lasts[there], rows, size, offset, chunk, other)
                weights = jnp.where(mask, scores * sigmoid, 0.0).astype(jnp.bfloat16)
                grad = jnp.where(mask, pulled * sigmoid * (1.0 + scores * (1.0 - sigmoid)), 0.0)
                key_total += dot(grad.astype(jnp.bfloat16), query, NN)
                value_total += dot(weights, delta, NN)
            if bk_ref is not None:
                key_total += bk_ref[there, lanes]
                value_total += bv_ref[there, lanes]
            gk_ref[there, lanes] = key_total
            gv_ref[there, lanes] = value_total


def far_kernel(factor, last_ref, k_ref, v_ref, bk_ref, bv_ref, *refs):
    qd = refs[: 2 * REACH]
    gk_ref, gv_ref, key_sum, value_sum = refs[2 * REACH :]
    key_sum[...] = bk_ref[...]
    value_sum[...] = bv_ref[...]
    for offset in range(1, REACH + 1):
        add_key_side(
            factor, offset, last_ref, k_ref, v_ref, qd[2 * offset - 2], qd[2 * offset - 1],
            key_sum, value_sum, key_sum, value_sum,
        )
    gk_ref[...] = (key_sum[...] * factor).astype(jnp.bfloat16)
    gv_ref[...] = value_sum[...].astype(jnp.bfloat16)


def call(kernel, outs, *args, scratch=()):
    return pl.pallas_call(
        kernel,
        out_shape=[jax.ShapeDtypeStruct(shape, dtype) for shape, dtype in outs],
        scratch_shapes=list(scratch),
        compiler_params=pltpu.CompilerParams(vmem_limit_bytes=VMEM_LIMIT),
    )(*args)


def shift(value, axis, steps):
    count = lax.axis_size(axis)
    return lax.ppermute(value, axis, [(source, (source + steps) % count) for source in range(count)])


def local(queries, key_vectors, value_vectors, gating, bounds, cotangent):
    block = queries.shape
    rows_dev = block[0]
    factor = DH ** (-0.5)
    heads = lax.axis_size("heads")
    first_row = lax.axis_index("rows") * rows_dev
    relative = (bounds - first_row).astype(jnp.float32)
    start, last = relative[0:1], relative[1:2]

    kv = [key_vectors, value_vectors]
    for offset in range(1, REACH + 1):
        kv += [shift(key_vectors, "rows", offset), shift(value_vectors, "rows", offset)]
    later = [shift(queries, "rows", -offset) for offset in range(1, REACH + 1)]

    attended, stats = call(
        functools.partial(forward_kernel, factor),
        [(block, jnp.float32), ((4, rows_dev), jnp.float32)],
        start, gating, cotangent, queries, *kv,
    )
    stats = jnp.stack([stats] + [shift(stats, "heads", step) for step in range(1, heads)])
    layer_out, grad_gating, delta = call(
        functools.partial(delta_kernel, float(block[1] * heads)),
        [(block, jnp.bfloat16)] * 3,
        attended, gating, cotangent, stats,
    )
    delta_later = [shift(delta, "rows", -offset) for offset in range(1, REACH + 1)]
    grad_queries, grad_key, grad_value = call(
        functools.partial(near_kernel, factor),
        [(block, jnp.bfloat16), (block, jnp.float32), (block, jnp.float32)],
        start, last, queries, delta, *kv,
    )
    pairs = [value for pair in zip(later, delta_later) for value in pair]
    grad_keys, grad_values = call(
        functools.partial(far_kernel, factor),
        [(block, jnp.bfloat16)] * 2,
        last, key_vectors, value_vectors, grad_key, grad_value, *pairs,
        scratch=[pltpu.VMEM(block, jnp.float32)] * 2,
    )
    return (layer_out, grad_queries, grad_keys, grad_values, grad_gating)


def solution(mesh):
    return jax.shard_map(
        local,
        mesh=mesh,
        in_specs=(
            P("rows", "heads"),
            P("rows", "heads"),
            P("rows", "heads"),
            P("rows", "heads"),
            P(None, "rows"),
            P("rows", "heads"),
        ),
        out_specs=(P("rows", "heads"),) * 5,
        check_vma=False,
    )
```

time: 67.4 us -> 44.6 us (0.66)
  the two profiles are of different devices: /device:TPU:22 before, /device:TPU:0 now
where the time goes in v1:
time: 44.6 us; the launch traced here: 44.4 us
  starting transfers between devices  16.4 us (37%)
  waiting for transfers between devices  12.9 us (29%)
  Pallas kernels  10.1 us (23%)
  local copies, waits for them, and re-layouts  4.33 us (10%)
  between operations  0.7 us (2%)
    ppermute x11, starting transfers between devices, shift(): lax.ppermute(value, axis, [(source, (source + steps) % count) for source...  16.4 us
    ppermute x11, waiting for transfers between devices, shift(): lax.ppermute(value, axis, [(source, (source + steps) % count) for source...  12.9 us
    pallas_call x4, Pallas kernels, call(): pl.pallas_call(kernel, out_shape=[jax.ShapeDtypeStruct(shape, dtype) for...  10.1 us
    unnamed x18, local copies, waits for them, and re-layouts  4.32 us
  transfers between devices with their start and end apart: 11, of which 4 were waited for; matrix products, arithmetic and copies ran while one was open for 0% of the time, Pallas kernels for 10%

profile of v1, /device:TPU:0, one launch (start us, length us, event | category | flops | bytes accessed | tf_op | source)
XLA Modules:
  0.0 44.4 jit_solution(18272557213112573535)
XLA Ops:
  0.6 3.0 %collective-permute-start = (bf16[512,128]{1,0:T(8,128)(2,1)}, bf16[512,128]{1,0:T(8,128)(2,1)S(1)}, u32[]{:S(2)}, u32[]{:S(2)}) collective-permute-start(bf16[512,128]{1,0:T(8,128)(2,1)} %k_ref.1), channel_id=1, source_target_pairs={{0,4},{4,8},{8,12},{12,16},{16,20},{20,24},{24,28},{28,0},{1,5},{5... | collective-permute-start | bytes 393224 | tf_op jit(solution)/shard_map/ppermute | solution.py:196
  3.7 1.6 %collective-permute-start.2 = (bf16[512,128]{1,0:T(8,128)(2,1)}, bf16[512,128]{1,0:T(8,128)(2,1)S(1)}, u32[]{:S(2)}, u32[]{:S(2)}) collective-permute-start(bf16[512,128]{1,0:T(8,128)(2,1)} %k_ref.1), channel_id=1, source_target_pairs={{0,8},{4,12},{8,16},{12,20},{16,24},{20,28},{24,0},{28,4},{1,9},{5... | collective-permute-start | bytes 393224 | tf_op jit(solution)/shard_map/ppermute | solution.py:196
  5.2 1.5 %collective-permute-start.1 = (bf16[512,128]{1,0:T(8,128)(2,1)}, bf16[512,128]{1,0:T(8,128)(2,1)S(1)}, u32[]{:S(2)}, u32[]{:S(2)}) collective-permute-start(bf16[512,128]{1,0:T(8,128)(2,1)} %v_ref.1), channel_id=1, source_target_pairs={{0,4},{4,8},{8,12},{12,16},{16,20},{20,24},{24,28},{28,0},{1,5},{5... | collective-permute-start | bytes 393224 | tf_op jit(solution)/shard_map/ppermute | solution.py:196
  6.7 1.6 %collective-permute-start.3 = (bf16[512,128]{1,0:T(8,128)(2,1)}, bf16[512,128]{1,0:T(8,128)(2,1)S(1)}, u32[]{:S(2)}, u32[]{:S(2)}) collective-permute-start(bf16[512,128]{1,0:T(8,128)(2,1)} %v_ref.1), channel_id=1, source_target_pairs={{0,8},{4,12},{8,16},{12,20},{16,24},{20,28},{24,0},{28,4},{1,9},{5... | collective-permute-start | bytes 393224 | tf_op jit(solution)/shard_map/ppermute | solution.py:196
  8.3 0.0 copy-start.8
  8.3 0.7 %copy-done.8 = s32[2,512]{1,0:T(2,128)S(1)} copy-done((s32[2,512]{1,0:T(2,128)S(1)}, s32[2,512]{1,0:T(2,128)}, u32[]{:S(2)}) %copy-start.8) | copy-done | bytes 4120
  9.0 2.2 %collective-permute-done.refs_2_ = bf16[512,128]{1,0:T(8,128)(2,1)S(1)} collective-permute-done((bf16[512,128]{1,0:T(8,128)(2,1)}, bf16[512,128]{1,0:T(8,128)(2,1)S(1)}, u32[]{:S(2)}, u32[]{:S(2)}) %collective-permute-start) | collective-permute-done | bytes 131104 | tf_op jit(solution)/shard_map/ppermute | solution.py:196
  11.2 5.6 %collective-permute-done.1.refs_3_ = bf16[512,128]{1,0:T(8,128)(2,1)S(1)} collective-permute-done((bf16[512,128]{1,0:T(8,128)(2,1)}, bf16[512,128]{1,0:T(8,128)(2,1)S(1)}, u32[]{:S(2)}, u32[]{:S(2)}) %collective-permute-start.1) | collective-permute-done | bytes 131104 | tf_op jit(solution)/shard_map/ppermute | solution.py:196
  16.8 0.0 collective-permute-done.2.refs_4_
  16.8 0.0 collective-permute-done.3.refs_5_
  16.9 0.0 copy-start
  16.9 0.9 %copy-done = bf16[512,128]{1,0:T(8,128)(2,1)S(1)} copy-done((bf16[512,128]{1,0:T(8,128)(2,1)S(1)}, bf16[512,128]{1,0:T(8,128)(2,1)}, u32[]{:S(2)}) %copy-start) | copy-done | bytes 131096
  17.8 0.0 copy-start.2
  17.8 0.9 %copy-done.2 = bf16[512,128]{1,0:T(8,128)(2,1)S(1)} copy-done((bf16[512,128]{1,0:T(8,128)(2,1)S(1)}, bf16[512,128]{1,0:T(8,128)(2,1)}, u32[]{:S(2)}) %copy-start.2) | copy-done | bytes 131096
  18.7 0.0 copy-start.4
  18.7 0.9 %copy-done.4 = bf16[512,128]{1,0:T(8,128)(2,1)S(1)} copy-done((bf16[512,128]{1,0:T(8,128)(2,1)S(1)}, bf16[512,128]{1,0:T(8,128)(2,1)}, u32[]{:S(2)}) %copy-start.4) | copy-done | bytes 131096
  19.6 0.0 copy-start.6
  19.6 0.9 %copy-done.6 = bf16[512,128]{1,0:T(8,128)(2,1)S(1)} copy-done((bf16[512,128]{1,0:T(8,128)(2,1)S(1)}, bf16[512,128]{1,0:T(8,128)(2,1)}, u32[]{:S(2)}) %copy-start.6) | copy-done | bytes 131096
  20.5 0.0 copy-start.5
  20.5 0.0 copy-start.7
  20.5 3.1 %shard_map.101 = (f32[512,128]{1,0:T(8,128)S(1)}, f32[4,512]{1,0:T(4,128)S(1)}) custom-call(f32[1,512]{1,0:T(1,128)S(1)} %get-tuple-element.26.start_ref, bf16[512,128]{1,0:T(8,128)(2,1)S(1)} %copy-done.4, bf16[512,128]{1,0:T(8,128)(2,1)S(1)} %copy-done.6, bf16[512,128]{1,0:T(8,128)(2,1)} %q_ref.3, bf16[512,128]{1,0:T(8,128)(2,1)S(1)} %copy-done, ...), custom_call_target="tpu_custom_call" | custom-call | tf_op jit(solution)/shard_map/pallas_call | solution.py:186
  23.6 0.0 collective-permute-start.6
  23.6 1.7 %collective-permute-start.5 = (f32[4,512]{1,0:T(4,128)S(1)}, f32[4,512]{1,0:T(4,128)S(1)}, u32[]{:S(2)}, u32[]{:S(2)}) collective-permute-start(f32[4,512]{1,0:T(4,128)S(1)} %get-tuple-element.16), channel_id=1, source_target_pairs={{0,2},{1,3},{2,0},{3,1},{4,6},{5,7},{6,4},{7,5},{8,10},{9,11},{10,... | collective-permute-start | bytes 24584 | tf_op jit(solution)/shard_map/ppermute | solution.py:196
  25.3 0.2 collective-permute-start.4
  25.5 3.5 %collective-permute-start.7 = (bf16[512,128]{1,0:T(8,128)(2,1)}, bf16[512,128]{1,0:T(8,128)(2,1)S(1)}, u32[]{:S(2)}, u32[]{:S(2)}) collective-permute-start(bf16[512,128]{1,0:T(8,128)(2,1)} %q_ref.3), channel_id=1, source_target_pairs={{0,28},{4,0},{8,4},{12,8},{16,12},{20,16},{24,20},{28,24},{1,29},{... | collective-permute-start | bytes 393224 | tf_op jit(solution)/shard_map/ppermute | solution.py:196
  29.0 0.5 %collective-permute-start.9 = (bf16[512,128]{1,0:T(8,128)(2,1)}, bf16[512,128]{1,0:T(8,128)(2,1)S(1)}, u32[]{:S(2)}, u32[]{:S(2)}) collective-permute-start(bf16[512,128]{1,0:T(8,128)(2,1)} %q_ref.3), channel_id=1, source_target_pairs={{0,24},{4,28},{8,0},{12,4},{16,8},{20,12},{24,16},{28,20},{1,25},{... | collective-permute-start | bytes 393224 | tf_op jit(solution)/shard_map/ppermute | solution.py:196
  29.4 0.0 collective-permute-done.6
  29.4 0.0 collective-permute-done.5
  29.5 0.0 collective-permute-done.4
  29.5 0.0 copy-done.5
  29.5 0.0 copy-done.7
  29.5 0.0 copy-start.1
  29.5 0.0 copy-start.3
  29.5 0.9 %shard_map.102 = (bf16[512,128]{1,0:T(8,128)(2,1)}, bf16[512,128]{1,0:T(8,128)(2,1)}, bf16[512,128]{1,0:T(8,128)(2,1)S(1)}) custom-call(f32[512,128]{1,0:T(8,128)S(1)} %get-tuple-element.15.att_ref, bf16[512,128]{1,0:T(8,128)(2,1)S(1)} %copy-done.5, bf16[512,128]{1,0:T(8,128)(2,1)S(1)} %copy-done.7, f32[4,4,512]{2,1,0:T(4,128)S(1)} %pad_maximum_fusion.stats_ref), custom_call_target="tpu_custom_call" | custom-call | tf_op jit(solution)/shard_map/pallas_call | solution.py:186
  30.5 2.4 %collective-permute-start.8 = (bf16[512,128]{1,0:T(8,128)(2,1)S(1)}, bf16[512,128]{1,0:T(8,128)(2,1)S(1)}, u32[]{:S(2)}, u32[]{:S(2)}) collective-permute-start(bf16[512,128]{1,0:T(8,128)(2,1)S(1)} %get-tuple-element.18.d_ref), channel_id=1, source_target_pairs={{0,28},{4,0},{8,4},{12,8},{16,12},{20,16},{24,20},{28,24},{1,29},{... | collective-permute-start | bytes 393224 | tf_op jit(solution)/shard_map/ppermute | solution.py:196
  32.8 0.5 %collective-permute-start.10 = (bf16[512,128]{1,0:T(8,128)(2,1)S(1)}, bf16[512,128]{1,0:T(8,128)(2,1)S(1)}, u32[]{:S(2)}, u32[]{:S(2)}) collective-permute-start(bf16[512,128]{1,0:T(8,128)(2,1)S(1)} %get-tuple-element.18.d_ref), channel_id=1, source_target_pairs={{0,24},{4,28},{8,0},{12,4},{16,8},{20,12},{24,16},{28,20},{1,25},{... | collective-permute-start | bytes 393224 | tf_op jit(solution)/shard_map/ppermute | solution.py:196
  33.3 0.0 copy-done.1
  33.3 0.0 copy-done.3
  33.3 3.6 %shard_map.103 = (bf16[512,128]{1,0:T(8,128)(2,1)}, f32[512,128]{1,0:T(8,128)S(1)}, f32[512,128]{1,0:T(8,128)S(1)}) custom-call(f32[1,512]{1,0:T(1,128)S(1)} %get-tuple-element.26.start_ref, f32[1,512]{1,0:T(1,128)S(1)} %get-tuple-element.25.last_ref, bf16[512,128]{1,0:T(8,128)(2,1)} %q_ref.3, bf16[512,128]{1,0:T(8,128)(2,1)S(1)} %get-tuple-element.18.d_ref, ...), custom_call_target="tpu_custom_call" | custom-call | tf_op jit(solution)/shard_map/pallas_call | solution.py:186
  36.9 0.0 collective-permute-done.7.refs_0_
  36.9 0.0 collective-permute-done.9.refs_2_
  36.9 1.7 %collective-permute-done.8.refs_1_ = bf16[512,128]{1,0:T(8,128)(2,1)S(1)} collective-permute-done((bf16[512,128]{1,0:T(8,128)(2,1)S(1)}, bf16[512,128]{1,0:T(8,128)(2,1)S(1)}, u32[]{:S(2)}, u32[]{:S(2)}) %collective-permute-start.8) | collective-permute-done | bytes 131104 | tf_op jit(solution)/shard_map/ppermute | solution.py:196
  38.6 3.3 %collective-permute-done.10.refs_3_ = bf16[512,128]{1,0:T(8,128)(2,1)S(1)} collective-permute-done((bf16[512,128]{1,0:T(8,128)(2,1)S(1)}, bf16[512,128]{1,0:T(8,128)(2,1)S(1)}, u32[]{:S(2)}, u32[]{:S(2)}) %collective-permute-start.10) | collective-permute-done | bytes 131104 | tf_op jit(solution)/shard_map/ppermute | solution.py:196
  42.0 2.4 %shard_map.104 = (bf16[512,128]{1,0:T(8,128)(2,1)}, bf16[512,128]{1,0:T(8,128)(2,1)}) custom-call(f32[1,512]{1,0:T(1,128)S(1)} %get-tuple-element.25.last_ref, bf16[512,128]{1,0:T(8,128)(2,1)S(1)} %copy-done.1, bf16[512,128]{1,0:T(8,128)(2,1)S(1)} %copy-done.3, f32[512,128]{1,0:T(8,128)S(1)} %get-tuple-element.20.bk_ref, ...), custom_call_target="tpu_custom_call" | custom-call | tf_op jit(solution)/shard_map/pallas_call | solution.py:186
  (3 shorter events, 0.0 us)
Async XLA Ops:
  0.6 10.6 %collective-permute-start = (bf16[512,128]{1,0:T(8,128)(2,1)}, bf16[512,128]{1,0:T(8,128)(2,1)S(1)}, u32[]{:S(2)}, u32[]{:S(2)}) collective-permute-start(bf16[512,128]{1,0:T(8,128)(2,1)} %k_ref.1), channel_id=1, source_target_pairs={{0,4},{4,8},{8,12},{12,16},{16,20},{20,24},{24,28},{28,0},{1,5},{5... | collective-permute-start | bytes 393224 | tf_op jit(solution)/shard_map/ppermute | solution.py:196
  3.7 13.2 %collective-permute-start.2 = (bf16[512,128]{1,0:T(8,128)(2,1)}, bf16[512,128]{1,0:T(8,128)(2,1)S(1)}, u32[]{:S(2)}, u32[]{:S(2)}) collective-permute-start(bf16[512,128]{1,0:T(8,128)(2,1)} %k_ref.1), channel_id=1, source_target_pairs={{0,8},{4,12},{8,16},{12,20},{16,24},{20,28},{24,0},{28,4},{1,9},{5... | collective-permute-start | bytes 393224 | tf_op jit(solution)/shard_map/ppermute | solution.py:196
  5.2 11.6 %collective-permute-start.1 = (bf16[512,128]{1,0:T(8,128)(2,1)}, bf16[512,128]{1,0:T(8,128)(2,1)S(1)}, u32[]{:S(2)}, u32[]{:S(2)}) collective-permute-start(bf16[512,128]{1,0:T(8,128)(2,1)} %v_ref.1), channel_id=1, source_target_pairs={{0,4},{4,8},{8,12},{12,16},{16,20},{20,24},{24,28},{28,0},{1,5},{5... | collective-permute-start | bytes 393224 | tf_op jit(solution)/shard_map/ppermute | solution.py:196
  6.7 10.1 %collective-permute-start.3 = (bf16[512,128]{1,0:T(8,128)(2,1)}, bf16[512,128]{1,0:T(8,128)(2,1)S(1)}, u32[]{:S(2)}, u32[]{:S(2)}) collective-permute-start(bf16[512,128]{1,0:T(8,128)(2,1)} %v_ref.1), channel_id=1, source_target_pairs={{0,8},{4,12},{8,16},{12,20},{16,24},{20,28},{24,0},{28,4},{1,9},{5... | collective-permute-start | bytes 393224 | tf_op jit(solution)/shard_map/ppermute | solution.py:196
  8.3 0.7 %copy-start.8 = (s32[2,512]{1,0:T(2,128)S(1)}, s32[2,512]{1,0:T(2,128)}, u32[]{:S(2)}) copy-start(s32[2,512]{1,0:T(2,128)} %param.10) | copy-start | bytes 12292
  16.9 0.9 %copy-start = (bf16[512,128]{1,0:T(8,128)(2,1)S(1)}, bf16[512,128]{1,0:T(8,128)(2,1)}, u32[]{:S(2)}) copy-start(bf16[512,128]{1,0:T(8,128)(2,1)} %k_ref.1) | copy-start | bytes 393220
  17.8 0.9 %copy-start.2 = (bf16[512,128]{1,0:T(8,128)(2,1)S(1)}, bf16[512,128]{1,0:T(8,128)(2,1)}, u32[]{:S(2)}) copy-start(bf16[512,128]{1,0:T(8,128)(2,1)} %v_ref.1) | copy-start | bytes 393220
  18.7 0.9 %copy-start.4 = (bf16[512,128]{1,0:T(8,128)(2,1)S(1)}, bf16[512,128]{1,0:T(8,128)(2,1)}, u32[]{:S(2)}) copy-start(bf16[512,128]{1,0:T(8,128)(2,1)} %gate_ref.3) | copy-start | bytes 393220
  19.6 0.9 %copy-start.6 = (bf16[512,128]{1,0:T(8,128)(2,1)S(1)}, bf16[512,128]{1,0:T(8,128)(2,1)}, u32[]{:S(2)}) copy-start(bf16[512,128]{1,0:T(8,128)(2,1)} %up_ref.3) | copy-start | bytes 393220
  20.5 9.0 %copy-start.5 = (bf16[512,128]{1,0:T(8,128)(2,1)S(1)}, bf16[512,128]{1,0:T(8,128)(2,1)}, u32[]{:S(2)}) copy-start(bf16[512,128]{1,0:T(8,128)(2,1)} %gate_ref.3) | copy-start | bytes 393220
  20.5 9.0 %copy-start.7 = (bf16[512,128]{1,0:T(8,128)(2,1)S(1)}, bf16[512,128]{1,0:T(8,128)(2,1)}, u32[]{:S(2)}) copy-start(bf16[512,128]{1,0:T(8,128)(2,1)} %up_ref.3) | copy-start | bytes 393220
  23.6 5.9 %collective-permute-start.6 = (f32[4,512]{1,0:T(4,128)S(1)}, f32[4,512]{1,0:T(4,128)S(1)}, u32[]{:S(2)}, u32[]{:S(2)}) collective-permute-start(f32[4,512]{1,0:T(4,128)S(1)} %get-tuple-element.16), channel_id=1, source_target_pairs={{0,3},{1,0},{2,1},{3,2},{4,7},{5,4},{6,5},{7,6},{8,11},{9,8},{10,9... | collective-permute-start | bytes 24584 | tf_op jit(solution)/shard_map/ppermute | solution.py:196
  23.6 5.9 %collective-permute-start.5 = (f32[4,512]{1,0:T(4,128)S(1)}, f32[4,512]{1,0:T(4,128)S(1)}, u32[]{:S(2)}, u32[]{:S(2)}) collective-permute-start(f32[4,512]{1,0:T(4,128)S(1)} %get-tuple-element.16), channel_id=1, source_target_pairs={{0,2},{1,3},{2,0},{3,1},{4,6},{5,7},{6,4},{7,5},{8,10},{9,11},{10,... | collective-permute-start | bytes 24584 | tf_op jit(solution)/shard_map/ppermute | solution.py:196
  25.3 4.2 %collective-permute-start.4 = (f32[4,512]{1,0:T(4,128)S(1)}, f32[4,512]{1,0:T(4,128)S(1)}, u32[]{:S(2)}, u32[]{:S(2)}) collective-permute-start(f32[4,512]{1,0:T(4,128)S(1)} %get-tuple-element.16), channel_id=1, source_target_pairs={{0,1},{1,2},{2,3},{3,0},{4,5},{5,6},{6,7},{7,4},{8,9},{9,10},{10,1... | collective-permute-start | bytes 24584 | tf_op jit(solution)/shard_map/ppermute | solution.py:196
  25.5 11.4 %collective-permute-start.7 = (bf16[512,128]{1,0:T(8,128)(2,1)}, bf16[512,128]{1,0:T(8,128)(2,1)S(1)}, u32[]{:S(2)}, u32[]{:S(2)}) collective-permute-start(bf16[512,128]{1,0:T(8,128)(2,1)} %q_ref.3), channel_id=1, source_target_pairs={{0,28},{4,0},{8,4},{12,8},{16,12},{20,16},{24,20},{28,24},{1,29},{... | collective-permute-start | bytes 393224 | tf_op jit(solution)/shard_map/ppermute | solution.py:196
  29.0 8.0 %collective-permute-start.9 = (bf16[512,128]{1,0:T(8,128)(2,1)}, bf16[512,128]{1,0:T(8,128)(2,1)S(1)}, u32[]{:S(2)}, u32[]{:S(2)}) collective-permute-start(bf16[512,128]{1,0:T(8,128)(2,1)} %q_ref.3), channel_id=1, source_target_pairs={{0,24},{4,28},{8,0},{12,4},{16,8},{20,12},{24,16},{28,20},{1,25},{... | collective-permute-start | bytes 393224 | tf_op jit(solution)/shard_map/ppermute | solution.py:196
  29.5 3.8 %copy-start.1 = (bf16[512,128]{1,0:T(8,128)(2,1)S(1)}, bf16[512,128]{1,0:T(8,128)(2,1)}, u32[]{:S(2)}) copy-start(bf16[512,128]{1,0:T(8,128)(2,1)} %k_ref.1) | copy-start | bytes 393220
  29.5 3.8 %copy-start.3 = (bf16[512,128]{1,0:T(8,128)(2,1)S(1)}, bf16[512,128]{1,0:T(8,128)(2,1)}, u32[]{:S(2)}) copy-start(bf16[512,128]{1,0:T(8,128)(2,1)} %v_ref.1) | copy-start | bytes 393220
  30.5 8.2 %collective-permute-start.8 = (bf16[512,128]{1,0:T(8,128)(2,1)S(1)}, bf16[512,128]{1,0:T(8,128)(2,1)S(1)}, u32[]{:S(2)}, u32[]{:S(2)}) collective-permute-start(bf16[512,128]{1,0:T(8,128)(2,1)S(1)} %get-tuple-element.18.d_ref), channel_id=1, source_target_pairs={{0,28},{4,0},{8,4},{12,8},{16,12},{20,16},{24,20},{28,24},{1,29},{... | collective-permute-start | bytes 393224 | tf_op jit(solution)/shard_map/ppermute | solution.py:196
  32.8 9.1 %collective-permute-start.10 = (bf16[512,128]{1,0:T(8,128)(2,1)S(1)}, bf16[512,128]{1,0:T(8,128)(2,1)S(1)}, u32[]{:S(2)}, u32[]{:S(2)}) collective-permute-start(bf16[512,128]{1,0:T(8,128)(2,1)S(1)} %get-tuple-element.18.d_ref), channel_id=1, source_target_pairs={{0,24},{4,28},{8,0},{12,4},{16,8},{20,12},{24,16},{28,20},{1,25},{... | collective-permute-start | bytes 393224 | tf_op jit(solution)/shard_map/ppermute | solution.py:196

commit v2 on v1

v2 whole, which is shorter than its diff:
```python
import functools

import jax
import jax.numpy as jnp
from jax import lax
from jax.experimental import pallas as pl
from jax.experimental.pallas import tpu as pltpu
from jax.sharding import PartitionSpec as P

DH = 128
REACH = 2
EPSILON = 1e-05
VMEM_LIMIT = 20 * 1024 * 1024

LANES = 128
NT = (((1,), (1,)), ((), ()))
NN = (((1,), (0,)), ((), ()))


def dot(left, right, dims):
    return lax.dot_general(left, right, dims, preferred_element_type=jnp.float32)


def column(row, width):
    return jnp.transpose(jnp.broadcast_to(row, (width, row.shape[1])))


def lane_sums(values):
    ones = jnp.ones((8, values.shape[1]), jnp.float32)
    return lax.dot_general(
        ones, values, NT, precision=lax.Precision.HIGHEST, preferred_element_type=jnp.float32
    )[:1]


def chunk_of(rows):
    return 256 if rows % 256 == 0 else rows


def query_mask(start, rows, offset, chunk):
    size, width = start.shape
    keys = lax.broadcasted_iota(jnp.int32, (size, width), 1) - offset * rows
    mask = keys.astype(jnp.float32) >= start
    if offset == 0:
        queries = lax.broadcasted_iota(jnp.int32, (size, width), 0) + chunk * size
        mask = mask & (keys <= queries)
    return mask


def key_mask(last, rows, offset, chunk):
    size, width = last.shape
    queries = lax.broadcasted_iota(jnp.int32, (size, width), 1) + offset * rows
    mask = queries.astype(jnp.float32) <= last
    if offset == 0:
        keys = lax.broadcasted_iota(jnp.int32, (size, width), 0) + chunk * size
        mask = mask & (keys <= queries)
    return mask


def silu_and_slope(scores, mask):
    scores = jnp.where(mask, scores, 0.0)
    sigmoid = jax.nn.sigmoid(scores)
    weights = scores * sigmoid
    slope = jnp.where(mask, sigmoid + weights * (1.0 - sigmoid), 0.0)
    return weights.astype(jnp.bfloat16), slope


def parts_of(rows, features):
    size = chunk_of(rows)
    lanes = [(head, slice(head * DH, head * DH + DH)) for head in range(features // DH)]
    chunks = [(chunk, slice(chunk * size, chunk * size + size)) for chunk in range(rows // size)]
    return lanes, chunks


def widen(ref, width):
    return jnp.concatenate([ref[...]] * (width // ref.shape[1]), axis=1)


def column_kernel(row_ref, start_ref, last_ref):
    start_ref[...] = column(row_ref[0:1, :], LANES)
    last_ref[...] = column(row_ref[1:2, :], LANES)


def own_kernel(factor, start_ref, last_ref, q_ref, k_ref, gate_ref, up_ref, *refs):
    weight_ref, slope_ref, weight_t_ref, slope_t_ref, scaled_ref, sum_ref = refs
    rows, features = q_ref.shape
    lanes, chunks = parts_of(rows, features)
    starts = widen(start_ref, rows)
    lasts = widen(last_ref, rows)
    for head, at in lanes:
        for chunk, here in chunks:
            scores = dot(q_ref[here, at], k_ref[:, at], NT) * factor
            weights, slope = silu_and_slope(scores, query_mask(starts[here], rows, 0, chunk))
            weight_ref[head, here, :] = weights
            slope_ref[head, here, :] = slope
            scores = dot(k_ref[here, at], q_ref[:, at], NT) * factor
            weights, slope = silu_and_slope(scores, key_mask(lasts[here], rows, 0, chunk))
            weight_t_ref[head, here, :] = weights
            slope_t_ref[head, here, :] = slope
    scaled = up_ref[...].astype(jnp.float32) * gate_ref[...].astype(jnp.float32)
    scaled_ref[...] = scaled
    sum_ref[...] = lane_sums(scaled)


def weight_kernel(factor, start_ref, q_ref, *refs):
    keys, (weight_ref, slope_ref) = refs[:REACH], refs[REACH:]
    rows, features = q_ref.shape
    lanes, chunks = parts_of(rows, features)
    starts = widen(start_ref, rows)
    for head, at in lanes:
        for chunk, here in chunks:
            for offset in range(1, REACH + 1):
                scores = dot(q_ref[here, at], keys[offset - 1][:, at], NT) * factor
                weights, slope = silu_and_slope(scores, query_mask(starts[here], rows, offset, chunk))
                weight_ref[head, offset - 1, here, :] = weights
                slope_ref[head, offset - 1, here, :] = slope


def later_kernel(factor, last_ref, k_ref, *refs):
    queries, (weight_ref, slope_ref) = refs[:REACH], refs[REACH:]
    rows, features = k_ref.shape
    lanes, chunks = parts_of(rows, features)
    lasts = widen(last_ref, rows)
    for head, at in lanes:
        for chunk, here in chunks:
            for offset in range(1, REACH + 1):
                scores = dot(k_ref[here, at], queries[offset - 1][:, at], NT) * factor
                weights, slope = silu_and_slope(scores, key_mask(lasts[here], rows, offset, chunk))
                weight_ref[head, offset - 1, here, :] = weights
                slope_ref[head, offset - 1, here, :] = slope


def attend_kernel(own_weight_ref, scaled_ref, sum_ref, weight_ref, *refs):
    values, (att_ref, stats_ref) = refs[: REACH + 1], refs[REACH + 1 :]
    rows, features = scaled_ref.shape
    lanes, chunks = parts_of(rows, features)
    for head, at in lanes:
        for chunk, here in chunks:
            total = dot(own_weight_ref[head, here, :], values[0][:, at], NN)
            for offset in range(REACH):
                total += dot(weight_ref[head, offset, here, :], values[offset + 1][:, at], NN)
            att_ref[here, at] = total
    att = att_ref[...]
    stats_ref[0:1, :] = lane_sums(att)
    stats_ref[1:2, :] = lane_sums(att * att)
    stats_ref[2:3, :] = sum_ref[...]
    stats_ref[3:4, :] = lane_sums(scaled_ref[...] * att)


def delta_kernel(total_features, att_ref, scaled_ref, *refs):
    stats_refs, (normed_ref, delta_ref) = refs[:-2], refs[-2:]
    stats = stats_refs[0][...]
    for ref in stats_refs[1:]:
        stats += ref[...]
    width = att_ref.shape[1]
    average = stats[0:1] / total_features
    inverse = lax.rsqrt(stats[1:2] / total_features - average * average + EPSILON)
    first = stats[2:3] / total_features
    second = inverse * (stats[3:4] - average * stats[2:3]) / total_features
    average, inverse, first, second = [column(row, width) for row in (average, inverse, first, second)]
    normed = (att_ref[...] - average) * inverse
    normed_ref[...] = normed
    delta_ref[...] = (inverse * (scaled_ref[...] - first - normed * second)).astype(jnp.bfloat16)


def near_kernel(factor, q_ref, k_ref, v_ref, gate_ref, up_ref, d_ref, normed_ref, own_slope_ref,
                own_weight_t_ref, own_slope_t_ref, slope_ref, *refs):
    keys, values, refs = refs[:REACH], refs[REACH : 2 * REACH], refs[2 * REACH :]
    gq_ref, gk_ref, gv_ref, out_ref, gg_ref = refs
    rows, features = q_ref.shape
    lanes, chunks = parts_of(rows, features)
    normed = normed_ref[...]
    out_ref[...] = (normed * gate_ref[...].astype(jnp.float32)).astype(jnp.bfloat16)
    gg_ref[...] = (normed * up_ref[...].astype(jnp.float32)).astype(jnp.bfloat16)
    for head, at in lanes:
        for chunk, here in chunks:
            delta = d_ref[here, at]
            grad = (dot(delta, v_ref[:, at], NT) * own_slope_ref[head, here, :]).astype(jnp.bfloat16)
            total = dot(grad, k_ref[:, at], NN)
            for offset in range(REACH):
                grad = dot(delta, values[offset][:, at], NT) * slope_ref[head, offset, here, :]
                total += dot(grad.astype(jnp.bfloat16), keys[offset][:, at], NN)
            gq_ref[here, at] = (total * factor).astype(jnp.bfloat16)
            grad = dot(v_ref[here, at], d_ref[:, at], NT) * own_slope_t_ref[head, here, :]
            gk_ref[here, at] = dot(grad.astype(jnp.bfloat16), q_ref[:, at], NN)
            gv_ref[here, at] = dot(own_weight_t_ref[head, here, :], d_ref[:, at], NN)


def far_kernel(factor, v_ref, near_k_ref, near_v_ref, weight_ref, slope_ref, *refs):
    queries, deltas, (gk_ref, gv_ref) = refs[:REACH], refs[REACH : 2 * REACH], refs[2 * REACH :]
    rows, features = v_ref.shape
    lanes, chunks = parts_of(rows, features)
    for head, at in lanes:
        for chunk, here in chunks:
            key_total = near_k_ref[here, at]
            value_total = near_v_ref[here, at]
            for offset in range(REACH):
                delta = deltas[offset][:, at]
                value_total += dot(weight_ref[head, offset, here, :], delta, NN)
                grad = dot(v_ref[here, at], delta, NT) * slope_ref[head, offset, here, :]
                key_total += dot(grad.astype(jnp.bfloat16), queries[offset][:, at], NN)
            gv_ref[here, at] = value_total.astype(jnp.bfloat16)
            gk_ref[here, at] = (key_total * factor).astype(jnp.bfloat16)


def call(kernel, outs, *args, cost=None):
    vmem = pl.BlockSpec(memory_space=pltpu.VMEM)
    return pl.pallas_call(
        kernel,
        out_shape=[jax.ShapeDtypeStruct(shape, dtype) for shape, dtype in outs],
        in_specs=[vmem] * len(args),
        out_specs=[vmem] * len(outs),
        cost_estimate=cost,
        compiler_params=pltpu.CompilerParams(vmem_limit_bytes=VMEM_LIMIT),
    )(*args)


def shift(value, axis, steps, ring=True):
    count = lax.axis_size(axis)
    pairs = [(source, source + steps) for source in range(count)]
    if ring:
        pairs = [(source, target % count) for source, target in pairs]
    return lax.ppermute(value, axis, [(s, t) for s, t in pairs if 0 <= t < count])


def local(queries, key_vectors, value_vectors, gating, bounds, cotangent):
    block = queries.shape
    rows_dev = block[0]
    heads_dev = block[1] // DH
    factor = DH ** (-0.5)
    heads = lax.axis_size("heads")
    first_row = lax.axis_index("rows") * rows_dev
    relative = (bounds - first_row).astype(jnp.float32)
    half, full = jnp.bfloat16, jnp.float32
    square = (rows_dev, rows_dev)
    steps = range(1, REACH + 1)

    keys = [shift(key_vectors, "rows", offset) for offset in steps]
    values = [shift(value_vectors, "rows", offset) for offset in steps]

    starts, lasts = call(
        column_kernel, [((rows_dev, LANES), full)] * 2, relative, cost=pl.CostEstimate(flops=10**10, transcendentals=0, bytes_accessed=4*10**7),
    )
    own = (heads_dev, *square)
    own_weights, own_slopes, own_weights_t, own_slopes_t, scaled, scaled_sum = call(
        functools.partial(own_kernel, factor),
        [(own, half), (own, full), (own, half), (own, full), (block, full), ((1, rows_dev), full)],
        starts, lasts, queries, key_vectors, gating, cotangent,
    )
    pair = (heads_dev, REACH, *square)
    weights, slopes = call(
        functools.partial(weight_kernel, factor), [(pair, half), (pair, full)], starts, queries, *keys
    )
    tied, _ = lax.optimization_barrier((queries, weights))
    later = [shift(queries, "rows", -1), shift(tied, "rows", -2)]
    attended, stats = call(
        attend_kernel,
        [(block, full), ((4, rows_dev), full)],
        own_weights, scaled, scaled_sum, weights, value_vectors, *values,
    )
    weights_t, slopes_t = call(
        functools.partial(later_kernel, factor), [(pair, half), (pair, full)], lasts, key_vectors, *later
    )
    all_stats = [stats] + [shift(stats, "heads", step) for step in range(1, heads)]
    all_stats, weights_t = lax.optimization_barrier((all_stats, weights_t))
    normed, delta = call(
        functools.partial(delta_kernel, float(block[1] * heads)),
        [(block, full), (block, half)],
        attended, scaled, *all_stats,
    )
    deltas = [shift(delta, "rows", -offset) for offset in steps]
    grad_queries, near_key, near_value, layer_out, grad_gating = call(
        functools.partial(near_kernel, factor),
        [(block, half), (block, full), (block, full), (block, half), (block, half)],
        queries, key_vectors, value_vectors, gating, cotangent, delta, normed,
        own_slopes, own_weights_t, own_slopes_t, slopes, *keys, *values,
    )
    grad_keys, grad_values = call(
        functools.partial(far_kernel, factor),
        [(block, half)] * 2,
        value_vectors, near_key, near_value, weights_t, slopes_t, *later, *deltas,
    )
    return (layer_out, grad_queries, grad_keys, grad_values, grad_gating)


def solution(mesh):
    return jax.shard_map(
        local,
        mesh=mesh,
        in_specs=(
            P("rows", "heads"),
            P("rows", "heads"),
            P("rows", "heads"),
            P("rows", "heads"),
            P(None, "rows"),
            P("rows", "heads"),
        ),
        out_specs=(P("rows", "heads"),) * 5,
        check_vma=False,
    )
```

time: 44.6 us -> 34.6 us (0.78)
  waiting for transfers between devices: 12.9 us -> 3.28 us
  local copies, waits for them, and re-layouts: 4.33 us -> 0.67 us
  starting transfers between devices: 16.4 us -> 20 us
  Pallas kernels: 10.1 us -> 9.06 us
  other arithmetic: 0.02 us -> 0.69 us
    ppermute x11, waiting for transfers between devices: 12.9 us -> 3.28 us  [shift(): lax.ppermute(value, axis, [(s, t) for s, t in pairs if 0 <= t < count])]
    unnamed x18 -> x10, local copies, waits for them, and re-layouts: 4.32 us -> 0.67 us
    ppermute x11, starting transfers between devices: 16.4 us -> 20 us  [shift(): lax.ppermute(value, axis, [(s, t) for s, t in pairs if 0 <= t < count])]
    pallas_call x4 -> x8, Pallas kernels: 10.1 us -> 9.06 us  [call(): pl.pallas_call(kernel, out_shape=[jax.ShapeDtypeStruct(shape, dtype) for...]
    convert_element_type x1, other arithmetic: 0.01 us -> 0.69 us  [local(): relative = (bounds - first_row).astype(jnp.float32)]
  transfers between devices with their start and end apart: 11 -> 11, of which waited for: 4 -> 3; matrix products, arithmetic and copies ran while one was open for 0% -> 2% of each run, Pallas kernels for 10% -> 20%
where the time goes in v2:
time: 34.6 us; the launch traced here: 34.4 us
  starting transfers between devices  20 us (58%)
  Pallas kernels  9.06 us (26%)
  waiting for transfers between devices  3.28 us (9%)
  between operations  0.73 us (2%)
  other arithmetic  0.69 us (2%)
  local copies, waits for them, and re-layouts  0.67 us (2%)
    ppermute x11, starting transfers between devices, shift(): lax.ppermute(value, axis, [(s, t) for s, t in pairs if 0 <= t < count])  20 us
    pallas_call x8, Pallas kernels, call(): pl.pallas_call(kernel, out_shape=[jax.ShapeDtypeStruct(shape, dtype) for...  9.06 us
    ppermute x11, waiting for transfers between devices, shift(): lax.ppermute(value, axis, [(s, t) for s, t in pairs if 0 <= t < count])  3.28 us
  transfers between devices with their start and end apart: 11, of which 3 were waited for; matrix products, arithmetic and copies ran while one was open for 2% of the time, Pallas kernels for 20%

profile of v2, /device:TPU:0, one launch (start us, length us, event | category | flops | bytes accessed | tf_op | source)
XLA Modules:
  0.0 34.4 jit_solution(556555956059134948)
XLA Ops:
  0.6 3.0 %collective-permute-start = (bf16[512,128]{1,0:T(8,128)(2,1)}, bf16[512,128]{1,0:T(8,128)(2,1)S(1)}, u32[]{:S(2)}, u32[]{:S(2)}) collective-permute-start(bf16[512,128]{1,0:T(8,128)(2,1)} %k_ref.5), channel_id=1, source_target_pairs={{0,4},{4,8},{8,12},{12,16},{16,20},{20,24},{24,28},{28,0},{1,5},{5... | collective-permute-start | bytes 393224 | tf_op jit(solution)/shard_map/ppermute | solution.py:222
  3.7 1.6 %collective-permute-start.1 = (bf16[512,128]{1,0:T(8,128)(2,1)}, bf16[512,128]{1,0:T(8,128)(2,1)S(1)}, u32[]{:S(2)}, u32[]{:S(2)}) collective-permute-start(bf16[512,128]{1,0:T(8,128)(2,1)} %k_ref.5), channel_id=1, source_target_pairs={{0,8},{4,12},{8,16},{12,20},{16,24},{20,28},{24,0},{28,4},{1,9},{5... | collective-permute-start | bytes 393224 | tf_op jit(solution)/shard_map/ppermute | solution.py:222
  5.2 1.5 %collective-permute-start.2 = (bf16[512,128]{1,0:T(8,128)(2,1)}, bf16[512,128]{1,0:T(8,128)(2,1)S(1)}, u32[]{:S(2)}, u32[]{:S(2)}) collective-permute-start(bf16[512,128]{1,0:T(8,128)(2,1)} %v_ref.3), channel_id=1, source_target_pairs={{0,4},{4,8},{8,12},{12,16},{16,20},{20,24},{24,28},{28,0},{1,5},{5... | collective-permute-start | bytes 393224 | tf_op jit(solution)/shard_map/ppermute | solution.py:222
  6.7 1.6 %collective-permute-start.3 = (bf16[512,128]{1,0:T(8,128)(2,1)}, bf16[512,128]{1,0:T(8,128)(2,1)S(1)}, u32[]{:S(2)}, u32[]{:S(2)}) collective-permute-start(bf16[512,128]{1,0:T(8,128)(2,1)} %v_ref.3), channel_id=1, source_target_pairs={{0,8},{4,12},{8,16},{12,20},{16,24},{20,28},{24,0},{28,4},{1,9},{5... | collective-permute-start | bytes 393224 | tf_op jit(solution)/shard_map/ppermute | solution.py:222
  8.3 3.2 %collective-permute-start.7 = (bf16[512,128]{1,0:T(8,128)(2,1)}, bf16[512,128]{1,0:T(8,128)(2,1)S(1)}, u32[]{:S(2)}, u32[]{:S(2)}) collective-permute-start(bf16[512,128]{1,0:T(8,128)(2,1)} %q_ref.5), channel_id=1, source_target_pairs={{0,28},{4,0},{8,4},{12,8},{16,12},{20,16},{24,20},{28,24},{1,29},{... | collective-permute-start | bytes 393224 | tf_op jit(solution)/shard_map/ppermute | solution.py:222
  11.5 0.7 %subtract_convert_fusion.row_ref = f32[2,512]{1,0:T(2,128)S(1)} fusion(s32[2,512]{1,0:T(2,128)} %param.10, s32[]{:T(128)S(6)} %mul.3), kind=kLoop, calls=%fused_computation | loop fusion | flops 2048 | bytes 8196 | tf_op jit(solution)/shard_map/convert_element_type | solution.py:232
  12.2 0.0 copy-start.1
  12.2 0.0 copy-start.2
  12.2 0.0 copy-start.3
  12.2 0.0 copy-start.4
  12.2 0.0 copy-start
  12.3 0.2 shard_map.101
  12.5 0.0 collective-permute-done.refs_0_
  12.5 0.0 collective-permute-done.1.refs_1_
  12.5 0.6 %copy-done.1 = bf16[512,128]{1,0:T(8,128)(2,1)S(1)} copy-done((bf16[512,128]{1,0:T(8,128)(2,1)S(1)}, bf16[512,128]{1,0:T(8,128)(2,1)}, u32[]{:S(2)}) %copy-start.1) | copy-done | bytes 131096
  13.1 0.9 %shard_map.103 = (bf16[1,2,512,512]{3,2,1,0:T(8,128)(2,1)S(1)}, f32[1,2,512,512]{3,2,1,0:T(8,128)S(1)}) custom-call(f32[512,128]{1,0:T(8,128)S(1)} %get-tuple-element.34.start_ref, bf16[512,128]{1,0:T(8,128)(2,1)S(1)} %copy-done.1, bf16[512,128]{1,0:T(8,128)(2,1)S(1)} %collective-permute-done.refs_0_, bf16[512,128]{1,0:T(8,128)(2,1)S(1)} %collective-permute-done.1.refs_1_), custom_call_target="tpu_custom_call" | custom-call | tf_op jit(solution)/shard_map/pallas_call | solution.py:207
  14.0 0.8 %collective-permute-start.8 = (bf16[512,128]{1,0:T(8,128)(2,1)S(1)}, bf16[512,128]{1,0:T(8,128)(2,1)S(1)}, u32[]{:S(2)}, u32[]{:S(2)}) collective-permute-start(bf16[512,128]{1,0:T(8,128)(2,1)S(1)} %copy-done.1), channel_id=1, source_target_pairs={{0,24},{4,28},{8,0},{12,4},{16,8},{20,12},{24,16},{28,20},{1,25},{... | collective-permute-start | bytes 393224 | tf_op jit(solution)/shard_map/ppermute | solution.py:222
  14.8 0.0 copy-done.2
  14.8 0.0 copy-done.3
  14.8 0.0 copy-done.4
  14.8 1.0 %shard_map.102 = (bf16[1,512,512]{2,1,0:T(8,128)(2,1)S(1)}, f32[1,512,512]{2,1,0:T(8,128)S(1)}, bf16[1,512,512]{2,1,0:T(8,128)(2,1)S(1)}, f32[1,512,512]{2,1,0:T...) custom-call(f32[512,128]{1,0:T(8,128)S(1)} %get-tuple-element.34.start_ref, ...), custom_call_target="tpu_custom_call" | custom-call | tf_op jit(solution)/shard_map/pallas_call | solution.py:207
  15.8 1.3 %collective-permute-done.2.refs_1_.refs_2_ = bf16[512,128]{1,0:T(8,128)(2,1)S(1)} collective-permute-done((bf16[512,128]{1,0:T(8,128)(2,1)}, bf16[512,128]{1,0:T(8,128)(2,1)S(1)}, u32[]{:S(2)}, u32[]{:S(2)}) %collective-permute-start.2) | collective-permute-done | bytes 131104 | tf_op jit(solution)/shard_map/ppermute | solution.py:222
  17.0 0.0 collective-permute-done.3.refs_2_.refs_3_
  17.0 0.0 copy-done
  17.0 1.3 %shard_map.104 = (f32[512,128]{1,0:T(8,128)S(1)}, f32[4,512]{1,0:T(4,128)S(1)}) custom-call(bf16[1,512,512]{2,1,0:T(8,128)(2,1)S(1)} %get-tuple-element.36.own_weight_ref, f32[512,128]{1,0:T(8,128)S(1)} %get-tuple-element.37.scaled_ref, f32[1,512]{1,0:T(1,128)S(1)} %get-tuple-element.38.sum_ref, bf16[1,2,512,512]{3,2,1,0:T(8,128)(2,1)S(1)} %get-tuple-element.39.weight_ref, ...), custom_call_target="tpu_custom_call" | custom-call | tf_op jit(solution)/shard_map/pallas_call | solution.py:207
  18.3 0.0 collective-permute-start.4
  18.3 1.7 %collective-permute-start.5 = (f32[4,512]{1,0:T(4,128)S(1)}, f32[4,512]{1,0:T(4,128)S(1)}, u32[]{:S(2)}, u32[]{:S(2)}) collective-permute-start(f32[4,512]{1,0:T(4,128)S(1)} %get-tuple-element.44.refs_0_), channel_id=1, source_target_pairs={{0,2},{1,3},{2,0},{3,1},{4,6},{5,7},{6,4},{7,5},{8,10},{9,11},{10,... | collective-permute-start | bytes 24584 | tf_op jit(solution)/shard_map/ppermute | solution.py:222
  20.0 1.4 %collective-permute-start.6 = (f32[4,512]{1,0:T(4,128)S(1)}, f32[4,512]{1,0:T(4,128)S(1)}, u32[]{:S(2)}, u32[]{:S(2)}) collective-permute-start(f32[4,512]{1,0:T(4,128)S(1)} %get-tuple-element.44.refs_0_), channel_id=1, source_target_pairs={{0,3},{1,0},{2,1},{3,2},{4,7},{5,4},{6,5},{7,6},{8,11},{9,8},{10,9... | collective-permute-start | bytes 24584 | tf_op jit(solution)/shard_map/ppermute | solution.py:222
  21.5 0.0 collective-permute-done.7.refs_0_
  21.5 0.0 collective-permute-done.8.refs_1_
  21.5 0.9 %shard_map.105 = (bf16[1,2,512,512]{3,2,1,0:T(8,128)(2,1)S(1)}, f32[1,2,512,512]{3,2,1,0:T(8,128)S(1)}) custom-call(f32[512,128]{1,0:T(8,128)S(1)} %get-tuple-element.35.last_ref, bf16[512,128]{1,0:T(8,128)(2,1)S(1)} %copy-done.2, bf16[512,128]{1,0:T(8,128)(2,1)S(1)} %collective-permute-done.7.refs_0_, bf16[512,128]{1,0:T(8,128)(2,1)S(1)} %collective-permute-done.8.refs_1_), custom_call_target="tpu_custom_call" | custom-call | tf_op jit(solution)/shard_map/pallas_call | solution.py:207
  22.4 0.0 collective-permute-done.4.refs_1_
  22.4 0.0 collective-permute-done.5.refs_2_
  22.4 0.4 %collective-permute-done.6.refs_3_ = f32[4,512]{1,0:T(4,128)S(1)} collective-permute-done((f32[4,512]{1,0:T(4,128)S(1)}, f32[4,512]{1,0:T(4,128)S(1)}, u32[]{:S(2)}, u32[]{:S(2)}) %collective-permute-start.6) | collective-permute-done | bytes 8224 | tf_op jit(solution)/shard_map/ppermute | solution.py:222
  22.8 0.3 %shard_map.106 = (f32[512,128]{1,0:T(8,128)S(1)}, bf16[512,128]{1,0:T(8,128)(2,1)S(1)}) custom-call(f32[512,128]{1,0:T(8,128)S(1)} %get-tuple-element.40.att_ref, f32[512,128]{1,0:T(8,128)S(1)} %get-tuple-element.37.scaled_ref, f32[4,512]{1,0:T(4,128)S(1)} %get-tuple-element.44.refs_0_, f32[4,512]{1,0:T(4,128)S(1)} %collective-permute-done.4.refs_1_, ...), custom_call_target="tpu_custom_call" | custom-call | tf_op jit(solution)/shard_map/pallas_call | solution.py:207
  23.2 1.7 %collective-permute-start.10 = (bf16[512,128]{1,0:T(8,128)(2,1)S(1)}, bf16[512,128]{1,0:T(8,128)(2,1)S(1)}, u32[]{:S(2)}, u32[]{:S(2)}) collective-permute-start(bf16[512,128]{1,0:T(8,128)(2,1)S(1)} %get-tuple-element.48.d_ref), channel_id=1, source_target_pairs={{0,24},{4,28},{8,0},{12,4},{16,8},{20,12},{24,16},{28,20},{1,25},{... | collective-permute-start | bytes 393224 | tf_op jit(solution)/shard_map/ppermute | solution.py:222
  24.9 3.5 %collective-permute-start.9 = (bf16[512,128]{1,0:T(8,128)(2,1)S(1)}, bf16[512,128]{1,0:T(8,128)(2,1)S(1)}, u32[]{:S(2)}, u32[]{:S(2)}) collective-permute-start(bf16[512,128]{1,0:T(8,128)(2,1)S(1)} %get-tuple-element.48.d_ref), channel_id=1, source_target_pairs={{0,28},{4,0},{8,4},{12,8},{16,12},{20,16},{24,20},{28,24},{1,29},{... | collective-permute-start | bytes 393224 | tf_op jit(solution)/shard_map/ppermute | solution.py:222
  28.4 2.5 %shard_map.107 = (bf16[512,128]{1,0:T(8,128)(2,1)}, f32[512,128]{1,0:T(8,128)S(1)}, f32[512,128]{1,0:T(8,128)S(1)}, bf16[512,128]{1,0:T(8,128)(2,1)}, bf16[512,128]{1,0:T(8,128)(2,1)}) custom-call(bf16[512,128]{1,0:T(8,128)(2,1)S(1)} %copy-done.1, bf16[512,128]{1,0:T(8,128)(2,1)S(1)} %copy-done.2, bf16[512,128]{1,0:T(8,128)(2,1)S(1)} %copy-done, ...), custom_call_target="tpu_custom_call" | custom-call | tf_op jit(solution)/shard_map/pallas_call | solution.py:207
  30.9 0.0 collective-permute-done.10.refs_3_
  30.9 1.6 %collective-permute-done.9.refs_2_ = bf16[512,128]{1,0:T(8,128)(2,1)S(1)} collective-permute-done((bf16[512,128]{1,0:T(8,128)(2,1)S(1)}, bf16[512,128]{1,0:T(8,128)(2,1)S(1)}, u32[]{:S(2)}, u32[]{:S(2)}) %collective-permute-start.9) | collective-permute-done | bytes 131104 | tf_op jit(solution)/shard_map/ppermute | solution.py:222
  32.5 1.9 %shard_map.108 = (bf16[512,128]{1,0:T(8,128)(2,1)}, bf16[512,128]{1,0:T(8,128)(2,1)}) custom-call(bf16[512,128]{1,0:T(8,128)(2,1)S(1)} %copy-done, f32[512,128]{1,0:T(8,128)S(1)} %get-tuple-element.56.near_k_ref, f32[512,128]{1,0:T(8,128)S(1)} %get-tuple-element.57.near_v_ref, bf16[1,2,512,512]{3,2,1,0:T(8,128)(2,1)S(1)} %get-tuple-element.58.weight_ref, ...), custom_call_target="tpu_custom_call" | custom-call | tf_op jit(solution)/shard_map/pallas_call | solution.py:207
Async XLA Ops:
  0.6 11.8 %collective-permute-start = (bf16[512,128]{1,0:T(8,128)(2,1)}, bf16[512,128]{1,0:T(8,128)(2,1)S(1)}, u32[]{:S(2)}, u32[]{:S(2)}) collective-permute-start(bf16[512,128]{1,0:T(8,128)(2,1)} %k_ref.5), channel_id=1, source_target_pairs={{0,4},{4,8},{8,12},{12,16},{16,20},{20,24},{24,28},{28,0},{1,5},{5... | collective-permute-start | bytes 393224 | tf_op jit(solution)/shard_map/ppermute | solution.py:222
  3.7 8.8 %collective-permute-start.1 = (bf16[512,128]{1,0:T(8,128)(2,1)}, bf16[512,128]{1,0:T(8,128)(2,1)S(1)}, u32[]{:S(2)}, u32[]{:S(2)}) collective-permute-start(bf16[512,128]{1,0:T(8,128)(2,1)} %k_ref.5), channel_id=1, source_target_pairs={{0,8},{4,12},{8,16},{12,20},{16,24},{20,28},{24,0},{28,4},{1,9},{5... | collective-permute-start | bytes 393224 | tf_op jit(solution)/shard_map/ppermute | solution.py:222
  5.2 11.8 %collective-permute-start.2 = (bf16[512,128]{1,0:T(8,128)(2,1)}, bf16[512,128]{1,0:T(8,128)(2,1)S(1)}, u32[]{:S(2)}, u32[]{:S(2)}) collective-permute-start(bf16[512,128]{1,0:T(8,128)(2,1)} %v_ref.3), channel_id=1, source_target_pairs={{0,4},{4,8},{8,12},{12,16},{16,20},{20,24},{24,28},{28,0},{1,5},{5... | collective-permute-start | bytes 393224 | tf_op jit(solution)/shard_map/ppermute | solution.py:222
  6.7 10.3 %collective-permute-start.3 = (bf16[512,128]{1,0:T(8,128)(2,1)}, bf16[512,128]{1,0:T(8,128)(2,1)S(1)}, u32[]{:S(2)}, u32[]{:S(2)}) collective-permute-start(bf16[512,128]{1,0:T(8,128)(2,1)} %v_ref.3), channel_id=1, source_target_pairs={{0,8},{4,12},{8,16},{12,20},{16,24},{20,28},{24,0},{28,4},{1,9},{5... | collective-permute-start | bytes 393224 | tf_op jit(solution)/shard_map/ppermute | solution.py:222
  8.3 13.2 %collective-permute-start.7 = (bf16[512,128]{1,0:T(8,128)(2,1)}, bf16[512,128]{1,0:T(8,128)(2,1)S(1)}, u32[]{:S(2)}, u32[]{:S(2)}) collective-permute-start(bf16[512,128]{1,0:T(8,128)(2,1)} %q_ref.5), channel_id=1, source_target_pairs={{0,28},{4,0},{8,4},{12,8},{16,12},{20,16},{24,20},{28,24},{1,29},{... | collective-permute-start | bytes 393224 | tf_op jit(solution)/shard_map/ppermute | solution.py:222
  12.2 0.9 %copy-start.1 = (bf16[512,128]{1,0:T(8,128)(2,1)S(1)}, bf16[512,128]{1,0:T(8,128)(2,1)}, u32[]{:S(2)}) copy-start(bf16[512,128]{1,0:T(8,128)(2,1)} %q_ref.5) | copy-start | bytes 393220
  12.2 2.6 %copy-start.2 = (bf16[512,128]{1,0:T(8,128)(2,1)S(1)}, bf16[512,128]{1,0:T(8,128)(2,1)}, u32[]{:S(2)}) copy-start(bf16[512,128]{1,0:T(8,128)(2,1)} %k_ref.5) | copy-start | bytes 393220
  12.2 2.6 %copy-start.3 = (bf16[512,128]{1,0:T(8,128)(2,1)S(1)}, bf16[512,128]{1,0:T(8,128)(2,1)}, u32[]{:S(2)}) copy-start(bf16[512,128]{1,0:T(8,128)(2,1)} %gate_ref.3) | copy-start | bytes 393220
  12.2 2.6 %copy-start.4 = (bf16[512,128]{1,0:T(8,128)(2,1)S(1)}, bf16[512,128]{1,0:T(8,128)(2,1)}, u32[]{:S(2)}) copy-start(bf16[512,128]{1,0:T(8,128)(2,1)} %up_ref.3) | copy-start | bytes 393220
  12.2 4.8 %copy-start = (bf16[512,128]{1,0:T(8,128)(2,1)S(1)}, bf16[512,128]{1,0:T(8,128)(2,1)}, u32[]{:S(2)}) copy-start(bf16[512,128]{1,0:T(8,128)(2,1)} %v_ref.3) | copy-start | bytes 393220
  14.0 7.5 %collective-permute-start.8 = (bf16[512,128]{1,0:T(8,128)(2,1)S(1)}, bf16[512,128]{1,0:T(8,128)(2,1)S(1)}, u32[]{:S(2)}, u32[]{:S(2)}) collective-permute-start(bf16[512,128]{1,0:T(8,128)(2,1)S(1)} %copy-done.1), channel_id=1, source_target_pairs={{0,24},{4,28},{8,0},{12,4},{16,8},{20,12},{24,16},{28,20},{1,25},{... | collective-permute-start | bytes 393224 | tf_op jit(solution)/shard_map/ppermute | solution.py:222
  18.3 4.1 %collective-permute-start.4 = (f32[4,512]{1,0:T(4,128)S(1)}, f32[4,512]{1,0:T(4,128)S(1)}, u32[]{:S(2)}, u32[]{:S(2)}) collective-permute-start(f32[4,512]{1,0:T(4,128)S(1)} %get-tuple-element.44.refs_0_), channel_id=1, source_target_pairs={{0,1},{1,2},{2,3},{3,0},{4,5},{5,6},{6,7},{7,4},{8,9},{9,10},{10,1... | collective-permute-start | bytes 24584 | tf_op jit(solution)/shard_map/ppermute | solution.py:222
  18.3 4.1 %collective-permute-start.5 = (f32[4,512]{1,0:T(4,128)S(1)}, f32[4,512]{1,0:T(4,128)S(1)}, u32[]{:S(2)}, u32[]{:S(2)}) collective-permute-start(f32[4,512]{1,0:T(4,128)S(1)} %get-tuple-element.44.refs_0_), channel_id=1, source_target_pairs={{0,2},{1,3},{2,0},{3,1},{4,6},{5,7},{6,4},{7,5},{8,10},{9,11},{10,... | collective-permute-start | bytes 24584 | tf_op jit(solution)/shard_map/ppermute | solution.py:222
  20.0 2.8 %collective-permute-start.6 = (f32[4,512]{1,0:T(4,128)S(1)}, f32[4,512]{1,0:T(4,128)S(1)}, u32[]{:S(2)}, u32[]{:S(2)}) collective-permute-start(f32[4,512]{1,0:T(4,128)S(1)} %get-tuple-element.44.refs_0_), channel_id=1, source_target_pairs={{0,3},{1,0},{2,1},{3,2},{4,7},{5,4},{6,5},{7,6},{8,11},{9,8},{10,9... | collective-permute-start | bytes 24584 | tf_op jit(solution)/shard_map/ppermute | solution.py:222
  23.2 7.7 %collective-permute-start.10 = (bf16[512,128]{1,0:T(8,128)(2,1)S(1)}, bf16[512,128]{1,0:T(8,128)(2,1)S(1)}, u32[]{:S(2)}, u32[]{:S(2)}) collective-permute-start(bf16[512,128]{1,0:T(8,128)(2,1)S(1)} %get-tuple-element.48.d_ref), channel_id=1, source_target_pairs={{0,24},{4,28},{8,0},{12,4},{16,8},{20,12},{24,16},{28,20},{1,25},{... | collective-permute-start | bytes 393224 | tf_op jit(solution)/shard_map/ppermute | solution.py:222
  24.9 7.6 %collective-permute-start.9 = (bf16[512,128]{1,0:T(8,128)(2,1)S(1)}, bf16[512,128]{1,0:T(8,128)(2,1)S(1)}, u32[]{:S(2)}, u32[]{:S(2)}) collective-permute-start(bf16[512,128]{1,0:T(8,128)(2,1)S(1)} %get-tuple-element.48.d_ref), channel_id=1, source_target_pairs={{0,28},{4,0},{8,4},{12,8},{16,12},{20,16},{24,20},{28,24},{1,29},{... | collective-permute-start | bytes 393224 | tf_op jit(solution)/shard_map/ppermute | solution.py:222

commit v3 on v2

--- a/solution.py
+++ b/solution.py
@@ -26,10 +26,7 @@
 
 
 def lane_sums(values):
-    ones = jnp.ones((8, values.shape[1]), jnp.float32)
-    return lax.dot_general(
-        ones, values, NT, precision=lax.Precision.HIGHEST, preferred_element_type=jnp.float32
-    )[:1]
+    return jnp.sum(jnp.transpose(values), axis=0, keepdims=True)
 
 
 def chunk_of(rows):
@@ -135,15 +132,17 @@
     lanes, chunks = parts_of(rows, features)
     for head, at in lanes:
         for chunk, here in chunks:
-            total = dot(own_weight_ref[head, here, :], values[0][:, at], NN)
+            total = dot(own_weight_ref[head, here, : here.stop], values[0][: here.stop, at], NN)
             for offset in range(REACH):
-                total += dot(weight_ref[head, offset, here, :], values[offset + 1][:, at], NN)
+                low = here.start if offset == REACH - 1 else 0
+                total += dot(weight_ref[head, offset, here, low:], values[offset + 1][low:, at], NN)
             att_ref[here, at] = total
-    att = att_ref[...]
-    stats_ref[0:1, :] = lane_sums(att)
-    stats_ref[1:2, :] = lane_sums(att * att)
+    att = jnp.transpose(att_ref[...])
+    scaled = jnp.transpose(scaled_ref[...])
+    stats_ref[0:1, :] = jnp.sum(att, axis=0, keepdims=True)
+    stats_ref[1:2, :] = jnp.sum(att * att, axis=0, keepdims=True)
     stats_ref[2:3, :] = sum_ref[...]
-    stats_ref[3:4, :] = lane_sums(scaled_ref[...] * att)
+    stats_ref[3:4, :] = jnp.sum(scaled * att, axis=0, keepdims=True)
 
 
 def delta_kernel(total_features, att_ref, scaled_ref, *refs):
@@ -191,15 +190,14 @@
     lanes, chunks = parts_of(rows, features)
     for head, at in lanes:
         for chunk, here in chunks:
-            key_total = near_k_ref[here, at]
-            value_total = near_v_ref[here, at]
-            for offset in range(REACH):
-                delta = deltas[offset][:, at]
-                value_total += dot(weight_ref[head, offset, here, :], delta, NN)
-                grad = dot(v_ref[here, at], delta, NT) * slope_ref[head, offset, here, :]
-                key_total += dot(grad.astype(jnp.bfloat16), queries[offset][:, at], NN)
-            gv_ref[here, at] = value_total.astype(jnp.bfloat16)
-            gk_ref[here, at] = (key_total * factor).astype(jnp.bfloat16)
+            ends = [here.stop if offset == REACH - 1 else rows for offset in range(REACH)]
+            delta = jnp.concatenate([ref[:end, at] for ref, end in zip(deltas, ends)], axis=0)
+            query = jnp.concatenate([ref[:end, at] for ref, end in zip(queries, ends)], axis=0)
+            slope = jnp.concatenate([slope_ref[head, offset, here, :end] for offset, end in enumerate(ends)], axis=1)
+            weight = jnp.concatenate([weight_ref[head, offset, here, :end] for offset, end in enumerate(ends)], axis=1)
+            grad = (dot(v_ref[here, at], delta, NT) * slope).astype(jnp.bfloat16)
+            gv_ref[here, at] = (near_v_ref[here, at] + dot(weight, delta, NN)).astype(jnp.bfloat16)
+            gk_ref[here, at] = ((near_k_ref[here, at] + dot(grad, query, NN)) * factor).astype(jnp.bfloat16)
 
 
 def call(kernel, outs, *args, cost=None):
@@ -220,6 +218,13 @@
     if ring:
         pairs = [(source, target % count) for source, target in pairs]
     return lax.ppermute(value, axis, [(s, t) for s, t in pairs if 0 <= t < count])
+
+
+def meet(value, axis, step):
+    count = lax.axis_size(axis)
+    if count & (count - 1):
+        return shift(value, axis, step)
+    return lax.ppermute(value, axis, [(source, source ^ step) for source in range(count)])
 
 
 def local(queries, key_vectors, value_vectors, gating, bounds, cotangent):
@@ -260,7 +265,7 @@
     weights_t, slopes_t = call(
         functools.partial(later_kernel, factor), [(pair, half), (pair, full)], lasts, key_vectors, *later
     )
-    all_stats = [stats] + [shift(stats, "heads", step) for step in range(1, heads)]
+    all_stats = [stats] + [meet(stats, "heads", step) for step in reversed(range(1, heads))]
     all_stats, weights_t = lax.optimization_barrier((all_stats, weights_t))
     normed, delta = call(
         functools.partial(delta_kernel, float(block[1] * heads)),

time: 34.6 us -> 32.8 us (0.948)
  Pallas kernels: 9.06 us -> 7.76 us
  starting transfers between devices: 20 us -> 19 us
  waiting for transfers between devices: 3.28 us -> 3.8 us
    ppermute x11 -> x8, starting transfers between devices: 20 us -> 17 us  [shift(): lax.ppermute(value, axis, [(s, t) for s, t in pairs if 0 <= t < count])]
    ppermute x0 -> x3, starting transfers between devices: none -> 1.92 us  [meet(): lax.ppermute(value, axis, [(source, source ^ step) for source in range(co...]
    pallas_call x8, Pallas kernels: 9.06 us -> 7.76 us  [call(): pl.pallas_call(kernel, out_shape=[jax.ShapeDtypeStruct(shape, dtype) for...]
    ppermute x0 -> x3, waiting for transfers between devices: none -> 0.96 us  [meet(): lax.ppermute(value, axis, [(source, source ^ step) for source in range(co...]
    ppermute x11 -> x8, waiting for transfers between devices: 3.28 us -> 2.84 us  [shift(): lax.ppermute(value, axis, [(s, t) for s, t in pairs if 0 <= t < count])]
  transfers between devices with their start and end apart: 11 -> 11, of which waited for: 3 -> 4; matrix products, arithmetic and copies ran while one was open for 2% -> 2% of each run, Pallas kernels for 20% -> 18%
where the time goes in v3:
time: 32.8 us; the launch traced here: 32.6 us
  starting transfers between devices  19 us (58%)
  Pallas kernels  7.76 us (24%)
  waiting for transfers between devices  3.8 us (12%)
  between operations  0.73 us (2%)
  other arithmetic  0.69 us (2%)
  local copies, waits for them, and re-layouts  0.67 us (2%)
    ppermute x8, starting transfers between devices, shift(): lax.ppermute(value, axis, [(s, t) for s, t in pairs if 0 <= t < count])  17 us
    pallas_call x8, Pallas kernels, call(): pl.pallas_call(kernel, out_shape=[jax.ShapeDtypeStruct(shape, dtype) for...  7.76 us
    ppermute x8, waiting for transfers between devices, shift(): lax.ppermute(value, axis, [(s, t) for s, t in pairs if 0 <= t < count])  2.84 us
    ppermute x3, starting transfers between devices, meet(): lax.ppermute(value, axis, [(source, source ^ step) for source in range(co...  1.92 us
    ppermute x3, waiting for transfers between devices, meet(): lax.ppermute(value, axis, [(source, source ^ step) for source in range(co...  0.96 us
    convert_element_type x1, other arithmetic, local(): relative = (bounds - first_row).astype(jnp.float32)  0.69 us
    unnamed x10, local copies, waits for them, and re-layouts  0.67 us
  transfers between devices with their start and end apart: 11, of which 4 were waited for; matrix products, arithmetic and copies ran while one was open for 2% of the time, Pallas kernels for 18%

profile of v3, /device:TPU:0, one launch (start us, length us, event | category | flops | bytes accessed | tf_op | source)
XLA Modules:
  0.0 32.6 jit_solution(6773611781941127508)
XLA Ops:
  0.6 3.0 %collective-permute-start = (bf16[512,128]{1,0:T(8,128)(2,1)}, bf16[512,128]{1,0:T(8,128)(2,1)S(1)}, u32[]{:S(2)}, u32[]{:S(2)}) collective-permute-start(bf16[512,128]{1,0:T(8,128)(2,1)} %k_ref.5), channel_id=1, source_target_pairs={{0,4},{4,8},{8,12},{12,16},{16,20},{20,24},{24,28},{28,0},{1,5},{5... | collective-permute-start | bytes 393224 | tf_op jit(solution)/shard_map/ppermute | solution.py:220
  3.7 1.6 %collective-permute-start.1 = (bf16[512,128]{1,0:T(8,128)(2,1)}, bf16[512,128]{1,0:T(8,128)(2,1)S(1)}, u32[]{:S(2)}, u32[]{:S(2)}) collective-permute-start(bf16[512,128]{1,0:T(8,128)(2,1)} %k_ref.5), channel_id=1, source_target_pairs={{0,8},{4,12},{8,16},{12,20},{16,24},{20,28},{24,0},{28,4},{1,9},{5... | collective-permute-start | bytes 393224 | tf_op jit(solution)/shard_map/ppermute | solution.py:220
  5.2 1.5 %collective-permute-start.2 = (bf16[512,128]{1,0:T(8,128)(2,1)}, bf16[512,128]{1,0:T(8,128)(2,1)S(1)}, u32[]{:S(2)}, u32[]{:S(2)}) collective-permute-start(bf16[512,128]{1,0:T(8,128)(2,1)} %v_ref.3), channel_id=1, source_target_pairs={{0,4},{4,8},{8,12},{12,16},{16,20},{20,24},{24,28},{28,0},{1,5},{5... | collective-permute-start | bytes 393224 | tf_op jit(solution)/shard_map/ppermute | solution.py:220
  6.7 1.6 %collective-permute-start.3 = (bf16[512,128]{1,0:T(8,128)(2,1)}, bf16[512,128]{1,0:T(8,128)(2,1)S(1)}, u32[]{:S(2)}, u32[]{:S(2)}) collective-permute-start(bf16[512,128]{1,0:T(8,128)(2,1)} %v_ref.3), channel_id=1, source_target_pairs={{0,8},{4,12},{8,16},{12,20},{16,24},{20,28},{24,0},{28,4},{1,9},{5... | collective-permute-start | bytes 393224 | tf_op jit(solution)/shard_map/ppermute | solution.py:220
  8.3 3.2 %collective-permute-start.7 = (bf16[512,128]{1,0:T(8,128)(2,1)}, bf16[512,128]{1,0:T(8,128)(2,1)S(1)}, u32[]{:S(2)}, u32[]{:S(2)}) collective-permute-start(bf16[512,128]{1,0:T(8,128)(2,1)} %q_ref.5), channel_id=1, source_target_pairs={{0,28},{4,0},{8,4},{12,8},{16,12},{20,16},{24,20},{28,24},{1,29},{... | collective-permute-start | bytes 393224 | tf_op jit(solution)/shard_map/ppermute | solution.py:220
  11.5 0.7 %subtract_convert_fusion.row_ref = f32[2,512]{1,0:T(2,128)S(1)} fusion(s32[2,512]{1,0:T(2,128)} %param.10, s32[]{:T(128)S(6)} %mul.3), kind=kLoop, calls=%fused_computation | loop fusion | flops 2048 | bytes 8196 | tf_op jit(solution)/shard_map/convert_element_type | solution.py:237
  12.2 0.0 copy-start.1
  12.2 0.0 copy-start.2
  12.2 0.0 copy-start.3
  12.2 0.0 copy-start.4
  12.2 0.0 copy-start
  12.3 0.2 shard_map.101
  12.5 0.0 collective-permute-done.refs_0_
  12.5 0.0 collective-permute-done.1.refs_1_
  12.5 0.6 %copy-done.1 = bf16[512,128]{1,0:T(8,128)(2,1)S(1)} copy-done((bf16[512,128]{1,0:T(8,128)(2,1)S(1)}, bf16[512,128]{1,0:T(8,128)(2,1)}, u32[]{:S(2)}) %copy-start.1) | copy-done | bytes 131096
  13.1 0.9 %shard_map.103 = (bf16[1,2,512,512]{3,2,1,0:T(8,128)(2,1)S(1)}, f32[1,2,512,512]{3,2,1,0:T(8,128)S(1)}) custom-call(f32[512,128]{1,0:T(8,128)S(1)} %get-tuple-element.34.start_ref, bf16[512,128]{1,0:T(8,128)(2,1)S(1)} %copy-done.1, bf16[512,128]{1,0:T(8,128)(2,1)S(1)} %collective-permute-done.refs_0_, bf16[512,128]{1,0:T(8,128)(2,1)S(1)} %collective-permute-done.1.refs_1_), custom_call_target="tpu_custom_call" | custom-call | tf_op jit(solution)/shard_map/pallas_call | solution.py:205
  14.0 0.8 %collective-permute-start.8 = (bf16[512,128]{1,0:T(8,128)(2,1)S(1)}, bf16[512,128]{1,0:T(8,128)(2,1)S(1)}, u32[]{:S(2)}, u32[]{:S(2)}) collective-permute-start(bf16[512,128]{1,0:T(8,128)(2,1)S(1)} %copy-done.1), channel_id=1, source_target_pairs={{0,24},{4,28},{8,0},{12,4},{16,8},{20,12},{24,16},{28,20},{1,25},{... | collective-permute-start | bytes 393224 | tf_op jit(solution)/shard_map/ppermute | solution.py:220
  14.8 0.0 copy-done.2
  14.8 0.0 copy-done.3
  14.8 0.0 copy-done.4
  14.8 0.7 %shard_map.102 = (bf16[1,512,512]{2,1,0:T(8,128)(2,1)S(1)}, f32[1,512,512]{2,1,0:T(8,128)S(1)}, bf16[1,512,512]{2,1,0:T(8,128)(2,1)S(1)}, f32[1,512,512]{2,1,0:T...) custom-call(f32[512,128]{1,0:T(8,128)S(1)} %get-tuple-element.34.start_ref, ...), custom_call_target="tpu_custom_call" | custom-call | tf_op jit(solution)/shard_map/pallas_call | solution.py:205
  15.5 1.5 %collective-permute-done.2.refs_1_.refs_2_ = bf16[512,128]{1,0:T(8,128)(2,1)S(1)} collective-permute-done((bf16[512,128]{1,0:T(8,128)(2,1)}, bf16[512,128]{1,0:T(8,128)(2,1)S(1)}, u32[]{:S(2)}, u32[]{:S(2)}) %collective-permute-start.2) | collective-permute-done | bytes 131104 | tf_op jit(solution)/shard_map/ppermute | solution.py:220
  17.0 0.0 collective-permute-done.3.refs_2_.refs_3_
  17.0 0.0 copy-done
  17.0 0.6 %shard_map.104 = (f32[512,128]{1,0:T(8,128)S(1)}, f32[4,512]{1,0:T(4,128)S(1)}) custom-call(bf16[1,512,512]{2,1,0:T(8,128)(2,1)S(1)} %get-tuple-element.36.own_weight_ref, f32[512,128]{1,0:T(8,128)S(1)} %get-tuple-element.37.scaled_ref, f32[1,512]{1,0:T(1,128)S(1)} %get-tuple-element.38.sum_ref, bf16[1,2,512,512]{3,2,1,0:T(8,128)(2,1)S(1)} %get-tuple-element.39.weight_ref, ...), custom_call_target="tpu_custom_call" | custom-call | tf_op jit(solution)/shard_map/pallas_call | solution.py:205
  17.7 0.1 collective-permute-start.4
  17.7 1.8 %collective-permute-start.5 = (f32[4,512]{1,0:T(4,128)S(1)}, f32[4,512]{1,0:T(4,128)S(1)}, u32[]{:S(2)}, u32[]{:S(2)}) collective-permute-start(f32[4,512]{1,0:T(4,128)S(1)} %get-tuple-element.44.refs_0_), channel_id=1, source_target_pairs={{0,2},{1,3},{2,0},{3,1},{4,6},{5,7},{6,4},{7,5},{8,10},{9,11},{10,... | collective-permute-start | bytes 24584 | tf_op jit(solution)/shard_map/ppermute | solution.py:227
  19.5 0.1 collective-permute-start.6
  19.6 0.0 collective-permute-done.7.refs_0_
  19.6 0.0 collective-permute-done.8.refs_1_
  19.6 0.9 %shard_map.105 = (bf16[1,2,512,512]{3,2,1,0:T(8,128)(2,1)S(1)}, f32[1,2,512,512]{3,2,1,0:T(8,128)S(1)}) custom-call(f32[512,128]{1,0:T(8,128)S(1)} %get-tuple-element.35.last_ref, bf16[512,128]{1,0:T(8,128)(2,1)S(1)} %copy-done.2, bf16[512,128]{1,0:T(8,128)(2,1)S(1)} %collective-permute-done.7.refs_0_, bf16[512,128]{1,0:T(8,128)(2,1)S(1)} %collective-permute-done.8.refs_1_), custom_call_target="tpu_custom_call" | custom-call | tf_op jit(solution)/shard_map/pallas_call | solution.py:205
  20.5 0.3 collective-permute-done.4.refs_1_
  20.8 0.7 %collective-permute-done.5.refs_2_ = f32[4,512]{1,0:T(4,128)S(1)} collective-permute-done((f32[4,512]{1,0:T(4,128)S(1)}, f32[4,512]{1,0:T(4,128)S(1)}, u32[]{:S(2)}, u32[]{:S(2)}) %collective-permute-start.5) | collective-permute-done | bytes 8224 | tf_op jit(solution)/shard_map/ppermute | solution.py:227
  21.5 0.0 collective-permute-done.6.refs_3_
  21.5 0.3 %shard_map.106 = (f32[512,128]{1,0:T(8,128)S(1)}, bf16[512,128]{1,0:T(8,128)(2,1)S(1)}) custom-call(f32[512,128]{1,0:T(8,128)S(1)} %get-tuple-element.40.att_ref, f32[512,128]{1,0:T(8,128)S(1)} %get-tuple-element.37.scaled_ref, f32[4,512]{1,0:T(4,128)S(1)} %get-tuple-element.44.refs_0_, f32[4,512]{1,0:T(4,128)S(1)} %collective-permute-done.4.refs_1_, ...), custom_call_target="tpu_custom_call" | custom-call | tf_op jit(solution)/shard_map/pallas_call | solution.py:205
  21.8 1.9 %collective-permute-start.10 = (bf16[512,128]{1,0:T(8,128)(2,1)S(1)}, bf16[512,128]{1,0:T(8,128)(2,1)S(1)}, u32[]{:S(2)}, u32[]{:S(2)}) collective-permute-start(bf16[512,128]{1,0:T(8,128)(2,1)S(1)} %get-tuple-element.48.d_ref), channel_id=1, source_target_pairs={{0,24},{4,28},{8,0},{12,4},{16,8},{20,12},{24,16},{28,20},{1,25},{... | collective-permute-start | bytes 393224 | tf_op jit(solution)/shard_map/ppermute | solution.py:220
  23.7 3.5 %collective-permute-start.9 = (bf16[512,128]{1,0:T(8,128)(2,1)S(1)}, bf16[512,128]{1,0:T(8,128)(2,1)S(1)}, u32[]{:S(2)}, u32[]{:S(2)}) collective-permute-start(bf16[512,128]{1,0:T(8,128)(2,1)S(1)} %get-tuple-element.48.d_ref), channel_id=1, source_target_pairs={{0,28},{4,0},{8,4},{12,8},{16,12},{20,16},{24,20},{28,24},{1,29},{... | collective-permute-start | bytes 393224 | tf_op jit(solution)/shard_map/ppermute | solution.py:220
  27.2 2.5 %shard_map.107 = (bf16[512,128]{1,0:T(8,128)(2,1)}, f32[512,128]{1,0:T(8,128)S(1)}, f32[512,128]{1,0:T(8,128)S(1)}, bf16[512,128]{1,0:T(8,128)(2,1)}, bf16[512,128]{1,0:T(8,128)(2,1)}) custom-call(bf16[512,128]{1,0:T(8,128)(2,1)S(1)} %copy-done.1, bf16[512,128]{1,0:T(8,128)(2,1)S(1)} %copy-done.2, bf16[512,128]{1,0:T(8,128)(2,1)S(1)} %copy-done, ...), custom_call_target="tpu_custom_call" | custom-call | tf_op jit(solution)/shard_map/pallas_call | solution.py:205
  29.7 0.0 collective-permute-done.10.refs_3_
  29.7 1.3 %collective-permute-done.9.refs_2_ = bf16[512,128]{1,0:T(8,128)(2,1)S(1)} collective-permute-done((bf16[512,128]{1,0:T(8,128)(2,1)S(1)}, bf16[512,128]{1,0:T(8,128)(2,1)S(1)}, u32[]{:S(2)}, u32[]{:S(2)}) %collective-permute-start.9) | collective-permute-done | bytes 131104 | tf_op jit(solution)/shard_map/ppermute | solution.py:220
  31.1 1.5 %shard_map.108 = (bf16[512,128]{1,0:T(8,128)(2,1)}, bf16[512,128]{1,0:T(8,128)(2,1)}) custom-call(bf16[512,128]{1,0:T(8,128)(2,1)S(1)} %copy-done, f32[512,128]{1,0:T(8,128)S(1)} %get-tuple-element.56.near_k_ref, f32[512,128]{1,0:T(8,128)S(1)} %get-tuple-element.57.near_v_ref, bf16[1,2,512,512]{3,2,1,0:T(8,128)(2,1)S(1)} %get-tuple-element.58.weight_ref, ...), custom_call_target="tpu_custom_call" | custom-call | tf_op jit(solution)/shard_map/pallas_call | solution.py:205
Async XLA Ops:
  0.6 11.8 %collective-permute-start = (bf16[512,128]{1,0:T(8,128)(2,1)}, bf16[512,128]{1,0:T(8,128)(2,1)S(1)}, u32[]{:S(2)}, u32[]{:S(2)}) collective-permute-start(bf16[512,128]{1,0:T(8,128)(2,1)} %k_ref.5), channel_id=1, source_target_pairs={{0,4},{4,8},{8,12},{12,16},{16,20},{20,24},{24,28},{28,0},{1,5},{5... | collective-permute-start | bytes 393224 | tf_op jit(solution)/shard_map/ppermute | solution.py:220
  3.7 8.8 %collective-permute-start.1 = (bf16[512,128]{1,0:T(8,128)(2,1)}, bf16[512,128]{1,0:T(8,128)(2,1)S(1)}, u32[]{:S(2)}, u32[]{:S(2)}) collective-permute-start(bf16[512,128]{1,0:T(8,128)(2,1)} %k_ref.5), channel_id=1, source_target_pairs={{0,8},{4,12},{8,16},{12,20},{16,24},{20,28},{24,0},{28,4},{1,9},{5... | collective-permute-start | bytes 393224 | tf_op jit(solution)/shard_map/ppermute | solution.py:220
  5.2 11.8 %collective-permute-start.2 = (bf16[512,128]{1,0:T(8,128)(2,1)}, bf16[512,128]{1,0:T(8,128)(2,1)S(1)}, u32[]{:S(2)}, u32[]{:S(2)}) collective-permute-start(bf16[512,128]{1,0:T(8,128)(2,1)} %v_ref.3), channel_id=1, source_target_pairs={{0,4},{4,8},{8,12},{12,16},{16,20},{20,24},{24,28},{28,0},{1,5},{5... | collective-permute-start | bytes 393224 | tf_op jit(solution)/shard_map/ppermute | solution.py:220
  6.7 10.3 %collective-permute-start.3 = (bf16[512,128]{1,0:T(8,128)(2,1)}, bf16[512,128]{1,0:T(8,128)(2,1)S(1)}, u32[]{:S(2)}, u32[]{:S(2)}) collective-permute-start(bf16[512,128]{1,0:T(8,128)(2,1)} %v_ref.3), channel_id=1, source_target_pairs={{0,8},{4,12},{8,16},{12,20},{16,24},{20,28},{24,0},{28,4},{1,9},{5... | collective-permute-start | bytes 393224 | tf_op jit(solution)/shard_map/ppermute | solution.py:220
  8.3 11.3 %collective-permute-start.7 = (bf16[512,128]{1,0:T(8,128)(2,1)}, bf16[512,128]{1,0:T(8,128)(2,1)S(1)}, u32[]{:S(2)}, u32[]{:S(2)}) collective-permute-start(bf16[512,128]{1,0:T(8,128)(2,1)} %q_ref.5), channel_id=1, source_target_pairs={{0,28},{4,0},{8,4},{12,8},{16,12},{20,16},{24,20},{28,24},{1,29},{... | collective-permute-start | bytes 393224 | tf_op jit(solution)/shard_map/ppermute | solution.py:220
  12.2 0.9 %copy-start.1 = (bf16[512,128]{1,0:T(8,128)(2,1)S(1)}, bf16[512,128]{1,0:T(8,128)(2,1)}, u32[]{:S(2)}) copy-start(bf16[512,128]{1,0:T(8,128)(2,1)} %q_ref.5) | copy-start | bytes 393220
  12.2 2.6 %copy-start.2 = (bf16[512,128]{1,0:T(8,128)(2,1)S(1)}, bf16[512,128]{1,0:T(8,128)(2,1)}, u32[]{:S(2)}) copy-start(bf16[512,128]{1,0:T(8,128)(2,1)} %k_ref.5) | copy-start | bytes 393220
  12.2 2.6 %copy-start.3 = (bf16[512,128]{1,0:T(8,128)(2,1)S(1)}, bf16[512,128]{1,0:T(8,128)(2,1)}, u32[]{:S(2)}) copy-start(bf16[512,128]{1,0:T(8,128)(2,1)} %gate_ref.3) | copy-start | bytes 393220
  12.2 2.6 %copy-start.4 = (bf16[512,128]{1,0:T(8,128)(2,1)S(1)}, bf16[512,128]{1,0:T(8,128)(2,1)}, u32[]{:S(2)}) copy-start(bf16[512,128]{1,0:T(8,128)(2,1)} %up_ref.3) | copy-start | bytes 393220
  12.2 4.8 %copy-start = (bf16[512,128]{1,0:T(8,128)(2,1)S(1)}, bf16[512,128]{1,0:T(8,128)(2,1)}, u32[]{:S(2)}) copy-start(bf16[512,128]{1,0:T(8,128)(2,1)} %v_ref.3) | copy-start | bytes 393220
  14.0 5.6 %collective-permute-start.8 = (bf16[512,128]{1,0:T(8,128)(2,1)S(1)}, bf16[512,128]{1,0:T(8,128)(2,1)S(1)}, u32[]{:S(2)}, u32[]{:S(2)}) collective-permute-start(bf16[512,128]{1,0:T(8,128)(2,1)S(1)} %copy-done.1), channel_id=1, source_target_pairs={{0,24},{4,28},{8,0},{12,4},{16,8},{20,12},{24,16},{28,20},{1,25},{... | collective-permute-start | bytes 393224 | tf_op jit(solution)/shard_map/ppermute | solution.py:220
  17.7 3.1 %collective-permute-start.4 = (f32[4,512]{1,0:T(4,128)S(1)}, f32[4,512]{1,0:T(4,128)S(1)}, u32[]{:S(2)}, u32[]{:S(2)}) collective-permute-start(f32[4,512]{1,0:T(4,128)S(1)} %get-tuple-element.44.refs_0_), channel_id=1, source_target_pairs={{0,3},{1,2},{2,1},{3,0},{4,7},{5,6},{6,5},{7,4},{8,11},{9,10},{10,... | collective-permute-start | bytes 24584 | tf_op jit(solution)/shard_map/ppermute | solution.py:227
  17.7 3.7 %collective-permute-start.5 = (f32[4,512]{1,0:T(4,128)S(1)}, f32[4,512]{1,0:T(4,128)S(1)}, u32[]{:S(2)}, u32[]{:S(2)}) collective-permute-start(f32[4,512]{1,0:T(4,128)S(1)} %get-tuple-element.44.refs_0_), channel_id=1, source_target_pairs={{0,2},{1,3},{2,0},{3,1},{4,6},{5,7},{6,4},{7,5},{8,10},{9,11},{10,... | collective-permute-start | bytes 24584 | tf_op jit(solution)/shard_map/ppermute | solution.py:227
  19.5 2.0 %collective-permute-start.6 = (f32[4,512]{1,0:T(4,128)S(1)}, f32[4,512]{1,0:T(4,128)S(1)}, u32[]{:S(2)}, u32[]{:S(2)}) collective-permute-start(f32[4,512]{1,0:T(4,128)S(1)} %get-tuple-element.44.refs_0_), channel_id=1, source_target_pairs={{0,1},{1,0},{2,3},{3,2},{4,5},{5,4},{6,7},{7,6},{8,9},{9,8},{10,11... | collective-permute-start | bytes 24584 | tf_op jit(solution)/shard_map/ppermute | solution.py:227
  21.8 7.9 %collective-permute-start.10 = (bf16[512,128]{1,0:T(8,128)(2,1)S(1)}, bf16[512,128]{1,0:T(8,128)(2,1)S(1)}, u32[]{:S(2)}, u32[]{:S(2)}) collective-permute-start(bf16[512,128]{1,0:T(8,128)(2,1)S(1)} %get-tuple-element.48.d_ref), channel_id=1, source_target_pairs={{0,24},{4,28},{8,0},{12,4},{16,8},{20,12},{24,16},{28,20},{1,25},{... | collective-permute-start | bytes 393224 | tf_op jit(solution)/shard_map/ppermute | solution.py:220
  23.7 7.4 %collective-permute-start.9 = (bf16[512,128]{1,0:T(8,128)(2,1)S(1)}, bf16[512,128]{1,0:T(8,128)(2,1)S(1)}, u32[]{:S(2)}, u32[]{:S(2)}) collective-permute-start(bf16[512,128]{1,0:T(8,128)(2,1)S(1)} %get-tuple-element.48.d_ref), channel_id=1, source_target_pairs={{0,28},{4,0},{8,4},{12,8},{16,12},{20,16},{24,20},{28,24},{1,29},{... | collective-permute-start | bytes 393224 | tf_op jit(solution)/shard_map/ppermute | solution.py:220

commit v4 on v3

--- a/solution.py
+++ b/solution.py
@@ -184,20 +184,19 @@
             gv_ref[here, at] = dot(own_weight_t_ref[head, here, :], d_ref[:, at], NN)
 
 
-def far_kernel(factor, v_ref, near_k_ref, near_v_ref, weight_ref, slope_ref, *refs):
-    queries, deltas, (gk_ref, gv_ref) = refs[:REACH], refs[REACH : 2 * REACH], refs[2 * REACH :]
+def far_kernel(factor, reach, v_ref, near_k_ref, near_v_ref, weight_ref, slope_ref, query_ref, d_ref, gk_ref, gv_ref):
     rows, features = v_ref.shape
     lanes, chunks = parts_of(rows, features)
-    for head, at in lanes:
-        for chunk, here in chunks:
-            ends = [here.stop if offset == REACH - 1 else rows for offset in range(REACH)]
-            delta = jnp.concatenate([ref[:end, at] for ref, end in zip(deltas, ends)], axis=0)
-            query = jnp.concatenate([ref[:end, at] for ref, end in zip(queries, ends)], axis=0)
-            slope = jnp.concatenate([slope_ref[head, offset, here, :end] for offset, end in enumerate(ends)], axis=1)
-            weight = jnp.concatenate([weight_ref[head, offset, here, :end] for offset, end in enumerate(ends)], axis=1)
-            grad = (dot(v_ref[here, at], delta, NT) * slope).astype(jnp.bfloat16)
-            gv_ref[here, at] = (near_v_ref[here, at] + dot(weight, delta, NN)).astype(jnp.bfloat16)
-            gk_ref[here, at] = ((near_k_ref[here, at] + dot(grad, query, NN)) * factor).astype(jnp.bfloat16)
+    last = reach == 1
+    for head, at in lanes:
+        for chunk, here in chunks:
+            end = here.stop if reach == REACH else rows
+            delta = d_ref[:end, at]
+            value = near_v_ref[here, at] + dot(weight_ref[head, reach - 1, here, :end], delta, NN)
+            grad = dot(v_ref[here, at], delta, NT) * slope_ref[head, reach - 1, here, :end]
+            key = near_k_ref[here, at] + dot(grad.astype(jnp.bfloat16), query_ref[:end, at], NN)
+            gv_ref[here, at] = value.astype(gv_ref.dtype)
+            gk_ref[here, at] = (key * factor if last else key).astype(gk_ref.dtype)
 
 
 def call(kernel, outs, *args, cost=None):
@@ -212,12 +211,11 @@
     )(*args)
 
 
-def shift(value, axis, steps, ring=True):
+def shift(value, axis, steps, around=True):
     count = lax.axis_size(axis)
     pairs = [(source, source + steps) for source in range(count)]
-    if ring:
-        pairs = [(source, target % count) for source, target in pairs]
-    return lax.ppermute(value, axis, [(s, t) for s, t in pairs if 0 <= t < count])
+    pairs = [(source, target % count) for source, target in pairs if around or 0 <= target < count]
+    return lax.ppermute(value, axis, pairs)
 
 
 def meet(value, axis, step):
@@ -239,8 +237,8 @@
     square = (rows_dev, rows_dev)
     steps = range(1, REACH + 1)
 
-    keys = [shift(key_vectors, "rows", offset) for offset in steps]
-    values = [shift(value_vectors, "rows", offset) for offset in steps]
+    keys = [shift(key_vectors, "rows", 1), shift(key_vectors, "rows", 2)]
+    values = [shift(value_vectors, "rows", 1), shift(value_vectors, "rows", 2)]
 
     starts, lasts = call(
         column_kernel, [((rows_dev, LANES), full)] * 2, relative, cost=pl.CostEstimate(flops=10**10, transcendentals=0, bytes_accessed=4*10**7),
@@ -256,7 +254,7 @@
         functools.partial(weight_kernel, factor), [(pair, half), (pair, full)], starts, queries, *keys
     )
     tied, _ = lax.optimization_barrier((queries, weights))
-    later = [shift(queries, "rows", -1), shift(tied, "rows", -2)]
+    later = [shift(queries, "rows", -1), shift(tied, "rows", -2, around=False)]
     attended, stats = call(
         attend_kernel,
         [(block, full), ((4, rows_dev), full)],
@@ -272,18 +270,21 @@
         [(block, full), (block, half)],
         attended, scaled, *all_stats,
     )
-    deltas = [shift(delta, "rows", -offset) for offset in steps]
+    deltas = [shift(delta, "rows", -1), shift(delta, "rows", -2)]
     grad_queries, near_key, near_value, layer_out, grad_gating = call(
         functools.partial(near_kernel, factor),
         [(block, half), (block, full), (block, full), (block, half), (block, half)],
         queries, key_vectors, value_vectors, gating, cotangent, delta, normed,
         own_slopes, own_weights_t, own_slopes_t, slopes, *keys, *values,
     )
-    grad_keys, grad_values = call(
-        functools.partial(far_kernel, factor),
-        [(block, half)] * 2,
-        value_vectors, near_key, near_value, weights_t, slopes_t, *later, *deltas,
-    )
+    sums = [near_key, near_value]
+    for offset in reversed(steps):
+        sums = call(
+            functools.partial(far_kernel, factor, offset),
+            [(block, half if offset == 1 else full)] * 2,
+            value_vectors, *sums, weights_t, slopes_t, later[offset - 1], deltas[offset - 1],
+        )
+    grad_keys, grad_values = sums
     return (layer_out, grad_queries, grad_keys, grad_values, grad_gating)
 
 

time: 32.8 us -> 31.3 us (0.954)
  starting transfers between devices: 19 us -> 17.8 us
  waiting for transfers between devices: 3.8 us -> 3.06 us
  Pallas kernels: 7.76 us -> 8.17 us
    ppermute x8, starting transfers between devices: 17 us -> 15.8 us  [shift(): return lax.ppermute(value, axis, pairs)]
    ppermute x3, waiting for transfers between devices: 0.96 us -> 0.01 us  [meet(): lax.ppermute(value, axis, [(source, source ^ step) for source in range(co...]
    pallas_call x8 -> x9, Pallas kernels: 7.76 us -> 8.17 us  [call(): pl.pallas_call(kernel, out_shape=[jax.ShapeDtypeStruct(shape, dtype) for...]
  transfers between devices with their start and end apart: 11 -> 11, of which waited for: 4 -> 3; matrix products, arithmetic and copies ran while one was open for 2% -> 2% of each run, Pallas kernels for 18% -> 21%
where the time goes in v4:
time: 31.3 us; the launch traced here: 31.1 us
  starting transfers between devices  17.8 us (57%)
  Pallas kernels  8.17 us (26%)
  waiting for transfers between devices  3.06 us (10%)
  between operations  0.78 us (2%)
  other arithmetic  0.69 us (2%)
  local copies, waits for them, and re-layouts  0.67 us (2%)
    ppermute x8, starting transfers between devices, shift(): return lax.ppermute(value, axis, pairs)  15.8 us
    pallas_call x9, Pallas kernels, call(): pl.pallas_call(kernel, out_shape=[jax.ShapeDtypeStruct(shape, dtype) for...  8.17 us
    ppermute x8, waiting for transfers between devices, shift(): return lax.ppermute(value, axis, pairs)  3.05 us
    ppermute x3, starting transfers between devices, meet(): lax.ppermute(value, axis, [(source, source ^ step) for source in range(co...  1.95 us
    convert_element_type x1, other arithmetic, local(): relative = (bounds - first_row).astype(jnp.float32)  0.69 us
    unnamed x10, local copies, waits for them, and re-layouts  0.67 us
  transfers between devices with their start and end apart: 11, of which 3 were waited for; matrix products, arithmetic and copies ran while one was open for 2% of the time, Pallas kernels for 21%

profile of v4, /device:TPU:0, one launch (start us, length us, event | category | flops | bytes accessed | tf_op | source)
XLA Modules:
  0.0 31.1 jit_solution(17384714772921721153)
XLA Ops:
  0.6 3.0 %collective-permute-start = (bf16[512,128]{1,0:T(8,128)(2,1)}, bf16[512,128]{1,0:T(8,128)(2,1)S(1)}, u32[]{:S(2)}, u32[]{:S(2)}) collective-permute-start(bf16[512,128]{1,0:T(8,128)(2,1)} %k_ref.5), channel_id=1, source_target_pairs={{0,4},{4,8},{8,12},{12,16},{16,20},{20,24},{24,28},{28,0},{1,5},{5... | collective-permute-start | bytes 393224 | tf_op jit(solution)/shard_map/ppermute | solution.py:218
  3.7 1.6 %collective-permute-start.1 = (bf16[512,128]{1,0:T(8,128)(2,1)}, bf16[512,128]{1,0:T(8,128)(2,1)S(1)}, u32[]{:S(2)}, u32[]{:S(2)}) collective-permute-start(bf16[512,128]{1,0:T(8,128)(2,1)} %k_ref.5), channel_id=1, source_target_pairs={{0,8},{4,12},{8,16},{12,20},{16,24},{20,28},{24,0},{28,4},{1,9},{5... | collective-permute-start | bytes 393224 | tf_op jit(solution)/shard_map/ppermute | solution.py:218
  5.2 1.5 %collective-permute-start.2 = (bf16[512,128]{1,0:T(8,128)(2,1)}, bf16[512,128]{1,0:T(8,128)(2,1)S(1)}, u32[]{:S(2)}, u32[]{:S(2)}) collective-permute-start(bf16[512,128]{1,0:T(8,128)(2,1)} %v_ref.5), channel_id=1, source_target_pairs={{0,4},{4,8},{8,12},{12,16},{16,20},{20,24},{24,28},{28,0},{1,5},{5... | collective-permute-start | bytes 393224 | tf_op jit(solution)/shard_map/ppermute | solution.py:218
  6.7 1.6 %collective-permute-start.3 = (bf16[512,128]{1,0:T(8,128)(2,1)}, bf16[512,128]{1,0:T(8,128)(2,1)S(1)}, u32[]{:S(2)}, u32[]{:S(2)}) collective-permute-start(bf16[512,128]{1,0:T(8,128)(2,1)} %v_ref.5), channel_id=1, source_target_pairs={{0,8},{4,12},{8,16},{12,20},{16,24},{20,28},{24,0},{28,4},{1,9},{5... | collective-permute-start | bytes 393224 | tf_op jit(solution)/shard_map/ppermute | solution.py:218
  8.3 3.2 %collective-permute-start.7 = (bf16[512,128]{1,0:T(8,128)(2,1)}, bf16[512,128]{1,0:T(8,128)(2,1)S(1)}, u32[]{:S(2)}, u32[]{:S(2)}) collective-permute-start(bf16[512,128]{1,0:T(8,128)(2,1)} %q_ref.5), channel_id=1, source_target_pairs={{0,28},{4,0},{8,4},{12,8},{16,12},{20,16},{24,20},{28,24},{1,29},{... | collective-permute-start | bytes 393224 | tf_op jit(solution)/shard_map/ppermute | solution.py:218
  11.5 0.7 %subtract_convert_fusion.row_ref = f32[2,512]{1,0:T(2,128)S(1)} fusion(s32[2,512]{1,0:T(2,128)} %param.10, s32[]{:T(128)S(6)} %mul.3), kind=kLoop, calls=%fused_computation | loop fusion | flops 2048 | bytes 8196 | tf_op jit(solution)/shard_map/convert_element_type | solution.py:235
  12.2 0.0 copy-start.1
  12.2 0.0 copy-start.2
  12.2 0.0 copy-start.3
  12.2 0.0 copy-start.4
  12.2 0.0 copy-start
  12.3 0.2 shard_map.101
  12.5 0.0 collective-permute-done.refs_0_
  12.5 0.0 collective-permute-done.1.refs_1_
  12.5 0.6 %copy-done.1 = bf16[512,128]{1,0:T(8,128)(2,1)S(1)} copy-done((bf16[512,128]{1,0:T(8,128)(2,1)S(1)}, bf16[512,128]{1,0:T(8,128)(2,1)}, u32[]{:S(2)}) %copy-start.1) | copy-done | bytes 131096
  13.1 0.9 %shard_map.103 = (bf16[1,2,512,512]{3,2,1,0:T(8,128)(2,1)S(1)}, f32[1,2,512,512]{3,2,1,0:T(8,128)S(1)}) custom-call(f32[512,128]{1,0:T(8,128)S(1)} %get-tuple-element.36.start_ref, bf16[512,128]{1,0:T(8,128)(2,1)S(1)} %copy-done.1, bf16[512,128]{1,0:T(8,128)(2,1)S(1)} %collective-permute-done.refs_0_, bf16[512,128]{1,0:T(8,128)(2,1)S(1)} %collective-permute-done.1.refs_1_), custom_call_target="tpu_custom_call" | custom-call | tf_op jit(solution)/shard_map/pallas_call | solution.py:204
  14.0 1.3 %collective-permute-start.8 = (bf16[512,128]{1,0:T(8,128)(2,1)S(1)}, bf16[512,128]{1,0:T(8,128)(2,1)S(1)}, u32[]{:S(2)}, u32[]{:S(2)}) collective-permute-start(bf16[512,128]{1,0:T(8,128)(2,1)S(1)} %copy-done.1), channel_id=1, source_target_pairs={{8,0},{12,4},{16,8},{20,12},{24,16},{28,20},{9,1},{13,5},{17,9},{2... | collective-permute-start | bytes 393224 | tf_op jit(solution)/shard_map/ppermute | solution.py:218
  15.3 0.0 copy-done.2
  15.3 0.0 copy-done.3
  15.3 0.0 copy-done.4
  15.3 0.7 %shard_map.102 = (bf16[1,512,512]{2,1,0:T(8,128)(2,1)S(1)}, f32[1,512,512]{2,1,0:T(8,128)S(1)}, bf16[1,512,512]{2,1,0:T(8,128)(2,1)S(1)}, f32[1,512,512]{2,1,0:T...) custom-call(f32[512,128]{1,0:T(8,128)S(1)} %get-tuple-element.36.start_ref, ...), custom_call_target="tpu_custom_call" | custom-call | tf_op jit(solution)/shard_map/pallas_call | solution.py:204
  16.1 0.8 %collective-permute-done.2.refs_1_.refs_2_ = bf16[512,128]{1,0:T(8,128)(2,1)S(1)} collective-permute-done((bf16[512,128]{1,0:T(8,128)(2,1)}, bf16[512,128]{1,0:T(8,128)(2,1)S(1)}, u32[]{:S(2)}, u32[]{:S(2)}) %collective-permute-start.2) | collective-permute-done | bytes 131104 | tf_op jit(solution)/shard_map/ppermute | solution.py:218
  16.9 0.0 collective-permute-done.3.refs_2_.refs_3_
  16.9 0.0 copy-done
  16.9 0.6 %shard_map.104 = (f32[512,128]{1,0:T(8,128)S(1)}, f32[4,512]{1,0:T(4,128)S(1)}) custom-call(bf16[1,512,512]{2,1,0:T(8,128)(2,1)S(1)} %get-tuple-element.38.own_weight_ref, f32[512,128]{1,0:T(8,128)S(1)} %get-tuple-element.39.scaled_ref, f32[1,512]{1,0:T(1,128)S(1)} %get-tuple-element.40.sum_ref, bf16[1,2,512,512]{3,2,1,0:T(8,128)(2,1)S(1)} %get-tuple-element.41.weight_ref, ...), custom_call_target="tpu_custom_call" | custom-call | tf_op jit(solution)/shard_map/pallas_call | solution.py:204
  17.5 0.1 collective-permute-start.4
  17.6 1.7 %collective-permute-start.5 = (f32[4,512]{1,0:T(4,128)S(1)}, f32[4,512]{1,0:T(4,128)S(1)}, u32[]{:S(2)}, u32[]{:S(2)}) collective-permute-start(f32[4,512]{1,0:T(4,128)S(1)} %get-tuple-element.46.refs_0_), channel_id=1, source_target_pairs={{0,2},{1,3},{2,0},{3,1},{4,6},{5,7},{6,4},{7,5},{8,10},{9,11},{10,... | collective-permute-start | bytes 24584 | tf_op jit(solution)/shard_map/ppermute | solution.py:225
  19.3 0.1 collective-permute-start.6
  19.5 0.0 collective-permute-done.7.refs_0_.query_ref
  19.5 1.4 %collective-permute-done.8.refs_1_.query_ref = bf16[512,128]{1,0:T(8,128)(2,1)S(1)} collective-permute-done((bf16[512,128]{1,0:T(8,128)(2,1)S(1)}, bf16[512,128]{1,0:T(8,128)(2,1)S(1)}, u32[]{:S(2)}, u32[]{:S(2)}) %collective-permute-start.8) | collective-permute-done | bytes 131104 | tf_op jit(solution)/shard_map/ppermute | solution.py:218
  20.9 0.9 %shard_map.105 = (bf16[1,2,512,512]{3,2,1,0:T(8,128)(2,1)S(1)}, f32[1,2,512,512]{3,2,1,0:T(8,128)S(1)}) custom-call(f32[512,128]{1,0:T(8,128)S(1)} %get-tuple-element.37.last_ref, bf16[512,128]{1,0:T(8,128)(2,1)S(1)} %copy-done.2, bf16[512,128]{1,0:T(8,128)(2,1)S(1)} %collective-permute-done.7.refs_0_.query_ref, ...), custom_call_target="tpu_custom_call" | custom-call | tf_op jit(solution)/shard_map/pallas_call | solution.py:204
  21.8 0.0 collective-permute-done.4.refs_1_
  21.8 0.0 collective-permute-done.5.refs_2_
  21.8 0.0 collective-permute-done.6.refs_3_
  21.8 0.3 %shard_map.106 = (f32[512,128]{1,0:T(8,128)S(1)}, bf16[512,128]{1,0:T(8,128)(2,1)S(1)}) custom-call(f32[512,128]{1,0:T(8,128)S(1)} %get-tuple-element.42.att_ref, f32[512,128]{1,0:T(8,128)S(1)} %get-tuple-element.39.scaled_ref, f32[4,512]{1,0:T(4,128)S(1)} %get-tuple-element.46.refs_0_, f32[4,512]{1,0:T(4,128)S(1)} %collective-permute-done.4.refs_1_, ...), custom_call_target="tpu_custom_call" | custom-call | tf_op jit(solution)/shard_map/pallas_call | solution.py:204
  22.1 1.5 %collective-permute-start.9 = (bf16[512,128]{1,0:T(8,128)(2,1)S(1)}, bf16[512,128]{1,0:T(8,128)(2,1)S(1)}, u32[]{:S(2)}, u32[]{:S(2)}) collective-permute-start(bf16[512,128]{1,0:T(8,128)(2,1)S(1)} %get-tuple-element.50.d_ref), channel_id=1, source_target_pairs={{0,24},{4,28},{8,0},{12,4},{16,8},{20,12},{24,16},{28,20},{1,25},{... | collective-permute-start | bytes 393224 | tf_op jit(solution)/shard_map/ppermute | solution.py:218
  23.7 2.1 %collective-permute-start.10 = (bf16[512,128]{1,0:T(8,128)(2,1)S(1)}, bf16[512,128]{1,0:T(8,128)(2,1)S(1)}, u32[]{:S(2)}, u32[]{:S(2)}) collective-permute-start(bf16[512,128]{1,0:T(8,128)(2,1)S(1)} %get-tuple-element.50.d_ref), channel_id=1, source_target_pairs={{0,28},{4,0},{8,4},{12,8},{16,12},{20,16},{24,20},{28,24},{1,29},{... | collective-permute-start | bytes 393224 | tf_op jit(solution)/shard_map/ppermute | solution.py:218
  25.8 2.5 %shard_map.107 = (bf16[512,128]{1,0:T(8,128)(2,1)}, f32[512,128]{1,0:T(8,128)S(1)}, f32[512,128]{1,0:T(8,128)S(1)}, bf16[512,128]{1,0:T(8,128)(2,1)}, bf16[512,128]{1,0:T(8,128)(2,1)}) custom-call(bf16[512,128]{1,0:T(8,128)(2,1)S(1)} %copy-done.1, bf16[512,128]{1,0:T(8,128)(2,1)S(1)} %copy-done.2, bf16[512,128]{1,0:T(8,128)(2,1)S(1)} %copy-done, ...), custom_call_target="tpu_custom_call" | custom-call | tf_op jit(solution)/shard_map/pallas_call | solution.py:204
  28.3 0.0 collective-permute-done.9.d_ref
  28.3 0.6 %shard_map.108 = (f32[512,128]{1,0:T(8,128)S(1)}, f32[512,128]{1,0:T(8,128)S(1)}) custom-call(bf16[512,128]{1,0:T(8,128)(2,1)S(1)} %copy-done, f32[512,128]{1,0:T(8,128)S(1)} %get-tuple-element.58.near_k_ref, f32[512,128]{1,0:T(8,128)S(1)} %get-tuple-element.59.near_v_ref, bf16[1,2,512,512]{3,2,1,0:T(8,128)(2,1)S(1)} %get-tuple-element.60.weight_ref, ...), custom_call_target="tpu_custom_call" | custom-call | tf_op jit(solution)/shard_map/pallas_call | solution.py:204
  28.9 0.8 %collective-permute-done.10.d_ref = bf16[512,128]{1,0:T(8,128)(2,1)S(1)} collective-permute-done((bf16[512,128]{1,0:T(8,128)(2,1)S(1)}, bf16[512,128]{1,0:T(8,128)(2,1)S(1)}, u32[]{:S(2)}, u32[]{:S(2)}) %collective-permute-start.10) | collective-permute-done | bytes 131104 | tf_op jit(solution)/shard_map/ppermute | solution.py:218
  29.8 1.4 %shard_map.109 = (bf16[512,128]{1,0:T(8,128)(2,1)}, bf16[512,128]{1,0:T(8,128)(2,1)}) custom-call(bf16[512,128]{1,0:T(8,128)(2,1)S(1)} %copy-done, f32[512,128]{1,0:T(8,128)S(1)} %get-tuple-element.62.near_k_ref, f32[512,128]{1,0:T(8,128)S(1)} %get-tuple-element.63.near_v_ref, bf16[1,2,512,512]{3,2,1,0:T(8,128)(2,1)S(1)} %get-tuple-element.60.weight_ref, ...), custom_call_target="tpu_custom_call" | custom-call | tf_op jit(solution)/shard_map/pallas_call | solution.py:204
Async XLA Ops:
  0.6 11.8 %collective-permute-start = (bf16[512,128]{1,0:T(8,128)(2,1)}, bf16[512,128]{1,0:T(8,128)(2,1)S(1)}, u32[]{:S(2)}, u32[]{:S(2)}) collective-permute-start(bf16[512,128]{1,0:T(8,128)(2,1)} %k_ref.5), channel_id=1, source_target_pairs={{0,4},{4,8},{8,12},{12,16},{16,20},{20,24},{24,28},{28,0},{1,5},{5... | collective-permute-start | bytes 393224 | tf_op jit(solution)/shard_map/ppermute | solution.py:218
  3.7 8.8 %collective-permute-start.1 = (bf16[512,128]{1,0:T(8,128)(2,1)}, bf16[512,128]{1,0:T(8,128)(2,1)S(1)}, u32[]{:S(2)}, u32[]{:S(2)}) collective-permute-start(bf16[512,128]{1,0:T(8,128)(2,1)} %k_ref.5), channel_id=1, source_target_pairs={{0,8},{4,12},{8,16},{12,20},{16,24},{20,28},{24,0},{28,4},{1,9},{5... | collective-permute-start | bytes 393224 | tf_op jit(solution)/shard_map/ppermute | solution.py:218
  5.2 11.7 %collective-permute-start.2 = (bf16[512,128]{1,0:T(8,128)(2,1)}, bf16[512,128]{1,0:T(8,128)(2,1)S(1)}, u32[]{:S(2)}, u32[]{:S(2)}) collective-permute-start(bf16[512,128]{1,0:T(8,128)(2,1)} %v_ref.5), channel_id=1, source_target_pairs={{0,4},{4,8},{8,12},{12,16},{16,20},{20,24},{24,28},{28,0},{1,5},{5... | collective-permute-start | bytes 393224 | tf_op jit(solution)/shard_map/ppermute | solution.py:218
  6.7 10.1 %collective-permute-start.3 = (bf16[512,128]{1,0:T(8,128)(2,1)}, bf16[512,128]{1,0:T(8,128)(2,1)S(1)}, u32[]{:S(2)}, u32[]{:S(2)}) collective-permute-start(bf16[512,128]{1,0:T(8,128)(2,1)} %v_ref.5), channel_id=1, source_target_pairs={{0,8},{4,12},{8,16},{12,20},{16,24},{20,28},{24,0},{28,4},{1,9},{5... | collective-permute-start | bytes 393224 | tf_op jit(solution)/shard_map/ppermute | solution.py:218
  8.3 11.1 %collective-permute-start.7 = (bf16[512,128]{1,0:T(8,128)(2,1)}, bf16[512,128]{1,0:T(8,128)(2,1)S(1)}, u32[]{:S(2)}, u32[]{:S(2)}) collective-permute-start(bf16[512,128]{1,0:T(8,128)(2,1)} %q_ref.5), channel_id=1, source_target_pairs={{0,28},{4,0},{8,4},{12,8},{16,12},{20,16},{24,20},{28,24},{1,29},{... | collective-permute-start | bytes 393224 | tf_op jit(solution)/shard_map/ppermute | solution.py:218
  12.2 0.9 %copy-start.1 = (bf16[512,128]{1,0:T(8,128)(2,1)S(1)}, bf16[512,128]{1,0:T(8,128)(2,1)}, u32[]{:S(2)}) copy-start(bf16[512,128]{1,0:T(8,128)(2,1)} %q_ref.5) | copy-start | bytes 393220
  12.2 3.1 %copy-start.2 = (bf16[512,128]{1,0:T(8,128)(2,1)S(1)}, bf16[512,128]{1,0:T(8,128)(2,1)}, u32[]{:S(2)}) copy-start(bf16[512,128]{1,0:T(8,128)(2,1)} %k_ref.5) | copy-start | bytes 393220
  12.2 3.1 %copy-start.3 = (bf16[512,128]{1,0:T(8,128)(2,1)S(1)}, bf16[512,128]{1,0:T(8,128)(2,1)}, u32[]{:S(2)}) copy-start(bf16[512,128]{1,0:T(8,128)(2,1)} %gate_ref.3) | copy-start | bytes 393220
  12.2 3.1 %copy-start.4 = (bf16[512,128]{1,0:T(8,128)(2,1)S(1)}, bf16[512,128]{1,0:T(8,128)(2,1)}, u32[]{:S(2)}) copy-start(bf16[512,128]{1,0:T(8,128)(2,1)} %up_ref.3) | copy-start | bytes 393220
  12.2 4.7 %copy-start = (bf16[512,128]{1,0:T(8,128)(2,1)S(1)}, bf16[512,128]{1,0:T(8,128)(2,1)}, u32[]{:S(2)}) copy-start(bf16[512,128]{1,0:T(8,128)(2,1)} %v_ref.5) | copy-start | bytes 393220
  14.0 6.9 %collective-permute-start.8 = (bf16[512,128]{1,0:T(8,128)(2,1)S(1)}, bf16[512,128]{1,0:T(8,128)(2,1)S(1)}, u32[]{:S(2)}, u32[]{:S(2)}) collective-permute-start(bf16[512,128]{1,0:T(8,128)(2,1)S(1)} %copy-done.1), channel_id=1, source_target_pairs={{8,0},{12,4},{16,8},{20,12},{24,16},{28,20},{9,1},{13,5},{17,9},{2... | collective-permute-start | bytes 393224 | tf_op jit(solution)/shard_map/ppermute | solution.py:218
  17.5 4.3 %collective-permute-start.4 = (f32[4,512]{1,0:T(4,128)S(1)}, f32[4,512]{1,0:T(4,128)S(1)}, u32[]{:S(2)}, u32[]{:S(2)}) collective-permute-start(f32[4,512]{1,0:T(4,128)S(1)} %get-tuple-element.46.refs_0_), channel_id=1, source_target_pairs={{0,3},{1,2},{2,1},{3,0},{4,7},{5,6},{6,5},{7,4},{8,11},{9,10},{10,... | collective-permute-start | bytes 24584 | tf_op jit(solution)/shard_map/ppermute | solution.py:225
  17.6 4.2 %collective-permute-start.5 = (f32[4,512]{1,0:T(4,128)S(1)}, f32[4,512]{1,0:T(4,128)S(1)}, u32[]{:S(2)}, u32[]{:S(2)}) collective-permute-start(f32[4,512]{1,0:T(4,128)S(1)} %get-tuple-element.46.refs_0_), channel_id=1, source_target_pairs={{0,2},{1,3},{2,0},{3,1},{4,6},{5,7},{6,4},{7,5},{8,10},{9,11},{10,... | collective-permute-start | bytes 24584 | tf_op jit(solution)/shard_map/ppermute | solution.py:225
  19.3 2.5 %collective-permute-start.6 = (f32[4,512]{1,0:T(4,128)S(1)}, f32[4,512]{1,0:T(4,128)S(1)}, u32[]{:S(2)}, u32[]{:S(2)}) collective-permute-start(f32[4,512]{1,0:T(4,128)S(1)} %get-tuple-element.46.refs_0_), channel_id=1, source_target_pairs={{0,1},{1,0},{2,3},{3,2},{4,5},{5,4},{6,7},{7,6},{8,9},{9,8},{10,11... | collective-permute-start | bytes 24584 | tf_op jit(solution)/shard_map/ppermute | solution.py:225
  22.1 6.2 %collective-permute-start.9 = (bf16[512,128]{1,0:T(8,128)(2,1)S(1)}, bf16[512,128]{1,0:T(8,128)(2,1)S(1)}, u32[]{:S(2)}, u32[]{:S(2)}) collective-permute-start(bf16[512,128]{1,0:T(8,128)(2,1)S(1)} %get-tuple-element.50.d_ref), channel_id=1, source_target_pairs={{0,24},{4,28},{8,0},{12,4},{16,8},{20,12},{24,16},{28,20},{1,25},{... | collective-permute-start | bytes 393224 | tf_op jit(solution)/shard_map/ppermute | solution.py:218
  23.7 6.1 %collective-permute-start.10 = (bf16[512,128]{1,0:T(8,128)(2,1)S(1)}, bf16[512,128]{1,0:T(8,128)(2,1)S(1)}, u32[]{:S(2)}, u32[]{:S(2)}) collective-permute-start(bf16[512,128]{1,0:T(8,128)(2,1)S(1)} %get-tuple-element.50.d_ref), channel_id=1, source_target_pairs={{0,28},{4,0},{8,4},{12,8},{16,12},{20,16},{24,20},{28,24},{1,29},{... | collective-permute-start | bytes 393224 | tf_op jit(solution)/shard_map/ppermute | solution.py:218

commit v5 on v4

--- a/solution.py
+++ b/solution.py
@@ -13,6 +13,7 @@
 VMEM_LIMIT = 20 * 1024 * 1024
 
 LANES = 128
+HINT = pl.CostEstimate(flops=10**10, transcendentals=0, bytes_accessed=4 * 10**7)
 NT = (((1,), (1,)), ((), ()))
 NN = (((1,), (0,)), ((), ()))
 
@@ -33,13 +34,11 @@
     return 256 if rows % 256 == 0 else rows
 
 
-def query_mask(start, rows, offset, chunk):
-    size, width = start.shape
-    keys = lax.broadcasted_iota(jnp.int32, (size, width), 1) - offset * rows
-    mask = keys.astype(jnp.float32) >= start
+def query_mask(start, rows, offset, order=None):
+    keys = (lax.broadcasted_iota(jnp.int32, start.shape, 1) - offset * rows).astype(jnp.float32)
+    mask = keys >= start
     if offset == 0:
-        queries = lax.broadcasted_iota(jnp.int32, (size, width), 0) + chunk * size
-        mask = mask & (keys <= queries)
+        mask = mask & (keys <= order)
     return mask
 
 
@@ -72,12 +71,16 @@
     return jnp.concatenate([ref[...]] * (width // ref.shape[1]), axis=1)
 
 
+def order_kernel(order_ref):
+    order_ref[...] = lax.broadcasted_iota(jnp.int32, order_ref.shape, 0).astype(jnp.float32)
+
+
 def column_kernel(row_ref, start_ref, last_ref):
     start_ref[...] = column(row_ref[0:1, :], LANES)
     last_ref[...] = column(row_ref[1:2, :], LANES)
 
 
-def own_kernel(factor, start_ref, last_ref, q_ref, k_ref, gate_ref, up_ref, *refs):
+def own_kernel(factor, order_ref, start_ref, last_ref, q_ref, k_ref, gate_ref, up_ref, *refs):
     weight_ref, slope_ref, weight_t_ref, slope_t_ref, scaled_ref, sum_ref = refs
     rows, features = q_ref.shape
     lanes, chunks = parts_of(rows, features)
@@ -86,7 +89,7 @@
     for head, at in lanes:
         for chunk, here in chunks:
             scores = dot(q_ref[here, at], k_ref[:, at], NT) * factor
-            weights, slope = silu_and_slope(scores, query_mask(starts[here], rows, 0, chunk))
+            weights, slope = silu_and_slope(scores, query_mask(starts[here], rows, 0, widen(order_ref, rows)[here]))
             weight_ref[head, here, :] = weights
             slope_ref[head, here, :] = slope
             scores = dot(k_ref[here, at], q_ref[:, at], NT) * factor
@@ -107,13 +110,15 @@
         for chunk, here in chunks:
             for offset in range(1, REACH + 1):
                 scores = dot(q_ref[here, at], keys[offset - 1][:, at], NT) * factor
-                weights, slope = silu_and_slope(scores, query_mask(starts[here], rows, offset, chunk))
+                weights, slope = silu_and_slope(scores, query_mask(starts[here], rows, offset))
                 weight_ref[head, offset - 1, here, :] = weights
                 slope_ref[head, offset - 1, here, :] = slope
 
 
-def later_kernel(factor, last_ref, k_ref, *refs):
-    queries, (weight_ref, slope_ref) = refs[:REACH], refs[REACH:]
+def later_kernel(factor, *refs):
+    flags, (last_ref, k_ref, *refs) = refs[:REACH], refs[REACH:]
+    taken, (weight_ref, slope_ref, *queries) = refs[: 2 * REACH], refs[2 * REACH :]
+    sort_blocks(flags, taken, queries, False)
     rows, features = k_ref.shape
     lanes, chunks = parts_of(rows, features)
     lasts = widen(last_ref, rows)
@@ -126,8 +131,11 @@
                 slope_ref[head, offset - 1, here, :] = slope
 
 
-def attend_kernel(own_weight_ref, scaled_ref, sum_ref, weight_ref, *refs):
-    values, (att_ref, stats_ref) = refs[: REACH + 1], refs[REACH + 1 :]
+def attend_kernel(*refs):
+    flags, (own_weight_ref, scaled_ref, sum_ref, weight_ref, own_ref, *refs) = refs[:REACH], refs[REACH:]
+    taken, (att_ref, stats_ref, *blocks) = refs[: 2 * REACH], refs[2 * REACH :]
+    sort_blocks(flags, taken, blocks, True)
+    values = [own_ref, *blocks]
     rows, features = scaled_ref.shape
     lanes, chunks = parts_of(rows, features)
     for head, at in lanes:
@@ -173,25 +181,29 @@
     for head, at in lanes:
         for chunk, here in chunks:
             delta = d_ref[here, at]
-            grad = (dot(delta, v_ref[:, at], NT) * own_slope_ref[head, here, :]).astype(jnp.bfloat16)
-            total = dot(grad, k_ref[:, at], NN)
+            till = here.stop
+            grad = dot(delta, v_ref[:till, at], NT) * own_slope_ref[head, here, :till]
+            total = dot(grad.astype(jnp.bfloat16), k_ref[:till, at], NN)
             for offset in range(REACH):
-                grad = dot(delta, values[offset][:, at], NT) * slope_ref[head, offset, here, :]
-                total += dot(grad.astype(jnp.bfloat16), keys[offset][:, at], NN)
+                low = here.start if offset == REACH - 1 else 0
+                grad = dot(delta, values[offset][low:, at], NT) * slope_ref[head, offset, here, low:]
+                total += dot(grad.astype(jnp.bfloat16), keys[offset][low:, at], NN)
             gq_ref[here, at] = (total * factor).astype(jnp.bfloat16)
-            grad = dot(v_ref[here, at], d_ref[:, at], NT) * own_slope_t_ref[head, here, :]
-            gk_ref[here, at] = dot(grad.astype(jnp.bfloat16), q_ref[:, at], NN)
-            gv_ref[here, at] = dot(own_weight_t_ref[head, here, :], d_ref[:, at], NN)
-
-
-def far_kernel(factor, reach, v_ref, near_k_ref, near_v_ref, weight_ref, slope_ref, query_ref, d_ref, gk_ref, gv_ref):
+            low = here.start
+            grad = dot(v_ref[here, at], d_ref[low:, at], NT) * own_slope_t_ref[head, here, low:]
+            gk_ref[here, at] = dot(grad.astype(jnp.bfloat16), q_ref[low:, at], NN)
+            gv_ref[here, at] = dot(own_weight_t_ref[head, here, low:], d_ref[low:, at], NN)
+
+
+def far_kernel(factor, reach, flag_ref, v_ref, near_k_ref, near_v_ref, weight_ref, slope_ref, query_ref, first_ref,
+               second_ref, gk_ref, gv_ref):
     rows, features = v_ref.shape
     lanes, chunks = parts_of(rows, features)
     last = reach == 1
     for head, at in lanes:
         for chunk, here in chunks:
             end = here.stop if reach == REACH else rows
-            delta = d_ref[:end, at]
+            delta = jnp.where(flag_ref[0] == 0, first_ref[:end, at], second_ref[:end, at])
             value = near_v_ref[here, at] + dot(weight_ref[head, reach - 1, here, :end], delta, NN)
             grad = dot(v_ref[here, at], delta, NT) * slope_ref[head, reach - 1, here, :end]
             key = near_k_ref[here, at] + dot(grad.astype(jnp.bfloat16), query_ref[:end, at], NN)
@@ -199,12 +211,12 @@
             gk_ref[here, at] = (key * factor if last else key).astype(gk_ref.dtype)
 
 
-def call(kernel, outs, *args, cost=None):
+def call(kernel, outs, *args, cost=None, scalars=0):
     vmem = pl.BlockSpec(memory_space=pltpu.VMEM)
     return pl.pallas_call(
         kernel,
         out_shape=[jax.ShapeDtypeStruct(shape, dtype) for shape, dtype in outs],
-        in_specs=[vmem] * len(args),
+        in_specs=[pl.BlockSpec(memory_space=pltpu.SMEM)] * scalars + [vmem] * (len(args) - scalars),
         out_specs=[vmem] * len(outs),
         cost_estimate=cost,
         compiler_params=pltpu.CompilerParams(vmem_limit_bytes=VMEM_LIMIT),
@@ -216,6 +228,40 @@
     pairs = [(source, source + steps) for source in range(count)]
     pairs = [(source, target % count) for source, target in pairs if around or 0 <= target < count]
     return lax.ppermute(value, axis, pairs)
+
+
+def trade(value, steps, late):
+    rows, heads = lax.axis_size("rows"), lax.axis_size("heads")
+    pairs = []
+    for row in range(rows):
+        other = ((row - steps * late) ^ steps) + steps * late
+        for head in range(heads):
+            alone = row < steps * late or other >= rows
+            target = (row, head ^ 1) if alone else (other, head)
+            pairs.append((row * heads + head, target[0] * heads + target[1]))
+    return lax.ppermute(value, ("rows", "heads"), pairs)
+
+
+def copy_if(condition, pairs):
+    @pl.when(condition)
+    def _():
+        for target, source in pairs:
+            target[...] = source[...]
+
+
+def pick_kernel(*refs):
+    flags, (up_ref, down_ref, *refs) = refs[:REACH], refs[REACH:]
+    for reach in range(REACH):
+        first, second = refs[2 * reach], refs[2 * reach + 1]
+        copy_if(flags[reach][0] == 0, [(first, up_ref), (second, down_ref)])
+        copy_if(flags[reach][0] == 1, [(first, down_ref), (second, up_ref)])
+
+
+def sort_blocks(flags, taken, blocks, before):
+    for reach in range(REACH):
+        first, second = taken[2 * reach], taken[2 * reach + 1]
+        copy_if(flags[reach][0] == int(before), [(blocks[reach], first)])
+        copy_if(flags[reach][0] == int(not before), [(blocks[reach], second)])
 
 
 def meet(value, axis, step):
@@ -238,39 +284,43 @@
     steps = range(1, REACH + 1)
 
     keys = [shift(key_vectors, "rows", 1), shift(key_vectors, "rows", 2)]
-    values = [shift(value_vectors, "rows", 1), shift(value_vectors, "rows", 2)]
-
-    starts, lasts = call(
-        column_kernel, [((rows_dev, LANES), full)] * 2, relative, cost=pl.CostEstimate(flops=10**10, transcendentals=0, bytes_accessed=4*10**7),
-    )
+
+    order, = call(order_kernel, [((rows_dev, LANES), full)], cost=HINT)
+    starts, lasts = call(column_kernel, [((rows_dev, LANES), full)] * 2, relative)
+    position = lax.axis_index("rows")
+    flags = [(position // reach % 2).astype(jnp.int32).reshape(1) for reach in steps]
+    tied, _ = lax.optimization_barrier((value_vectors, order))
+    given = call(pick_kernel, [(block, half)] * (2 * REACH), *flags, tied, queries, scalars=REACH)
+    taken = [trade(given[0], 1, 0), trade(given[1], 1, 1), trade(given[2], 2, 0), trade(given[3], 2, 1)]
     own = (heads_dev, *square)
     own_weights, own_slopes, own_weights_t, own_slopes_t, scaled, scaled_sum = call(
         functools.partial(own_kernel, factor),
         [(own, half), (own, full), (own, half), (own, full), (block, full), ((1, rows_dev), full)],
-        starts, lasts, queries, key_vectors, gating, cotangent,
+        order, starts, lasts, queries, key_vectors, gating, cotangent,
     )
     pair = (heads_dev, REACH, *square)
     weights, slopes = call(
         functools.partial(weight_kernel, factor), [(pair, half), (pair, full)], starts, queries, *keys
     )
-    tied, _ = lax.optimization_barrier((queries, weights))
-    later = [shift(queries, "rows", -1), shift(tied, "rows", -2, around=False)]
-    attended, stats = call(
+    attended, stats, *values = call(
         attend_kernel,
-        [(block, full), ((4, rows_dev), full)],
-        own_weights, scaled, scaled_sum, weights, value_vectors, *values,
-    )
-    weights_t, slopes_t = call(
-        functools.partial(later_kernel, factor), [(pair, half), (pair, full)], lasts, key_vectors, *later
-    )
-    all_stats = [stats] + [meet(stats, "heads", step) for step in reversed(range(1, heads))]
+        [(block, full), ((4, rows_dev), full)] + [(block, half)] * REACH,
+        *flags, own_weights, scaled, scaled_sum, weights, value_vectors, *taken, scalars=REACH,
+    )
+    weights_t, slopes_t, *later = call(
+        functools.partial(later_kernel, factor),
+        [(pair, half), (pair, full)] + [(block, half)] * REACH,
+        *flags, lasts, key_vectors, *taken, scalars=REACH,
+    )
+    all_stats = [stats] + [meet(stats, "heads", step) for step in range(1, heads)]
     all_stats, weights_t = lax.optimization_barrier((all_stats, weights_t))
     normed, delta = call(
         functools.partial(delta_kernel, float(block[1] * heads)),
         [(block, full), (block, half)],
         attended, scaled, *all_stats,
     )
-    deltas = [shift(delta, "rows", -1), shift(delta, "rows", -2)]
+    delta_one = [shift(delta, "rows", -1)] * 2
+    deltas = [delta_one, [trade(delta, 2, 0), trade(delta, 2, 1)]]
     grad_queries, near_key, near_value, layer_out, grad_gating = call(
         functools.partial(near_kernel, factor),
         [(block, half), (block, full), (block, full), (block, half), (block, half)],
@@ -282,7 +332,8 @@
         sums = call(
             functools.partial(far_kernel, factor, offset),
             [(block, half if offset == 1 else full)] * 2,
-            value_vectors, *sums, weights_t, slopes_t, later[offset - 1], deltas[offset - 1],
+            flags[offset - 1], value_vectors, *sums, weights_t, slopes_t, later[offset - 1], *deltas[offset - 1],
+            scalars=1,
         )
     grad_keys, grad_values = sums
     return (layer_out, grad_queries, grad_keys, grad_values, grad_gating)

time: 31.3 us -> 31.2 us (level)
  waiting for transfers between devices: 3.06 us -> 5.58 us
  starting transfers between devices: 17.8 us -> 16.4 us
  other arithmetic: 0.69 us -> 0.01 us
  local copies, waits for them, and re-layouts: 0.67 us -> 0.03 us
    ppermute x8 -> x3, starting transfers between devices: 15.8 us -> 7.19 us  [shift(): return lax.ppermute(value, axis, pairs)]
    ppermute x0 -> x6, starting transfers between devices: none -> 7.32 us  [trade(): return lax.ppermute(value, ('rows', 'heads'), pairs)]
    ppermute x8 -> x3, waiting for transfers between devices: 3.05 us -> 4.63 us  [shift(): return lax.ppermute(value, axis, pairs)]
    ppermute x3, waiting for transfers between devices: 0.01 us -> 0.93 us  [meet(): lax.ppermute(value, axis, [(source, source ^ step) for source in range(co...]
    convert_element_type x1, other arithmetic: 0.69 us -> 0.01 us  [local(): relative = (bounds - first_row).astype(jnp.float32)]
    unnamed x10 -> x12, local copies, waits for them, and re-layouts: 0.67 us -> 0.03 us
    pallas_call x9 -> x11, Pallas kernels: 8.17 us -> 8.17 us  [call(): pl.pallas_call(kernel, out_shape=[jax.ShapeDtypeStruct(shape, dtype) for...]
  transfers between devices with their start and end apart: 11 -> 12, of which waited for: 3 -> 5; matrix products, arithmetic and copies ran while one was open for 2% -> 0% of each run, Pallas kernels for 21% -> 19%
where the time goes in v5:
time: 31.2 us; the launch traced here: 31.1 us
  starting transfers between devices  16.4 us (53%)
  Pallas kernels  8.17 us (26%)
  waiting for transfers between devices  5.58 us (18%)
  between operations  0.86 us (3%)
    pallas_call x11, Pallas kernels, call(): pl.pallas_call(kernel, out_shape=[jax.ShapeDtypeStruct(shape, dtype) for...  8.17 us
    ppermute x6, starting transfers between devices, trade(): return lax.ppermute(value, ('rows', 'heads'), pairs)  7.32 us
    ppermute x3, starting transfers between devices, shift(): return lax.ppermute(value, axis, pairs)  7.19 us
    ppermute x3, waiting for transfers between devices, shift(): return lax.ppermute(value, axis, pairs)  4.63 us
    ppermute x3, starting transfers between devices, meet(): lax.ppermute(value, axis, [(source, source ^ step) for source in range(co...  1.92 us
    ppermute x3, waiting for transfers between devices, meet(): lax.ppermute(value, axis, [(source, source ^ step) for source in range(co...  0.93 us
  transfers between devices with their start and end apart: 12, of which 5 were waited for; matrix products, arithmetic and copies ran while one was open for 0% of the time, Pallas kernels for 19%

profile of v5, /device:TPU:0, one launch (start us, length us, event | category | flops | bytes accessed | tf_op | source)
XLA Modules:
  0.0 31.1 jit_solution(9752289305790238060)
XLA Ops:
  0.6 0.0 copy-start.2
  0.6 0.0 copy-start
  0.7 0.0 copy-start.1
  0.7 0.0 copy-start.5
  0.7 0.0 copy-start.4
  0.7 0.0 copy-start.3
  0.7 3.1 %collective-permute-start.1 = (bf16[512,128]{1,0:T(8,128)(2,1)}, bf16[512,128]{1,0:T(8,128)(2,1)S(1)}, u32[]{:S(2)}, u32[]{:S(2)}) collective-permute-start(bf16[512,128]{1,0:T(8,128)(2,1)} %k_ref.3), channel_id=1, source_target_pairs={{0,8},{4,12},{8,16},{12,20},{16,24},{20,28},{24,0},{28,4},{1,9},{5... | collective-permute-start | bytes 393224 | tf_op jit(solution)/shard_map/ppermute | solution.py:230
  3.8 1.5 %collective-permute-start = (bf16[512,128]{1,0:T(8,128)(2,1)}, bf16[512,128]{1,0:T(8,128)(2,1)S(1)}, u32[]{:S(2)}, u32[]{:S(2)}) collective-permute-start(bf16[512,128]{1,0:T(8,128)(2,1)} %k_ref.3), channel_id=1, source_target_pairs={{0,4},{4,8},{8,12},{12,16},{16,20},{20,24},{24,28},{28,0},{1,5},{5... | collective-permute-start | bytes 393224 | tf_op jit(solution)/shard_map/ppermute | solution.py:230
  5.3 0.0 copy-done
  5.4 0.0 copy-done.1
  5.4 0.1 shard_map.105
  5.4 1.6 %collective-permute-start.2 = (bf16[512,128]{1,0:T(8,128)(2,1)S(1)}, bf16[512,128]{1,0:T(8,128)(2,1)S(1)}, u32[]{:S(2)}, u32[]{:S(2)}) collective-permute-start(bf16[512,128]{1,0:T(8,128)(2,1)S(1)} %get-tuple-element.51), channel_id=1, source_target_pairs={{0,4},{1,5},{2,6},{3,7},{4,0},{5,1},{6,2},{7,3},{8,12},{9,13},{10,... | collective-permute-start | bytes 393224 | tf_op jit(solution)/shard_map/ppermute | solution.py:242
  7.0 0.0 collective-permute-start.3
  7.0 2.0 %collective-permute-start.4 = (bf16[512,128]{1,0:T(8,128)(2,1)S(1)}, bf16[512,128]{1,0:T(8,128)(2,1)S(1)}, u32[]{:S(2)}, u32[]{:S(2)}) collective-permute-start(bf16[512,128]{1,0:T(8,128)(2,1)S(1)} %get-tuple-element.53), channel_id=1, source_target_pairs={{0,8},{1,9},{2,10},{3,11},{4,12},{5,13},{6,14},{7,15},{8,0},{9,1},... | collective-permute-start | bytes 393224 | tf_op jit(solution)/shard_map/ppermute | solution.py:242
  9.0 0.6 %collective-permute-done.1.refs_1_ = bf16[512,128]{1,0:T(8,128)(2,1)S(1)} collective-permute-done((bf16[512,128]{1,0:T(8,128)(2,1)}, bf16[512,128]{1,0:T(8,128)(2,1)S(1)}, u32[]{:S(2)}, u32[]{:S(2)}) %collective-permute-start.1) | collective-permute-done | bytes 131104 | tf_op jit(solution)/shard_map/ppermute | solution.py:230
  9.6 0.0 collective-permute-start.5
  9.6 0.0 copy-done.5
  9.6 0.2 shard_map.102
  9.8 0.0 copy-done.2
  9.8 0.0 copy-done.4
  9.8 0.0 copy-done.3
  9.8 0.9 %shard_map.103 = (bf16[1,512,512]{2,1,0:T(8,128)(2,1)S(1)}, f32[1,512,512]{2,1,0:T(8,128)S(1)}, bf16[1,512,512]{2,1,0:T(8,128)(2,1)S(1)}, f32[1,512,512]{2,1,0:T...) custom-call(f32[512,128]{1,0:T(8,128)S(1)} %shard_map.101.order_ref, ...), custom_call_target="tpu_custom_call" | custom-call | tf_op jit(solution)/shard_map/pallas_call | solution.py:216
  10.8 3.6 %collective-permute-done.refs_0_ = bf16[512,128]{1,0:T(8,128)(2,1)S(1)} collective-permute-done((bf16[512,128]{1,0:T(8,128)(2,1)}, bf16[512,128]{1,0:T(8,128)(2,1)S(1)}, u32[]{:S(2)}, u32[]{:S(2)}) %collective-permute-start) | collective-permute-done | bytes 131104 | tf_op jit(solution)/shard_map/ppermute | solution.py:230
  14.3 0.9 %shard_map.104 = (bf16[1,2,512,512]{3,2,1,0:T(8,128)(2,1)S(1)}, f32[1,2,512,512]{3,2,1,0:T(8,128)S(1)}) custom-call(f32[512,128]{1,0:T(8,128)S(1)} %get-tuple-element.44.start_ref, bf16[512,128]{1,0:T(8,128)(2,1)S(1)} %copy-done.1, bf16[512,128]{1,0:T(8,128)(2,1)S(1)} %collective-permute-done.refs_0_, bf16[512,128]{1,0:T(8,128)(2,1)S(1)} %collective-permute-done.1.refs_1_), custom_call_target="tpu_custom_call" | custom-call | tf_op jit(solution)/shard_map/pallas_call | solution.py:216
  15.2 0.0 collective-permute-done.2.refs_7_.refs_4_
  15.2 0.0 collective-permute-done.3.refs_8_.refs_5_
  15.3 0.0 collective-permute-done.4.refs_9_.refs_6_
  15.3 0.0 collective-permute-done.5.refs_10_.refs_7_
  15.3 0.7 %shard_map.106 = (f32[512,128]{1,0:T(8,128)S(1)}, f32[4,512]{1,0:T(4,128)S(1)}, bf16[512,128]{1,0:T(8,128)(2,1)S(1)}, bf16[512,128]{1,0:T(8,128)(2,1)S(1)}) custom-call(s32[1]{0:T(128)} %bitcast.refs_0_.flag_ref, s32[1]{0:T(128)} %bitcast.1.refs_1_.flag_ref, bf16[1,512,512]{2,1,0:T(8,128)(2,1)S(1)} %get-tuple-element.46.refs_2_, ...), custom_call_target="tpu_custom_call" | custom-call | tf_op jit(solution)/shard_map/pallas_call | solution.py:216
  15.9 0.1 collective-permute-start.8
  16.0 1.6 %collective-permute-start.7 = (f32[4,512]{1,0:T(4,128)S(1)}, f32[4,512]{1,0:T(4,128)S(1)}, u32[]{:S(2)}, u32[]{:S(2)}) collective-permute-start(f32[4,512]{1,0:T(4,128)S(1)} %get-tuple-element.58.refs_0_), channel_id=1, source_target_pairs={{0,2},{1,3},{2,0},{3,1},{4,6},{5,7},{6,4},{7,5},{8,10},{9,11},{10,... | collective-permute-start | bytes 24584 | tf_op jit(solution)/shard_map/ppermute | solution.py:271
  17.6 0.3 collective-permute-start.6
  17.9 0.9 %shard_map.107 = (bf16[1,2,512,512]{3,2,1,0:T(8,128)(2,1)S(1)}, f32[1,2,512,512]{3,2,1,0:T(8,128)S(1)}, bf16[512,128]{1,0:T(8,128)(2,1)S(1)}, bf16[512,128]{1,0:T(8,128)(2,1)S(1)}) custom-call(s32[1]{0:T(128)} %bitcast.refs_0_.flag_ref, s32[1]{0:T(128)} %bitcast.1.refs_1_.flag_ref, f32[512,128]{1,0:T(8,128)S(1)} %get-tuple-element.45.last_ref.refs_2_, ...), custom_call_target="tpu_custom_call" | custom-call | tf_op jit(solution)/shard_map/pallas_call | solution.py:216
  18.8 0.3 %collective-permute-done.8.refs_3_ = f32[4,512]{1,0:T(4,128)S(1)} collective-permute-done((f32[4,512]{1,0:T(4,128)S(1)}, f32[4,512]{1,0:T(4,128)S(1)}, u32[]{:S(2)}, u32[]{:S(2)}) %collective-permute-start.8) | collective-permute-done | bytes 8224 | tf_op jit(solution)/shard_map/ppermute | solution.py:271
  19.1 0.6 %collective-permute-done.7.refs_2_ = f32[4,512]{1,0:T(4,128)S(1)} collective-permute-done((f32[4,512]{1,0:T(4,128)S(1)}, f32[4,512]{1,0:T(4,128)S(1)}, u32[]{:S(2)}, u32[]{:S(2)}) %collective-permute-start.7) | collective-permute-done | bytes 8224 | tf_op jit(solution)/shard_map/ppermute | solution.py:271
  19.7 0.0 collective-permute-done.6.refs_1_
  19.7 0.4 %shard_map.108 = (f32[512,128]{1,0:T(8,128)S(1)}, bf16[512,128]{1,0:T(8,128)(2,1)S(1)}) custom-call(f32[512,128]{1,0:T(8,128)S(1)} %get-tuple-element.55.att_ref, f32[512,128]{1,0:T(8,128)S(1)} %get-tuple-element.47.refs_3_.scaled_ref, f32[4,512]{1,0:T(4,128)S(1)} %get-tuple-element.58.refs_0_, f32[4,512]{1,0:T(4,128)S(1)} %collective-permute-done.6.refs_1_, ...), custom_call_target="tpu_custom_call" | custom-call | tf_op jit(solution)/shard_map/pallas_call | solution.py:216
  20.1 0.4 %collective-permute-start.10 = (bf16[512,128]{1,0:T(8,128)(2,1)S(1)}, bf16[512,128]{1,0:T(8,128)(2,1)S(1)}, u32[]{:S(2)}, u32[]{:S(2)}) collective-permute-start(bf16[512,128]{1,0:T(8,128)(2,1)S(1)} %get-tuple-element.62.d_ref), channel_id=1, source_target_pairs={{0,1},{1,0},{2,3},{3,2},{4,5},{5,4},{6,7},{7,6},{8,16},{9,17},{10,... | collective-permute-start | bytes 393224 | tf_op jit(solution)/shard_map/ppermute | solution.py:242
  20.5 3.3 %collective-permute-start.9 = (bf16[512,128]{1,0:T(8,128)(2,1)S(1)}, bf16[512,128]{1,0:T(8,128)(2,1)S(1)}, u32[]{:S(2)}, u32[]{:S(2)}) collective-permute-start(bf16[512,128]{1,0:T(8,128)(2,1)S(1)} %get-tuple-element.62.d_ref), channel_id=1, source_target_pairs={{0,8},{1,9},{2,10},{3,11},{4,12},{5,13},{6,14},{7,15},{8,0},{9,1},... | collective-permute-start | bytes 393224 | tf_op jit(solution)/shard_map/ppermute | solution.py:242
  23.9 2.6 %collective-permute-start.11 = (bf16[512,128]{1,0:T(8,128)(2,1)S(1)}, bf16[512,128]{1,0:T(8,128)(2,1)S(1)}, u32[]{:S(2)}, u32[]{:S(2)}) collective-permute-start(bf16[512,128]{1,0:T(8,128)(2,1)S(1)} %get-tuple-element.62.d_ref), channel_id=1, source_target_pairs={{0,28},{4,0},{8,4},{12,8},{16,12},{20,16},{24,20},{28,24},{1,29},{... | collective-permute-start | bytes 393224 | tf_op jit(solution)/shard_map/ppermute | solution.py:230
  26.5 2.1 %shard_map.109 = (bf16[512,128]{1,0:T(8,128)(2,1)}, f32[512,128]{1,0:T(8,128)S(1)}, f32[512,128]{1,0:T(8,128)S(1)}, bf16[512,128]{1,0:T(8,128)(2,1)}, bf16[512,128]{1,0:T(8,128)(2,1)}) custom-call(bf16[512,128]{1,0:T(8,128)(2,1)S(1)} %copy-done.1, bf16[512,128]{1,0:T(8,128)(2,1)S(1)} %copy-done.2, bf16[512,128]{1,0:T(8,128)(2,1)S(1)} %copy-done, ...), custom_call_target="tpu_custom_call" | custom-call | tf_op jit(solution)/shard_map/pallas_call | solution.py:216
  28.6 0.0 collective-permute-done.10.second_ref
  28.6 0.0 collective-permute-done.9.first_ref
  28.6 0.6 %shard_map.110 = (f32[512,128]{1,0:T(8,128)S(1)}, f32[512,128]{1,0:T(8,128)S(1)}) custom-call(s32[1]{0:T(128)} %bitcast.1.refs_1_.flag_ref, bf16[512,128]{1,0:T(8,128)(2,1)S(1)} %copy-done, f32[512,128]{1,0:T(8,128)S(1)} %get-tuple-element.72.near_k_ref, f32[512,128]{1,0:T(8,128)S(1)} %get-tuple-element.73.near_v_ref, ...), custom_call_target="tpu_custom_call" | custom-call | tf_op jit(solution)/shard_map/pallas_call | solution.py:216
  29.2 0.4 %collective-permute-done.11.first_ref.second_ref = bf16[512,128]{1,0:T(8,128)(2,1)S(1)} collective-permute-done((bf16[512,128]{1,0:T(8,128)(2,1)S(1)}, bf16[512,128]{1,0:T(8,128)(2,1)S(1)}, u32[]{:S(2)}, u32[]{:S(2)}) %collective-permute-start.11) | collective-permute-done | bytes 131104 | tf_op jit(solution)/shard_map/ppermute | solution.py:230
  29.7 1.4 %shard_map.111 = (bf16[512,128]{1,0:T(8,128)(2,1)}, bf16[512,128]{1,0:T(8,128)(2,1)}) custom-call(s32[1]{0:T(128)} %bitcast.refs_0_.flag_ref, bf16[512,128]{1,0:T(8,128)(2,1)S(1)} %copy-done, f32[512,128]{1,0:T(8,128)S(1)} %get-tuple-element.77.near_k_ref, f32[512,128]{1,0:T(8,128)S(1)} %get-tuple-element.78.near_v_ref, ...), custom_call_target="tpu_custom_call" | custom-call | tf_op jit(solution)/shard_map/pallas_call | solution.py:216
  (2 shorter events, 0.0 us)
Async XLA Ops:
  0.6 9.2 %copy-start.2 = (bf16[512,128]{1,0:T(8,128)(2,1)S(1)}, bf16[512,128]{1,0:T(8,128)(2,1)}, u32[]{:S(2)}) copy-start(bf16[512,128]{1,0:T(8,128)(2,1)} %k_ref.3) | copy-start | bytes 393220
  0.6 4.7 %copy-start = (bf16[512,128]{1,0:T(8,128)(2,1)S(1)}, bf16[512,128]{1,0:T(8,128)(2,1)}, u32[]{:S(2)}) copy-start(bf16[512,128]{1,0:T(8,128)(2,1)} %v_ref.5) | copy-start | bytes 393220
  0.7 4.7 %copy-start.1 = (bf16[512,128]{1,0:T(8,128)(2,1)S(1)}, bf16[512,128]{1,0:T(8,128)(2,1)}, u32[]{:S(2)}) copy-start(bf16[512,128]{1,0:T(8,128)(2,1)} %q_ref.5) | copy-start | bytes 393220
  0.7 8.9 %copy-start.5 = (s32[2,512]{1,0:T(2,128)S(1)}, s32[2,512]{1,0:T(2,128)}, u32[]{:S(2)}) copy-start(s32[2,512]{1,0:T(2,128)} %param.10) | copy-start | bytes 12292
  0.7 9.2 %copy-start.4 = (bf16[512,128]{1,0:T(8,128)(2,1)S(1)}, bf16[512,128]{1,0:T(8,128)(2,1)}, u32[]{:S(2)}) copy-start(bf16[512,128]{1,0:T(8,128)(2,1)} %up_ref.3) | copy-start | bytes 393220
  0.7 9.2 %copy-start.3 = (bf16[512,128]{1,0:T(8,128)(2,1)S(1)}, bf16[512,128]{1,0:T(8,128)(2,1)}, u32[]{:S(2)}) copy-start(bf16[512,128]{1,0:T(8,128)(2,1)} %gate_ref.3) | copy-start | bytes 393220
  0.7 8.9 %collective-permute-start.1 = (bf16[512,128]{1,0:T(8,128)(2,1)}, bf16[512,128]{1,0:T(8,128)(2,1)S(1)}, u32[]{:S(2)}, u32[]{:S(2)}) collective-permute-start(bf16[512,128]{1,0:T(8,128)(2,1)} %k_ref.3), channel_id=1, source_target_pairs={{0,8},{4,12},{8,16},{12,20},{16,24},{20,28},{24,0},{28,4},{1,9},{5... | collective-permute-start | bytes 393224 | tf_op jit(solution)/shard_map/ppermute | solution.py:230
  3.8 10.6 %collective-permute-start = (bf16[512,128]{1,0:T(8,128)(2,1)}, bf16[512,128]{1,0:T(8,128)(2,1)S(1)}, u32[]{:S(2)}, u32[]{:S(2)}) collective-permute-start(bf16[512,128]{1,0:T(8,128)(2,1)} %k_ref.3), channel_id=1, source_target_pairs={{0,4},{4,8},{8,12},{12,16},{16,20},{20,24},{24,28},{28,0},{1,5},{5... | collective-permute-start | bytes 393224 | tf_op jit(solution)/shard_map/ppermute | solution.py:230
  5.4 9.8 %collective-permute-start.2 = (bf16[512,128]{1,0:T(8,128)(2,1)S(1)}, bf16[512,128]{1,0:T(8,128)(2,1)S(1)}, u32[]{:S(2)}, u32[]{:S(2)}) collective-permute-start(bf16[512,128]{1,0:T(8,128)(2,1)S(1)} %get-tuple-element.51), channel_id=1, source_target_pairs={{0,4},{1,5},{2,6},{3,7},{4,0},{5,1},{6,2},{7,3},{8,12},{9,13},{10,... | collective-permute-start | bytes 393224 | tf_op jit(solution)/shard_map/ppermute | solution.py:242
  7.0 8.2 %collective-permute-start.3 = (bf16[512,128]{1,0:T(8,128)(2,1)S(1)}, bf16[512,128]{1,0:T(8,128)(2,1)S(1)}, u32[]{:S(2)}, u32[]{:S(2)}) collective-permute-start(bf16[512,128]{1,0:T(8,128)(2,1)S(1)} %get-tuple-element.52), channel_id=1, source_target_pairs={{0,1},{1,0},{2,3},{3,2},{4,8},{5,9},{6,10},{7,11},{8,4},{9,5},{10,... | collective-permute-start | bytes 393224 | tf_op jit(solution)/shard_map/ppermute | solution.py:242
  7.0 8.2 %collective-permute-start.4 = (bf16[512,128]{1,0:T(8,128)(2,1)S(1)}, bf16[512,128]{1,0:T(8,128)(2,1)S(1)}, u32[]{:S(2)}, u32[]{:S(2)}) collective-permute-start(bf16[512,128]{1,0:T(8,128)(2,1)S(1)} %get-tuple-element.53), channel_id=1, source_target_pairs={{0,8},{1,9},{2,10},{3,11},{4,12},{5,13},{6,14},{7,15},{8,0},{9,1},... | collective-permute-start | bytes 393224 | tf_op jit(solution)/shard_map/ppermute | solution.py:242
  9.6 5.7 %collective-permute-start.5 = (bf16[512,128]{1,0:T(8,128)(2,1)S(1)}, bf16[512,128]{1,0:T(8,128)(2,1)S(1)}, u32[]{:S(2)}, u32[]{:S(2)}) collective-permute-start(bf16[512,128]{1,0:T(8,128)(2,1)S(1)} %get-tuple-element.54), channel_id=1, source_target_pairs={{0,1},{1,0},{2,3},{3,2},{4,5},{5,4},{6,7},{7,6},{8,16},{9,17},{10,... | collective-permute-start | bytes 393224 | tf_op jit(solution)/shard_map/ppermute | solution.py:242
  15.9 3.2 %collective-permute-start.8 = (f32[4,512]{1,0:T(4,128)S(1)}, f32[4,512]{1,0:T(4,128)S(1)}, u32[]{:S(2)}, u32[]{:S(2)}) collective-permute-start(f32[4,512]{1,0:T(4,128)S(1)} %get-tuple-element.58.refs_0_), channel_id=1, source_target_pairs={{0,3},{1,2},{2,1},{3,0},{4,7},{5,6},{6,5},{7,4},{8,11},{9,10},{10,... | collective-permute-start | bytes 24584 | tf_op jit(solution)/shard_map/ppermute | solution.py:271
  16.0 3.7 %collective-permute-start.7 = (f32[4,512]{1,0:T(4,128)S(1)}, f32[4,512]{1,0:T(4,128)S(1)}, u32[]{:S(2)}, u32[]{:S(2)}) collective-permute-start(f32[4,512]{1,0:T(4,128)S(1)} %get-tuple-element.58.refs_0_), channel_id=1, source_target_pairs={{0,2},{1,3},{2,0},{3,1},{4,6},{5,7},{6,4},{7,5},{8,10},{9,11},{10,... | collective-permute-start | bytes 24584 | tf_op jit(solution)/shard_map/ppermute | solution.py:271
  17.6 2.2 %collective-permute-start.6 = (f32[4,512]{1,0:T(4,128)S(1)}, f32[4,512]{1,0:T(4,128)S(1)}, u32[]{:S(2)}, u32[]{:S(2)}) collective-permute-start(f32[4,512]{1,0:T(4,128)S(1)} %get-tuple-element.58.refs_0_), channel_id=1, source_target_pairs={{0,1},{1,0},{2,3},{3,2},{4,5},{5,4},{6,7},{7,6},{8,9},{9,8},{10,11... | collective-permute-start | bytes 24584 | tf_op jit(solution)/shard_map/ppermute | solution.py:271
  20.1 8.5 %collective-permute-start.10 = (bf16[512,128]{1,0:T(8,128)(2,1)S(1)}, bf16[512,128]{1,0:T(8,128)(2,1)S(1)}, u32[]{:S(2)}, u32[]{:S(2)}) collective-permute-start(bf16[512,128]{1,0:T(8,128)(2,1)S(1)} %get-tuple-element.62.d_ref), channel_id=1, source_target_pairs={{0,1},{1,0},{2,3},{3,2},{4,5},{5,4},{6,7},{7,6},{8,16},{9,17},{10,... | collective-permute-start | bytes 393224 | tf_op jit(solution)/shard_map/ppermute | solution.py:242
  20.5 8.1 %collective-permute-start.9 = (bf16[512,128]{1,0:T(8,128)(2,1)S(1)}, bf16[512,128]{1,0:T(8,128)(2,1)S(1)}, u32[]{:S(2)}, u32[]{:S(2)}) collective-permute-start(bf16[512,128]{1,0:T(8,128)(2,1)S(1)} %get-tuple-element.62.d_ref), channel_id=1, source_target_pairs={{0,8},{1,9},{2,10},{3,11},{4,12},{5,13},{6,14},{7,15},{8,0},{9,1},... | collective-permute-start | bytes 393224 | tf_op jit(solution)/shard_map/ppermute | solution.py:242
  23.9 5.8 %collective-permute-start.11 = (bf16[512,128]{1,0:T(8,128)(2,1)S(1)}, bf16[512,128]{1,0:T(8,128)(2,1)S(1)}, u32[]{:S(2)}, u32[]{:S(2)}) collective-permute-start(bf16[512,128]{1,0:T(8,128)(2,1)S(1)} %get-tuple-element.62.d_ref), channel_id=1, source_target_pairs={{0,28},{4,0},{8,4},{12,8},{16,12},{20,16},{24,20},{28,24},{1,29},{... | collective-permute-start | bytes 393224 | tf_op jit(solution)/shard_map/ppermute | solution.py:230

commit v6 on v5

--- a/solution.py
+++ b/solution.py
@@ -211,13 +211,44 @@
             gk_ref[here, at] = (key * factor if last else key).astype(gk_ref.dtype)
 
 
-def call(kernel, outs, *args, cost=None, scalars=0):
+def last_kernel(factor, v_ref, more_k_ref, more_v_ref, weight_ref, slope_ref, query_ref, d_ref, gk_ref, gv_ref,
+                key_out, value_out, sems):
+    rows, features = v_ref.shape
+    lanes, chunks = parts_of(rows, features)
+    moves = []
+
+    def leave(source, target, here):
+        move = pltpu.make_async_copy(source.at[here, :], target.at[here, :], sems.at[len(moves)])
+        move.start()
+        moves.append(move)
+
+    grads = {}
+    for chunk, here in chunks:
+        for head, at in lanes:
+            grad = dot(v_ref[here, at], d_ref[:, at], NT) * slope_ref[head, 0, here, :]
+            grads[chunk, head] = grad.astype(jnp.bfloat16)
+    for chunk, here in chunks:
+        for head, at in lanes:
+            value = more_v_ref[here, at] + dot(weight_ref[head, 0, here, :], d_ref[:, at], NN)
+            value_out[here, at] = value.astype(value_out.dtype)
+        leave(value_out, gv_ref, here)
+    for chunk, here in chunks:
+        for head, at in lanes:
+            key = more_k_ref[here, at] + dot(grads[chunk, head], query_ref[:, at], NN)
+            key_out[here, at] = (key * factor).astype(key_out.dtype)
+        leave(key_out, gk_ref, here)
+    for move in moves:
+        move.wait()
+
+
+def call(kernel, outs, *args, cost=None, scalars=0, place=pltpu.VMEM, scratch=()):
     vmem = pl.BlockSpec(memory_space=pltpu.VMEM)
     return pl.pallas_call(
         kernel,
         out_shape=[jax.ShapeDtypeStruct(shape, dtype) for shape, dtype in outs],
         in_specs=[pl.BlockSpec(memory_space=pltpu.SMEM)] * scalars + [vmem] * (len(args) - scalars),
-        out_specs=[vmem] * len(outs),
+        out_specs=[pl.BlockSpec(memory_space=place)] * len(outs),
+        scratch_shapes=list(scratch),
         cost_estimate=cost,
         compiler_params=pltpu.CompilerParams(vmem_limit_bytes=VMEM_LIMIT),
     )(*args)
@@ -328,14 +359,20 @@
         own_slopes, own_weights_t, own_slopes_t, slopes, *keys, *values,
     )
     sums = [near_key, near_value]
-    for offset in reversed(steps):
+    for offset in range(REACH, 1, -1):
         sums = call(
             functools.partial(far_kernel, factor, offset),
-            [(block, half if offset == 1 else full)] * 2,
+            [(block, full)] * 2,
             flags[offset - 1], value_vectors, *sums, weights_t, slopes_t, later[offset - 1], *deltas[offset - 1],
             scalars=1,
         )
-    grad_keys, grad_values = sums
+    copies = 2 * (rows_dev // chunk_of(rows_dev))
+    grad_keys, grad_values = call(
+        functools.partial(last_kernel, factor),
+        [(block, half)] * 2,
+        value_vectors, *sums, weights_t, slopes_t, later[0], deltas[0][0],
+        place=pl.ANY, scratch=[pltpu.VMEM(block, half)] * 2 + [pltpu.SemaphoreType.DMA((copies,))],
+    )
     return (layer_out, grad_queries, grad_keys, grad_values, grad_gating)
 
 

time: 31.2 us -> 31.1 us (level)
  no operation moved by 1% of the time
where the time goes in v6:
time: 31.1 us; the launch traced here: 30.9 us
  starting transfers between devices  16.4 us (53%)
  Pallas kernels  8.02 us (26%)
  waiting for transfers between devices  5.56 us (18%)
  between operations  0.86 us (3%)
    pallas_call x11, Pallas kernels, call(): pl.pallas_call(kernel, out_shape=[jax.ShapeDtypeStruct(shape, dtype) for...  8.02 us
    ppermute x6, starting transfers between devices, trade(): return lax.ppermute(value, ('rows', 'heads'), pairs)  7.32 us
    ppermute x3, starting transfers between devices, shift(): return lax.ppermute(value, axis, pairs)  7.2 us
    ppermute x3, waiting for transfers between devices, shift(): return lax.ppermute(value, axis, pairs)  4.61 us
    ppermute x3, starting transfers between devices, meet(): lax.ppermute(value, axis, [(source, source ^ step) for source in range(co...  1.92 us
    ppermute x3, waiting for transfers between devices, meet(): lax.ppermute(value, axis, [(source, source ^ step) for source in range(co...  0.94 us
  transfers between devices with their start and end apart: 12, of which 5 were waited for; matrix products, arithmetic and copies ran while one was open for 0% of the time, Pallas kernels for 19%

profile of v6, /device:TPU:0, one launch (start us, length us, event | category | flops | bytes accessed | tf_op | source)
XLA Modules:
  0.0 30.9 jit_solution(15976729085956062757)
XLA Ops:
  0.6 0.0 copy-start.2
  0.6 0.0 copy-start
  0.7 0.0 copy-start.1
  0.7 0.0 copy-start.5
  0.7 0.0 copy-start.4
  0.7 0.0 copy-start.3
  0.7 3.1 %collective-permute-start.1 = (bf16[512,128]{1,0:T(8,128)(2,1)}, bf16[512,128]{1,0:T(8,128)(2,1)S(1)}, u32[]{:S(2)}, u32[]{:S(2)}) collective-permute-start(bf16[512,128]{1,0:T(8,128)(2,1)} %k_ref.3), channel_id=1, source_target_pairs={{0,8},{4,12},{8,16},{12,20},{16,24},{20,28},{24,0},{28,4},{1,9},{5... | collective-permute-start | bytes 393224 | tf_op jit(solution)/shard_map/ppermute | solution.py:261
  3.8 1.5 %collective-permute-start = (bf16[512,128]{1,0:T(8,128)(2,1)}, bf16[512,128]{1,0:T(8,128)(2,1)S(1)}, u32[]{:S(2)}, u32[]{:S(2)}) collective-permute-start(bf16[512,128]{1,0:T(8,128)(2,1)} %k_ref.3), channel_id=1, source_target_pairs={{0,4},{4,8},{8,12},{12,16},{16,20},{20,24},{24,28},{28,0},{1,5},{5... | collective-permute-start | bytes 393224 | tf_op jit(solution)/shard_map/ppermute | solution.py:261
  5.3 0.0 copy-done
  5.4 0.0 copy-done.1
  5.4 0.1 shard_map.105
  5.4 1.6 %collective-permute-start.2 = (bf16[512,128]{1,0:T(8,128)(2,1)S(1)}, bf16[512,128]{1,0:T(8,128)(2,1)S(1)}, u32[]{:S(2)}, u32[]{:S(2)}) collective-permute-start(bf16[512,128]{1,0:T(8,128)(2,1)S(1)} %get-tuple-element.51), channel_id=1, source_target_pairs={{0,4},{1,5},{2,6},{3,7},{4,0},{5,1},{6,2},{7,3},{8,12},{9,13},{10,... | collective-permute-start | bytes 393224 | tf_op jit(solution)/shard_map/ppermute | solution.py:273
  7.0 0.0 collective-permute-start.3
  7.0 2.0 %collective-permute-start.4 = (bf16[512,128]{1,0:T(8,128)(2,1)S(1)}, bf16[512,128]{1,0:T(8,128)(2,1)S(1)}, u32[]{:S(2)}, u32[]{:S(2)}) collective-permute-start(bf16[512,128]{1,0:T(8,128)(2,1)S(1)} %get-tuple-element.53), channel_id=1, source_target_pairs={{0,8},{1,9},{2,10},{3,11},{4,12},{5,13},{6,14},{7,15},{8,0},{9,1},... | collective-permute-start | bytes 393224 | tf_op jit(solution)/shard_map/ppermute | solution.py:273
  9.0 0.6 %collective-permute-done.1.refs_1_ = bf16[512,128]{1,0:T(8,128)(2,1)S(1)} collective-permute-done((bf16[512,128]{1,0:T(8,128)(2,1)}, bf16[512,128]{1,0:T(8,128)(2,1)S(1)}, u32[]{:S(2)}, u32[]{:S(2)}) %collective-permute-start.1) | collective-permute-done | bytes 131104 | tf_op jit(solution)/shard_map/ppermute | solution.py:261
  9.6 0.0 collective-permute-start.5
  9.6 0.0 copy-done.5
  9.6 0.2 shard_map.102
  9.8 0.0 copy-done.2
  9.8 0.0 copy-done.4
  9.8 0.0 copy-done.3
  9.8 0.9 %shard_map.103 = (bf16[1,512,512]{2,1,0:T(8,128)(2,1)S(1)}, f32[1,512,512]{2,1,0:T(8,128)S(1)}, bf16[1,512,512]{2,1,0:T(8,128)(2,1)S(1)}, f32[1,512,512]{2,1,0:T...) custom-call(f32[512,128]{1,0:T(8,128)S(1)} %shard_map.101.order_ref, ...), custom_call_target="tpu_custom_call" | custom-call | tf_op jit(solution)/shard_map/pallas_call | solution.py:246
  10.8 3.6 %collective-permute-done.refs_0_ = bf16[512,128]{1,0:T(8,128)(2,1)S(1)} collective-permute-done((bf16[512,128]{1,0:T(8,128)(2,1)}, bf16[512,128]{1,0:T(8,128)(2,1)S(1)}, u32[]{:S(2)}, u32[]{:S(2)}) %collective-permute-start) | collective-permute-done | bytes 131104 | tf_op jit(solution)/shard_map/ppermute | solution.py:261
  14.3 0.9 %shard_map.104 = (bf16[1,2,512,512]{3,2,1,0:T(8,128)(2,1)S(1)}, f32[1,2,512,512]{3,2,1,0:T(8,128)S(1)}) custom-call(f32[512,128]{1,0:T(8,128)S(1)} %get-tuple-element.44.start_ref, bf16[512,128]{1,0:T(8,128)(2,1)S(1)} %copy-done.1, bf16[512,128]{1,0:T(8,128)(2,1)S(1)} %collective-permute-done.refs_0_, bf16[512,128]{1,0:T(8,128)(2,1)S(1)} %collective-permute-done.1.refs_1_), custom_call_target="tpu_custom_call" | custom-call | tf_op jit(solution)/shard_map/pallas_call | solution.py:246
  15.2 0.0 collective-permute-done.2.refs_7_.refs_4_
  15.2 0.0 collective-permute-done.3.refs_8_.refs_5_
  15.3 0.0 collective-permute-done.4.refs_9_.refs_6_
  15.3 0.0 collective-permute-done.5.refs_10_.refs_7_
  15.3 0.7 %shard_map.106 = (f32[512,128]{1,0:T(8,128)S(1)}, f32[4,512]{1,0:T(4,128)S(1)}, bf16[512,128]{1,0:T(8,128)(2,1)S(1)}, bf16[512,128]{1,0:T(8,128)(2,1)S(1)}) custom-call(s32[1]{0:T(128)} %bitcast.refs_0_, s32[1]{0:T(128)} %bitcast.1.refs_1_.flag_ref, bf16[1,512,512]{2,1,0:T(8,128)(2,1)S(1)} %get-tuple-element.46.refs_2_, ...), custom_call_target="tpu_custom_call" | custom-call | tf_op jit(solution)/shard_map/pallas_call | solution.py:246
  15.9 0.1 collective-permute-start.8
  16.0 1.6 %collective-permute-start.7 = (f32[4,512]{1,0:T(4,128)S(1)}, f32[4,512]{1,0:T(4,128)S(1)}, u32[]{:S(2)}, u32[]{:S(2)}) collective-permute-start(f32[4,512]{1,0:T(4,128)S(1)} %get-tuple-element.58.refs_0_), channel_id=1, source_target_pairs={{0,2},{1,3},{2,0},{3,1},{4,6},{5,7},{6,4},{7,5},{8,10},{9,11},{10,... | collective-permute-start | bytes 24584 | tf_op jit(solution)/shard_map/ppermute | solution.py:302
  17.6 0.3 collective-permute-start.6
  17.9 0.9 %shard_map.107 = (bf16[1,2,512,512]{3,2,1,0:T(8,128)(2,1)S(1)}, f32[1,2,512,512]{3,2,1,0:T(8,128)S(1)}, bf16[512,128]{1,0:T(8,128)(2,1)S(1)}, bf16[512,128]{1,0:T(8,128)(2,1)S(1)}) custom-call(s32[1]{0:T(128)} %bitcast.refs_0_, s32[1]{0:T(128)} %bitcast.1.refs_1_.flag_ref, f32[512,128]{1,0:T(8,128)S(1)} %get-tuple-element.45.last_ref.refs_2_, ...), custom_call_target="tpu_custom_call" | custom-call | tf_op jit(solution)/shard_map/pallas_call | solution.py:246
  18.8 0.3 %collective-permute-done.8.refs_3_ = f32[4,512]{1,0:T(4,128)S(1)} collective-permute-done((f32[4,512]{1,0:T(4,128)S(1)}, f32[4,512]{1,0:T(4,128)S(1)}, u32[]{:S(2)}, u32[]{:S(2)}) %collective-permute-start.8) | collective-permute-done | bytes 8224 | tf_op jit(solution)/shard_map/ppermute | solution.py:302
  19.1 0.6 %collective-permute-done.7.refs_2_ = f32[4,512]{1,0:T(4,128)S(1)} collective-permute-done((f32[4,512]{1,0:T(4,128)S(1)}, f32[4,512]{1,0:T(4,128)S(1)}, u32[]{:S(2)}, u32[]{:S(2)}) %collective-permute-start.7) | collective-permute-done | bytes 8224 | tf_op jit(solution)/shard_map/ppermute | solution.py:302
  19.7 0.0 collective-permute-done.6.refs_1_
  19.7 0.4 %shard_map.108 = (f32[512,128]{1,0:T(8,128)S(1)}, bf16[512,128]{1,0:T(8,128)(2,1)S(1)}) custom-call(f32[512,128]{1,0:T(8,128)S(1)} %get-tuple-element.55.att_ref, f32[512,128]{1,0:T(8,128)S(1)} %get-tuple-element.47.refs_3_.scaled_ref, f32[4,512]{1,0:T(4,128)S(1)} %get-tuple-element.58.refs_0_, f32[4,512]{1,0:T(4,128)S(1)} %collective-permute-done.6.refs_1_, ...), custom_call_target="tpu_custom_call" | custom-call | tf_op jit(solution)/shard_map/pallas_call | solution.py:246
  20.1 0.4 %collective-permute-start.10 = (bf16[512,128]{1,0:T(8,128)(2,1)S(1)}, bf16[512,128]{1,0:T(8,128)(2,1)S(1)}, u32[]{:S(2)}, u32[]{:S(2)}) collective-permute-start(bf16[512,128]{1,0:T(8,128)(2,1)S(1)} %get-tuple-element.62.d_ref), channel_id=1, source_target_pairs={{0,1},{1,0},{2,3},{3,2},{4,5},{5,4},{6,7},{7,6},{8,16},{9,17},{10,... | collective-permute-start | bytes 393224 | tf_op jit(solution)/shard_map/ppermute | solution.py:273
  20.5 3.3 %collective-permute-start.9 = (bf16[512,128]{1,0:T(8,128)(2,1)S(1)}, bf16[512,128]{1,0:T(8,128)(2,1)S(1)}, u32[]{:S(2)}, u32[]{:S(2)}) collective-permute-start(bf16[512,128]{1,0:T(8,128)(2,1)S(1)} %get-tuple-element.62.d_ref), channel_id=1, source_target_pairs={{0,8},{1,9},{2,10},{3,11},{4,12},{5,13},{6,14},{7,15},{8,0},{9,1},... | collective-permute-start | bytes 393224 | tf_op jit(solution)/shard_map/ppermute | solution.py:273
  23.9 2.6 %collective-permute-start.11 = (bf16[512,128]{1,0:T(8,128)(2,1)S(1)}, bf16[512,128]{1,0:T(8,128)(2,1)S(1)}, u32[]{:S(2)}, u32[]{:S(2)}) collective-permute-start(bf16[512,128]{1,0:T(8,128)(2,1)S(1)} %get-tuple-element.62.d_ref), channel_id=1, source_target_pairs={{0,28},{4,0},{8,4},{12,8},{16,12},{20,16},{24,20},{28,24},{1,29},{... | collective-permute-start | bytes 393224 | tf_op jit(solution)/shard_map/ppermute | solution.py:261
  26.5 2.1 %shard_map.109 = (bf16[512,128]{1,0:T(8,128)(2,1)}, f32[512,128]{1,0:T(8,128)S(1)}, f32[512,128]{1,0:T(8,128)S(1)}, bf16[512,128]{1,0:T(8,128)(2,1)}, bf16[512,128]{1,0:T(8,128)(2,1)}) custom-call(bf16[512,128]{1,0:T(8,128)(2,1)S(1)} %copy-done.1, bf16[512,128]{1,0:T(8,128)(2,1)S(1)} %copy-done.2, bf16[512,128]{1,0:T(8,128)(2,1)S(1)} %copy-done, ...), custom_call_target="tpu_custom_call" | custom-call | tf_op jit(solution)/shard_map/pallas_call | solution.py:246
  28.6 0.0 collective-permute-done.10.second_ref
  28.6 0.0 collective-permute-done.9.first_ref
  28.6 0.6 %shard_map.110 = (f32[512,128]{1,0:T(8,128)S(1)}, f32[512,128]{1,0:T(8,128)S(1)}) custom-call(s32[1]{0:T(128)} %bitcast.1.refs_1_.flag_ref, bf16[512,128]{1,0:T(8,128)(2,1)S(1)} %copy-done, f32[512,128]{1,0:T(8,128)S(1)} %get-tuple-element.72.near_k_ref, f32[512,128]{1,0:T(8,128)S(1)} %get-tuple-element.73.near_v_ref, ...), custom_call_target="tpu_custom_call" | custom-call | tf_op jit(solution)/shard_map/pallas_call | solution.py:246
  29.3 0.4 %collective-permute-done.11.d_ref = bf16[512,128]{1,0:T(8,128)(2,1)S(1)} collective-permute-done((bf16[512,128]{1,0:T(8,128)(2,1)S(1)}, bf16[512,128]{1,0:T(8,128)(2,1)S(1)}, u32[]{:S(2)}, u32[]{:S(2)}) %collective-permute-start.11) | collective-permute-done | bytes 131104 | tf_op jit(solution)/shard_map/ppermute | solution.py:261
  29.7 1.2 %shard_map.111 = (bf16[512,128]{1,0:T(8,128)(2,1)}, bf16[512,128]{1,0:T(8,128)(2,1)}) custom-call(bf16[512,128]{1,0:T(8,128)(2,1)S(1)} %copy-done, f32[512,128]{1,0:T(8,128)S(1)} %get-tuple-element.77.more_k_ref, f32[512,128]{1,0:T(8,128)S(1)} %get-tuple-element.78.more_v_ref, bf16[1,2,512,512]{3,2,1,0:T(8,128)(2,1)S(1)} %get-tuple-element.74.weight_ref, ...), custom_call_target="tpu_custom_call" | custom-call | tf_op jit(solution)/shard_map/pallas_call | solution.py:246
  (2 shorter events, 0.0 us)
Async XLA Ops:
  0.6 9.2 %copy-start.2 = (bf16[512,128]{1,0:T(8,128)(2,1)S(1)}, bf16[512,128]{1,0:T(8,128)(2,1)}, u32[]{:S(2)}) copy-start(bf16[512,128]{1,0:T(8,128)(2,1)} %k_ref.3) | copy-start | bytes 393220
  0.6 4.7 %copy-start = (bf16[512,128]{1,0:T(8,128)(2,1)S(1)}, bf16[512,128]{1,0:T(8,128)(2,1)}, u32[]{:S(2)}) copy-start(bf16[512,128]{1,0:T(8,128)(2,1)} %v_ref.5) | copy-start | bytes 393220
  0.7 4.7 %copy-start.1 = (bf16[512,128]{1,0:T(8,128)(2,1)S(1)}, bf16[512,128]{1,0:T(8,128)(2,1)}, u32[]{:S(2)}) copy-start(bf16[512,128]{1,0:T(8,128)(2,1)} %q_ref.5) | copy-start | bytes 393220
  0.7 8.9 %copy-start.5 = (s32[2,512]{1,0:T(2,128)S(1)}, s32[2,512]{1,0:T(2,128)}, u32[]{:S(2)}) copy-start(s32[2,512]{1,0:T(2,128)} %param.10) | copy-start | bytes 12292
  0.7 9.2 %copy-start.4 = (bf16[512,128]{1,0:T(8,128)(2,1)S(1)}, bf16[512,128]{1,0:T(8,128)(2,1)}, u32[]{:S(2)}) copy-start(bf16[512,128]{1,0:T(8,128)(2,1)} %up_ref.3) | copy-start | bytes 393220
  0.7 9.2 %copy-start.3 = (bf16[512,128]{1,0:T(8,128)(2,1)S(1)}, bf16[512,128]{1,0:T(8,128)(2,1)}, u32[]{:S(2)}) copy-start(bf16[512,128]{1,0:T(8,128)(2,1)} %gate_ref.3) | copy-start | bytes 393220
  0.7 8.9 %collective-permute-start.1 = (bf16[512,128]{1,0:T(8,128)(2,1)}, bf16[512,128]{1,0:T(8,128)(2,1)S(1)}, u32[]{:S(2)}, u32[]{:S(2)}) collective-permute-start(bf16[512,128]{1,0:T(8,128)(2,1)} %k_ref.3), channel_id=1, source_target_pairs={{0,8},{4,12},{8,16},{12,20},{16,24},{20,28},{24,0},{28,4},{1,9},{5... | collective-permute-start | bytes 393224 | tf_op jit(solution)/shard_map/ppermute | solution.py:261
  3.8 10.6 %collective-permute-start = (bf16[512,128]{1,0:T(8,128)(2,1)}, bf16[512,128]{1,0:T(8,128)(2,1)S(1)}, u32[]{:S(2)}, u32[]{:S(2)}) collective-permute-start(bf16[512,128]{1,0:T(8,128)(2,1)} %k_ref.3), channel_id=1, source_target_pairs={{0,4},{4,8},{8,12},{12,16},{16,20},{20,24},{24,28},{28,0},{1,5},{5... | collective-permute-start | bytes 393224 | tf_op jit(solution)/shard_map/ppermute | solution.py:261
  5.4 9.8 %collective-permute-start.2 = (bf16[512,128]{1,0:T(8,128)(2,1)S(1)}, bf16[512,128]{1,0:T(8,128)(2,1)S(1)}, u32[]{:S(2)}, u32[]{:S(2)}) collective-permute-start(bf16[512,128]{1,0:T(8,128)(2,1)S(1)} %get-tuple-element.51), channel_id=1, source_target_pairs={{0,4},{1,5},{2,6},{3,7},{4,0},{5,1},{6,2},{7,3},{8,12},{9,13},{10,... | collective-permute-start | bytes 393224 | tf_op jit(solution)/shard_map/ppermute | solution.py:273
  7.0 8.2 %collective-permute-start.3 = (bf16[512,128]{1,0:T(8,128)(2,1)S(1)}, bf16[512,128]{1,0:T(8,128)(2,1)S(1)}, u32[]{:S(2)}, u32[]{:S(2)}) collective-permute-start(bf16[512,128]{1,0:T(8,128)(2,1)S(1)} %get-tuple-element.52), channel_id=1, source_target_pairs={{0,1},{1,0},{2,3},{3,2},{4,8},{5,9},{6,10},{7,11},{8,4},{9,5},{10,... | collective-permute-start | bytes 393224 | tf_op jit(solution)/shard_map/ppermute | solution.py:273
  7.0 8.2 %collective-permute-start.4 = (bf16[512,128]{1,0:T(8,128)(2,1)S(1)}, bf16[512,128]{1,0:T(8,128)(2,1)S(1)}, u32[]{:S(2)}, u32[]{:S(2)}) collective-permute-start(bf16[512,128]{1,0:T(8,128)(2,1)S(1)} %get-tuple-element.53), channel_id=1, source_target_pairs={{0,8},{1,9},{2,10},{3,11},{4,12},{5,13},{6,14},{7,15},{8,0},{9,1},... | collective-permute-start | bytes 393224 | tf_op jit(solution)/shard_map/ppermute | solution.py:273
  9.6 5.7 %collective-permute-start.5 = (bf16[512,128]{1,0:T(8,128)(2,1)S(1)}, bf16[512,128]{1,0:T(8,128)(2,1)S(1)}, u32[]{:S(2)}, u32[]{:S(2)}) collective-permute-start(bf16[512,128]{1,0:T(8,128)(2,1)S(1)} %get-tuple-element.54), channel_id=1, source_target_pairs={{0,1},{1,0},{2,3},{3,2},{4,5},{5,4},{6,7},{7,6},{8,16},{9,17},{10,... | collective-permute-start | bytes 393224 | tf_op jit(solution)/shard_map/ppermute | solution.py:273
  15.9 3.2 %collective-permute-start.8 = (f32[4,512]{1,0:T(4,128)S(1)}, f32[4,512]{1,0:T(4,128)S(1)}, u32[]{:S(2)}, u32[]{:S(2)}) collective-permute-start(f32[4,512]{1,0:T(4,128)S(1)} %get-tuple-element.58.refs_0_), channel_id=1, source_target_pairs={{0,3},{1,2},{2,1},{3,0},{4,7},{5,6},{6,5},{7,4},{8,11},{9,10},{10,... | collective-permute-start | bytes 24584 | tf_op jit(solution)/shard_map/ppermute | solution.py:302
  16.0 3.7 %collective-permute-start.7 = (f32[4,512]{1,0:T(4,128)S(1)}, f32[4,512]{1,0:T(4,128)S(1)}, u32[]{:S(2)}, u32[]{:S(2)}) collective-permute-start(f32[4,512]{1,0:T(4,128)S(1)} %get-tuple-element.58.refs_0_), channel_id=1, source_target_pairs={{0,2},{1,3},{2,0},{3,1},{4,6},{5,7},{6,4},{7,5},{8,10},{9,11},{10,... | collective-permute-start | bytes 24584 | tf_op jit(solution)/shard_map/ppermute | solution.py:302
  17.6 2.2 %collective-permute-start.6 = (f32[4,512]{1,0:T(4,128)S(1)}, f32[4,512]{1,0:T(4,128)S(1)}, u32[]{:S(2)}, u32[]{:S(2)}) collective-permute-start(f32[4,512]{1,0:T(4,128)S(1)} %get-tuple-element.58.refs_0_), channel_id=1, source_target_pairs={{0,1},{1,0},{2,3},{3,2},{4,5},{5,4},{6,7},{7,6},{8,9},{9,8},{10,11... | collective-permute-start | bytes 24584 | tf_op jit(solution)/shard_map/ppermute | solution.py:302
  20.1 8.5 %collective-permute-start.10 = (bf16[512,128]{1,0:T(8,128)(2,1)S(1)}, bf16[512,128]{1,0:T(8,128)(2,1)S(1)}, u32[]{:S(2)}, u32[]{:S(2)}) collective-permute-start(bf16[512,128]{1,0:T(8,128)(2,1)S(1)} %get-tuple-element.62.d_ref), channel_id=1, source_target_pairs={{0,1},{1,0},{2,3},{3,2},{4,5},{5,4},{6,7},{7,6},{8,16},{9,17},{10,... | collective-permute-start | bytes 393224 | tf_op jit(solution)/shard_map/ppermute | solution.py:273
  20.5 8.1 %collective-permute-start.9 = (bf16[512,128]{1,0:T(8,128)(2,1)S(1)}, bf16[512,128]{1,0:T(8,128)(2,1)S(1)}, u32[]{:S(2)}, u32[]{:S(2)}) collective-permute-start(bf16[512,128]{1,0:T(8,128)(2,1)S(1)} %get-tuple-element.62.d_ref), channel_id=1, source_target_pairs={{0,8},{1,9},{2,10},{3,11},{4,12},{5,13},{6,14},{7,15},{8,0},{9,1},... | collective-permute-start | bytes 393224 | tf_op jit(solution)/shard_map/ppermute | solution.py:273
  23.9 5.8 %collective-permute-start.11 = (bf16[512,128]{1,0:T(8,128)(2,1)S(1)}, bf16[512,128]{1,0:T(8,128)(2,1)S(1)}, u32[]{:S(2)}, u32[]{:S(2)}) collective-permute-start(bf16[512,128]{1,0:T(8,128)(2,1)S(1)} %get-tuple-element.62.d_ref), channel_id=1, source_target_pairs={{0,28},{4,0},{8,4},{12,8},{16,12},{20,16},{24,20},{28,24},{1,29},{... | collective-permute-start | bytes 393224 | tf_op jit(solution)/shard_map/ppermute | solution.py:261

commit v7 on v6

--- a/solution.py
+++ b/solution.py
@@ -222,16 +222,16 @@
         move.start()
         moves.append(move)
 
+    for chunk, here in chunks:
+        for head, at in lanes:
+            value = more_v_ref[here, at] + dot(weight_ref[head, 0, here, :], d_ref[:, at], NN)
+            value_out[here, at] = value.astype(value_out.dtype)
+        leave(value_out, gv_ref, here)
     grads = {}
     for chunk, here in chunks:
         for head, at in lanes:
             grad = dot(v_ref[here, at], d_ref[:, at], NT) * slope_ref[head, 0, here, :]
             grads[chunk, head] = grad.astype(jnp.bfloat16)
-    for chunk, here in chunks:
-        for head, at in lanes:
-            value = more_v_ref[here, at] + dot(weight_ref[head, 0, here, :], d_ref[:, at], NN)
-            value_out[here, at] = value.astype(value_out.dtype)
-        leave(value_out, gv_ref, here)
     for chunk, here in chunks:
         for head, at in lanes:
             key = more_k_ref[here, at] + dot(grads[chunk, head], query_ref[:, at], NN)

time: 31.1 us -> 31.1 us (level)
  no operation moved by 1% of the time
where the time goes in v7:
time: 31.1 us; the launch traced here: 30.9 us
  starting transfers between devices  16.4 us (53%)
  Pallas kernels  8.01 us (26%)
  waiting for transfers between devices  5.56 us (18%)
  between operations  0.86 us (3%)
    pallas_call x11, Pallas kernels, call(): pl.pallas_call(kernel, out_shape=[jax.ShapeDtypeStruct(shape, dtype) for...  8.01 us
    ppermute x6, starting transfers between devices, trade(): return lax.ppermute(value, ('rows', 'heads'), pairs)  7.32 us
    ppermute x3, starting transfers between devices, shift(): return lax.ppermute(value, axis, pairs)  7.2 us
    ppermute x3, waiting for transfers between devices, shift(): return lax.ppermute(value, axis, pairs)  4.61 us
    ppermute x3, starting transfers between devices, meet(): lax.ppermute(value, axis, [(source, source ^ step) for source in range(co...  1.92 us
    ppermute x3, waiting for transfers between devices, meet(): lax.ppermute(value, axis, [(source, source ^ step) for source in range(co...  0.94 us
  transfers between devices with their start and end apart: 12, of which 5 were waited for; matrix products, arithmetic and copies ran while one was open for 0% of the time, Pallas kernels for 19%

profile of v7, /device:TPU:0, one launch (start us, length us, event | category | flops | bytes accessed | tf_op | source)
XLA Modules:
  0.0 30.9 jit_solution(3816893323993893218)
XLA Ops:
  0.6 0.0 copy-start.2
  0.6 0.0 copy-start
  0.7 0.0 copy-start.1
  0.7 0.0 copy-start.5
  0.7 0.0 copy-start.4
  0.7 0.0 copy-start.3
  0.7 3.1 %collective-permute-start.1 = (bf16[512,128]{1,0:T(8,128)(2,1)}, bf16[512,128]{1,0:T(8,128)(2,1)S(1)}, u32[]{:S(2)}, u32[]{:S(2)}) collective-permute-start(bf16[512,128]{1,0:T(8,128)(2,1)} %k_ref.3), channel_id=1, source_target_pairs={{0,8},{4,12},{8,16},{12,20},{16,24},{20,28},{24,0},{28,4},{1,9},{5... | collective-permute-start | bytes 393224 | tf_op jit(solution)/shard_map/ppermute | solution.py:261
  3.8 1.5 %collective-permute-start = (bf16[512,128]{1,0:T(8,128)(2,1)}, bf16[512,128]{1,0:T(8,128)(2,1)S(1)}, u32[]{:S(2)}, u32[]{:S(2)}) collective-permute-start(bf16[512,128]{1,0:T(8,128)(2,1)} %k_ref.3), channel_id=1, source_target_pairs={{0,4},{4,8},{8,12},{12,16},{16,20},{20,24},{24,28},{28,0},{1,5},{5... | collective-permute-start | bytes 393224 | tf_op jit(solution)/shard_map/ppermute | solution.py:261
  5.3 0.0 copy-done
  5.4 0.0 copy-done.1
  5.4 0.1 shard_map.105
  5.4 1.6 %collective-permute-start.2 = (bf16[512,128]{1,0:T(8,128)(2,1)S(1)}, bf16[512,128]{1,0:T(8,128)(2,1)S(1)}, u32[]{:S(2)}, u32[]{:S(2)}) collective-permute-start(bf16[512,128]{1,0:T(8,128)(2,1)S(1)} %get-tuple-element.51), channel_id=1, source_target_pairs={{0,4},{1,5},{2,6},{3,7},{4,0},{5,1},{6,2},{7,3},{8,12},{9,13},{10,... | collective-permute-start | bytes 393224 | tf_op jit(solution)/shard_map/ppermute | solution.py:273
  7.0 0.0 collective-permute-start.3
  7.0 2.0 %collective-permute-start.4 = (bf16[512,128]{1,0:T(8,128)(2,1)S(1)}, bf16[512,128]{1,0:T(8,128)(2,1)S(1)}, u32[]{:S(2)}, u32[]{:S(2)}) collective-permute-start(bf16[512,128]{1,0:T(8,128)(2,1)S(1)} %get-tuple-element.53), channel_id=1, source_target_pairs={{0,8},{1,9},{2,10},{3,11},{4,12},{5,13},{6,14},{7,15},{8,0},{9,1},... | collective-permute-start | bytes 393224 | tf_op jit(solution)/shard_map/ppermute | solution.py:273
  9.0 0.6 %collective-permute-done.1.refs_1_ = bf16[512,128]{1,0:T(8,128)(2,1)S(1)} collective-permute-done((bf16[512,128]{1,0:T(8,128)(2,1)}, bf16[512,128]{1,0:T(8,128)(2,1)S(1)}, u32[]{:S(2)}, u32[]{:S(2)}) %collective-permute-start.1) | collective-permute-done | bytes 131104 | tf_op jit(solution)/shard_map/ppermute | solution.py:261
  9.6 0.0 collective-permute-start.5
  9.6 0.0 copy-done.5
  9.6 0.2 shard_map.102
  9.8 0.0 copy-done.2
  9.8 0.0 copy-done.4
  9.8 0.0 copy-done.3
  9.8 0.9 %shard_map.103 = (bf16[1,512,512]{2,1,0:T(8,128)(2,1)S(1)}, f32[1,512,512]{2,1,0:T(8,128)S(1)}, bf16[1,512,512]{2,1,0:T(8,128)(2,1)S(1)}, f32[1,512,512]{2,1,0:T...) custom-call(f32[512,128]{1,0:T(8,128)S(1)} %shard_map.101.order_ref, ...), custom_call_target="tpu_custom_call" | custom-call | tf_op jit(solution)/shard_map/pallas_call | solution.py:246
  10.8 3.6 %collective-permute-done.refs_0_ = bf16[512,128]{1,0:T(8,128)(2,1)S(1)} collective-permute-done((bf16[512,128]{1,0:T(8,128)(2,1)}, bf16[512,128]{1,0:T(8,128)(2,1)S(1)}, u32[]{:S(2)}, u32[]{:S(2)}) %collective-permute-start) | collective-permute-done | bytes 131104 | tf_op jit(solution)/shard_map/ppermute | solution.py:261
  14.3 0.9 %shard_map.104 = (bf16[1,2,512,512]{3,2,1,0:T(8,128)(2,1)S(1)}, f32[1,2,512,512]{3,2,1,0:T(8,128)S(1)}) custom-call(f32[512,128]{1,0:T(8,128)S(1)} %get-tuple-element.44.start_ref, bf16[512,128]{1,0:T(8,128)(2,1)S(1)} %copy-done.1, bf16[512,128]{1,0:T(8,128)(2,1)S(1)} %collective-permute-done.refs_0_, bf16[512,128]{1,0:T(8,128)(2,1)S(1)} %collective-permute-done.1.refs_1_), custom_call_target="tpu_custom_call" | custom-call | tf_op jit(solution)/shard_map/pallas_call | solution.py:246
  15.2 0.0 collective-permute-done.2.refs_7_.refs_4_
  15.2 0.0 collective-permute-done.3.refs_8_.refs_5_
  15.3 0.0 collective-permute-done.4.refs_9_.refs_6_
  15.3 0.0 collective-permute-done.5.refs_10_.refs_7_
  15.3 0.7 %shard_map.106 = (f32[512,128]{1,0:T(8,128)S(1)}, f32[4,512]{1,0:T(4,128)S(1)}, bf16[512,128]{1,0:T(8,128)(2,1)S(1)}, bf16[512,128]{1,0:T(8,128)(2,1)S(1)}) custom-call(s32[1]{0:T(128)} %bitcast.refs_0_, s32[1]{0:T(128)} %bitcast.1.refs_1_.flag_ref, bf16[1,512,512]{2,1,0:T(8,128)(2,1)S(1)} %get-tuple-element.46.refs_2_, ...), custom_call_target="tpu_custom_call" | custom-call | tf_op jit(solution)/shard_map/pallas_call | solution.py:246
  15.9 0.1 collective-permute-start.8
  16.0 1.6 %collective-permute-start.7 = (f32[4,512]{1,0:T(4,128)S(1)}, f32[4,512]{1,0:T(4,128)S(1)}, u32[]{:S(2)}, u32[]{:S(2)}) collective-permute-start(f32[4,512]{1,0:T(4,128)S(1)} %get-tuple-element.58.refs_0_), channel_id=1, source_target_pairs={{0,2},{1,3},{2,0},{3,1},{4,6},{5,7},{6,4},{7,5},{8,10},{9,11},{10,... | collective-permute-start | bytes 24584 | tf_op jit(solution)/shard_map/ppermute | solution.py:302
  17.6 0.3 collective-permute-start.6
  17.9 0.9 %shard_map.107 = (bf16[1,2,512,512]{3,2,1,0:T(8,128)(2,1)S(1)}, f32[1,2,512,512]{3,2,1,0:T(8,128)S(1)}, bf16[512,128]{1,0:T(8,128)(2,1)S(1)}, bf16[512,128]{1,0:T(8,128)(2,1)S(1)}) custom-call(s32[1]{0:T(128)} %bitcast.refs_0_, s32[1]{0:T(128)} %bitcast.1.refs_1_.flag_ref, f32[512,128]{1,0:T(8,128)S(1)} %get-tuple-element.45.last_ref.refs_2_, ...), custom_call_target="tpu_custom_call" | custom-call | tf_op jit(solution)/shard_map/pallas_call | solution.py:246
  18.8 0.3 %collective-permute-done.8.refs_3_ = f32[4,512]{1,0:T(4,128)S(1)} collective-permute-done((f32[4,512]{1,0:T(4,128)S(1)}, f32[4,512]{1,0:T(4,128)S(1)}, u32[]{:S(2)}, u32[]{:S(2)}) %collective-permute-start.8) | collective-permute-done | bytes 8224 | tf_op jit(solution)/shard_map/ppermute | solution.py:302
  19.1 0.6 %collective-permute-done.7.refs_2_ = f32[4,512]{1,0:T(4,128)S(1)} collective-permute-done((f32[4,512]{1,0:T(4,128)S(1)}, f32[4,512]{1,0:T(4,128)S(1)}, u32[]{:S(2)}, u32[]{:S(2)}) %collective-permute-start.7) | collective-permute-done | bytes 8224 | tf_op jit(solution)/shard_map/ppermute | solution.py:302
  19.7 0.0 collective-permute-done.6.refs_1_
  19.7 0.4 %shard_map.108 = (f32[512,128]{1,0:T(8,128)S(1)}, bf16[512,128]{1,0:T(8,128)(2,1)S(1)}) custom-call(f32[512,128]{1,0:T(8,128)S(1)} %get-tuple-element.55.att_ref, f32[512,128]{1,0:T(8,128)S(1)} %get-tuple-element.47.refs_3_.scaled_ref, f32[4,512]{1,0:T(4,128)S(1)} %get-tuple-element.58.refs_0_, f32[4,512]{1,0:T(4,128)S(1)} %collective-permute-done.6.refs_1_, ...), custom_call_target="tpu_custom_call" | custom-call | tf_op jit(solution)/shard_map/pallas_call | solution.py:246
  20.1 0.4 %collective-permute-start.10 = (bf16[512,128]{1,0:T(8,128)(2,1)S(1)}, bf16[512,128]{1,0:T(8,128)(2,1)S(1)}, u32[]{:S(2)}, u32[]{:S(2)}) collective-permute-start(bf16[512,128]{1,0:T(8,128)(2,1)S(1)} %get-tuple-element.62.d_ref), channel_id=1, source_target_pairs={{0,1},{1,0},{2,3},{3,2},{4,5},{5,4},{6,7},{7,6},{8,16},{9,17},{10,... | collective-permute-start | bytes 393224 | tf_op jit(solution)/shard_map/ppermute | solution.py:273
  20.5 3.3 %collective-permute-start.9 = (bf16[512,128]{1,0:T(8,128)(2,1)S(1)}, bf16[512,128]{1,0:T(8,128)(2,1)S(1)}, u32[]{:S(2)}, u32[]{:S(2)}) collective-permute-start(bf16[512,128]{1,0:T(8,128)(2,1)S(1)} %get-tuple-element.62.d_ref), channel_id=1, source_target_pairs={{0,8},{1,9},{2,10},{3,11},{4,12},{5,13},{6,14},{7,15},{8,0},{9,1},... | collective-permute-start | bytes 393224 | tf_op jit(solution)/shard_map/ppermute | solution.py:273
  23.9 2.6 %collective-permute-start.11 = (bf16[512,128]{1,0:T(8,128)(2,1)S(1)}, bf16[512,128]{1,0:T(8,128)(2,1)S(1)}, u32[]{:S(2)}, u32[]{:S(2)}) collective-permute-start(bf16[512,128]{1,0:T(8,128)(2,1)S(1)} %get-tuple-element.62.d_ref), channel_id=1, source_target_pairs={{0,28},{4,0},{8,4},{12,8},{16,12},{20,16},{24,20},{28,24},{1,29},{... | collective-permute-start | bytes 393224 | tf_op jit(solution)/shard_map/ppermute | solution.py:261
  26.5 2.1 %shard_map.109 = (bf16[512,128]{1,0:T(8,128)(2,1)}, f32[512,128]{1,0:T(8,128)S(1)}, f32[512,128]{1,0:T(8,128)S(1)}, bf16[512,128]{1,0:T(8,128)(2,1)}, bf16[512,128]{1,0:T(8,128)(2,1)}) custom-call(bf16[512,128]{1,0:T(8,128)(2,1)S(1)} %copy-done.1, bf16[512,128]{1,0:T(8,128)(2,1)S(1)} %copy-done.2, bf16[512,128]{1,0:T(8,128)(2,1)S(1)} %copy-done, ...), custom_call_target="tpu_custom_call" | custom-call | tf_op jit(solution)/shard_map/pallas_call | solution.py:246
  28.6 0.0 collective-permute-done.10.second_ref
  28.6 0.0 collective-permute-done.9.first_ref
  28.6 0.6 %shard_map.110 = (f32[512,128]{1,0:T(8,128)S(1)}, f32[512,128]{1,0:T(8,128)S(1)}) custom-call(s32[1]{0:T(128)} %bitcast.1.refs_1_.flag_ref, bf16[512,128]{1,0:T(8,128)(2,1)S(1)} %copy-done, f32[512,128]{1,0:T(8,128)S(1)} %get-tuple-element.72.near_k_ref, f32[512,128]{1,0:T(8,128)S(1)} %get-tuple-element.73.near_v_ref, ...), custom_call_target="tpu_custom_call" | custom-call | tf_op jit(solution)/shard_map/pallas_call | solution.py:246
  29.3 0.4 %collective-permute-done.11.d_ref = bf16[512,128]{1,0:T(8,128)(2,1)S(1)} collective-permute-done((bf16[512,128]{1,0:T(8,128)(2,1)S(1)}, bf16[512,128]{1,0:T(8,128)(2,1)S(1)}, u32[]{:S(2)}, u32[]{:S(2)}) %collective-permute-start.11) | collective-permute-done | bytes 131104 | tf_op jit(solution)/shard_map/ppermute | solution.py:261
  29.7 1.2 %shard_map.111 = (bf16[512,128]{1,0:T(8,128)(2,1)}, bf16[512,128]{1,0:T(8,128)(2,1)}) custom-call(bf16[512,128]{1,0:T(8,128)(2,1)S(1)} %copy-done, f32[512,128]{1,0:T(8,128)S(1)} %get-tuple-element.77.more_k_ref, f32[512,128]{1,0:T(8,128)S(1)} %get-tuple-element.78.more_v_ref, bf16[1,2,512,512]{3,2,1,0:T(8,128)(2,1)S(1)} %get-tuple-element.74.weight_ref, ...), custom_call_target="tpu_custom_call" | custom-call | tf_op jit(solution)/shard_map/pallas_call | solution.py:246
  (2 shorter events, 0.0 us)
Async XLA Ops:
  0.6 9.2 %copy-start.2 = (bf16[512,128]{1,0:T(8,128)(2,1)S(1)}, bf16[512,128]{1,0:T(8,128)(2,1)}, u32[]{:S(2)}) copy-start(bf16[512,128]{1,0:T(8,128)(2,1)} %k_ref.3) | copy-start | bytes 393220
  0.6 4.7 %copy-start = (bf16[512,128]{1,0:T(8,128)(2,1)S(1)}, bf16[512,128]{1,0:T(8,128)(2,1)}, u32[]{:S(2)}) copy-start(bf16[512,128]{1,0:T(8,128)(2,1)} %v_ref.5) | copy-start | bytes 393220
  0.7 4.7 %copy-start.1 = (bf16[512,128]{1,0:T(8,128)(2,1)S(1)}, bf16[512,128]{1,0:T(8,128)(2,1)}, u32[]{:S(2)}) copy-start(bf16[512,128]{1,0:T(8,128)(2,1)} %q_ref.5) | copy-start | bytes 393220
  0.7 8.9 %copy-start.5 = (s32[2,512]{1,0:T(2,128)S(1)}, s32[2,512]{1,0:T(2,128)}, u32[]{:S(2)}) copy-start(s32[2,512]{1,0:T(2,128)} %param.10) | copy-start | bytes 12292
  0.7 9.2 %copy-start.4 = (bf16[512,128]{1,0:T(8,128)(2,1)S(1)}, bf16[512,128]{1,0:T(8,128)(2,1)}, u32[]{:S(2)}) copy-start(bf16[512,128]{1,0:T(8,128)(2,1)} %up_ref.3) | copy-start | bytes 393220
  0.7 9.2 %copy-start.3 = (bf16[512,128]{1,0:T(8,128)(2,1)S(1)}, bf16[512,128]{1,0:T(8,128)(2,1)}, u32[]{:S(2)}) copy-start(bf16[512,128]{1,0:T(8,128)(2,1)} %gate_ref.3) | copy-start | bytes 393220
  0.7 8.9 %collective-permute-start.1 = (bf16[512,128]{1,0:T(8,128)(2,1)}, bf16[512,128]{1,0:T(8,128)(2,1)S(1)}, u32[]{:S(2)}, u32[]{:S(2)}) collective-permute-start(bf16[512,128]{1,0:T(8,128)(2,1)} %k_ref.3), channel_id=1, source_target_pairs={{0,8},{4,12},{8,16},{12,20},{16,24},{20,28},{24,0},{28,4},{1,9},{5... | collective-permute-start | bytes 393224 | tf_op jit(solution)/shard_map/ppermute | solution.py:261
  3.8 10.6 %collective-permute-start = (bf16[512,128]{1,0:T(8,128)(2,1)}, bf16[512,128]{1,0:T(8,128)(2,1)S(1)}, u32[]{:S(2)}, u32[]{:S(2)}) collective-permute-start(bf16[512,128]{1,0:T(8,128)(2,1)} %k_ref.3), channel_id=1, source_target_pairs={{0,4},{4,8},{8,12},{12,16},{16,20},{20,24},{24,28},{28,0},{1,5},{5... | collective-permute-start | bytes 393224 | tf_op jit(solution)/shard_map/ppermute | solution.py:261
  5.4 9.8 %collective-permute-start.2 = (bf16[512,128]{1,0:T(8,128)(2,1)S(1)}, bf16[512,128]{1,0:T(8,128)(2,1)S(1)}, u32[]{:S(2)}, u32[]{:S(2)}) collective-permute-start(bf16[512,128]{1,0:T(8,128)(2,1)S(1)} %get-tuple-element.51), channel_id=1, source_target_pairs={{0,4},{1,5},{2,6},{3,7},{4,0},{5,1},{6,2},{7,3},{8,12},{9,13},{10,... | collective-permute-start | bytes 393224 | tf_op jit(solution)/shard_map/ppermute | solution.py:273
  7.0 8.2 %collective-permute-start.3 = (bf16[512,128]{1,0:T(8,128)(2,1)S(1)}, bf16[512,128]{1,0:T(8,128)(2,1)S(1)}, u32[]{:S(2)}, u32[]{:S(2)}) collective-permute-start(bf16[512,128]{1,0:T(8,128)(2,1)S(1)} %get-tuple-element.52), channel_id=1, source_target_pairs={{0,1},{1,0},{2,3},{3,2},{4,8},{5,9},{6,10},{7,11},{8,4},{9,5},{10,... | collective-permute-start | bytes 393224 | tf_op jit(solution)/shard_map/ppermute | solution.py:273
  7.0 8.2 %collective-permute-start.4 = (bf16[512,128]{1,0:T(8,128)(2,1)S(1)}, bf16[512,128]{1,0:T(8,128)(2,1)S(1)}, u32[]{:S(2)}, u32[]{:S(2)}) collective-permute-start(bf16[512,128]{1,0:T(8,128)(2,1)S(1)} %get-tuple-element.53), channel_id=1, source_target_pairs={{0,8},{1,9},{2,10},{3,11},{4,12},{5,13},{6,14},{7,15},{8,0},{9,1},... | collective-permute-start | bytes 393224 | tf_op jit(solution)/shard_map/ppermute | solution.py:273
  9.6 5.7 %collective-permute-start.5 = (bf16[512,128]{1,0:T(8,128)(2,1)S(1)}, bf16[512,128]{1,0:T(8,128)(2,1)S(1)}, u32[]{:S(2)}, u32[]{:S(2)}) collective-permute-start(bf16[512,128]{1,0:T(8,128)(2,1)S(1)} %get-tuple-element.54), channel_id=1, source_target_pairs={{0,1},{1,0},{2,3},{3,2},{4,5},{5,4},{6,7},{7,6},{8,16},{9,17},{10,... | collective-permute-start | bytes 393224 | tf_op jit(solution)/shard_map/ppermute | solution.py:273
  15.9 3.2 %collective-permute-start.8 = (f32[4,512]{1,0:T(4,128)S(1)}, f32[4,512]{1,0:T(4,128)S(1)}, u32[]{:S(2)}, u32[]{:S(2)}) collective-permute-start(f32[4,512]{1,0:T(4,128)S(1)} %get-tuple-element.58.refs_0_), channel_id=1, source_target_pairs={{0,3},{1,2},{2,1},{3,0},{4,7},{5,6},{6,5},{7,4},{8,11},{9,10},{10,... | collective-permute-start | bytes 24584 | tf_op jit(solution)/shard_map/ppermute | solution.py:302
  16.0 3.7 %collective-permute-start.7 = (f32[4,512]{1,0:T(4,128)S(1)}, f32[4,512]{1,0:T(4,128)S(1)}, u32[]{:S(2)}, u32[]{:S(2)}) collective-permute-start(f32[4,512]{1,0:T(4,128)S(1)} %get-tuple-element.58.refs_0_), channel_id=1, source_target_pairs={{0,2},{1,3},{2,0},{3,1},{4,6},{5,7},{6,4},{7,5},{8,10},{9,11},{10,... | collective-permute-start | bytes 24584 | tf_op jit(solution)/shard_map/ppermute | solution.py:302
  17.6 2.2 %collective-permute-start.6 = (f32[4,512]{1,0:T(4,128)S(1)}, f32[4,512]{1,0:T(4,128)S(1)}, u32[]{:S(2)}, u32[]{:S(2)}) collective-permute-start(f32[4,512]{1,0:T(4,128)S(1)} %get-tuple-element.58.refs_0_), channel_id=1, source_target_pairs={{0,1},{1,0},{2,3},{3,2},{4,5},{5,4},{6,7},{7,6},{8,9},{9,8},{10,11... | collective-permute-start | bytes 24584 | tf_op jit(solution)/shard_map/ppermute | solution.py:302
  20.1 8.5 %collective-permute-start.10 = (bf16[512,128]{1,0:T(8,128)(2,1)S(1)}, bf16[512,128]{1,0:T(8,128)(2,1)S(1)}, u32[]{:S(2)}, u32[]{:S(2)}) collective-permute-start(bf16[512,128]{1,0:T(8,128)(2,1)S(1)} %get-tuple-element.62.d_ref), channel_id=1, source_target_pairs={{0,1},{1,0},{2,3},{3,2},{4,5},{5,4},{6,7},{7,6},{8,16},{9,17},{10,... | collective-permute-start | bytes 393224 | tf_op jit(solution)/shard_map/ppermute | solution.py:273
  20.5 8.1 %collective-permute-start.9 = (bf16[512,128]{1,0:T(8,128)(2,1)S(1)}, bf16[512,128]{1,0:T(8,128)(2,1)S(1)}, u32[]{:S(2)}, u32[]{:S(2)}) collective-permute-start(bf16[512,128]{1,0:T(8,128)(2,1)S(1)} %get-tuple-element.62.d_ref), channel_id=1, source_target_pairs={{0,8},{1,9},{2,10},{3,11},{4,12},{5,13},{6,14},{7,15},{8,0},{9,1},... | collective-permute-start | bytes 393224 | tf_op jit(solution)/shard_map/ppermute | solution.py:273
  23.9 5.8 %collective-permute-start.11 = (bf16[512,128]{1,0:T(8,128)(2,1)S(1)}, bf16[512,128]{1,0:T(8,128)(2,1)S(1)}, u32[]{:S(2)}, u32[]{:S(2)}) collective-permute-start(bf16[512,128]{1,0:T(8,128)(2,1)S(1)} %get-tuple-element.62.d_ref), channel_id=1, source_target_pairs={{0,28},{4,0},{8,4},{12,8},{16,12},{20,16},{24,20},{28,24},{1,29},{... | collective-permute-start | bytes 393224 | tf_op jit(solution)/shard_map/ppermute | solution.py:261
